TPU v7x, 128 devices: a whole 4x4x4 slice. The times are simulated.
128 devices in a mesh: region: 8 (over y, core), member: 16 (over x, z).
Axes of the slice: x: 4, y: 4, z: 4, core: 2. Of those that a mesh axis runs over, the one named last changes fastest.
Arguments:
- interface_load: float32 [2048, 1024], P(('region', 'member')), may hold values from -23 to 23
- schur_values: float32 [2048, 16, 4096], P(('region', 'member')), may hold values from -0.04 to 2.04, as said below
- schur_columns: int32 [2048, 16], P(('region', 'member')), may hold values from 0 to 2047, as said below
- coupling: float32 [256, 1024, 512], P(('region', 'member')), may hold values from -0.25 to 0.25
- layer_inverse: float32 [256, 1024, 1024], P(('region', 'member')), may hold values from -0.1875 to 0.1875
- interior_load: float32 [256, 16, 1024], P(('region', 'member')), may hold values from -6 to 6
- adjacency: int32 [256, 8], P(('region', 'member')), may hold values from 0 to 2047, as said below
- live_counts: int32 [256], P(('region', 'member')), may hold values from 4 to 8, as said below
Outputs:
- solution: float32 [2048, 1024], P(('region', 'member'))
- residual: float32 [2048, 1024], P(('region', 'member'))
- interior: float32 [256, 16, 1024], P(('region', 'member'))
Inputs may be any that keep to these rules, and one draw needn't show every extreme that they name: `schur_columns`: block row i of region g = i // 256 stores its own block in slot 0; slot 1 holds a block of region g - 1 and slot 2 one of region g + 1 (of region g itself at the ends), each such block named by exactly one row of region g; the other slots name blocks of regions g - 1 to g + 1 that exist. Call the blocks b with (b % 256) // 16 = m the blocks of member index m; the rows of one device name at most 32 distinct blocks of any one member index, and exactly 32 for some member index on every device of a region other than the first and last. `schur_values`: the slot 0 block of each row is 2 times the identity plus small entries; all other entries are small. `adjacency`: the substructures of device d (those with index // 2 equal to d) name blocks of regions r - 1 to r + 1 that exist, where r = d // 16; slots past the live count hold such blocks too. `live_counts`: every substructure with an even index has all 8 slots live.
All inputs are finite; a program needn't handle non-finite values.
Results may differ from a plain program's by a relative error of at most 0.0003.
Values sent between devices are 32-bit elements; how exact they have to be, the bound alone decides.
No kernel may reach another device: no remote copies, remote signals or barrier semaphores. Data moves between devices by JAX's collectives and lax.ppermute only.
A program may use at most 128 MiB of HBM per device.

v0:
```python
import jax
import jax.numpy as jnp
from jax import lax
from jax.sharding import PartitionSpec as P

NB = 64
CASES = 16
ITERS = 2


HIGHEST_MODE = lax.Precision.HIGHEST


def extended(block, sides, width):
    for axis, dim in sides:
        count = lax.axis_size(axis)
        forward = [(i, i + 1) for i in range(count - 1)]
        backward = [(target, source) for source, target in forward]
        low = lax.ppermute(
            lax.slice_in_dim(block, block.shape[dim] - width, None, axis=dim), axis, forward
        )
        high = lax.ppermute(lax.slice_in_dim(block, 0, width, axis=dim), axis, backward)
        block = jnp.concatenate([low, block, high], axis=dim)
    return block


def apply_schur(values, column_ids, field):
    blocks = field.reshape(field.shape[0], CASES, NB)[column_ids]
    matrices = values.reshape(values.shape[0], values.shape[1], NB, NB)
    result = jnp.einsum("ikrq,ikcq->icr", matrices, blocks, precision=HIGHEST_MODE)
    return result.reshape(result.shape[0], CASES * NB)


def case_partial(left, right):
    return jnp.sum((left * right).reshape(-1, CASES, NB), axis=(0, 2))


def widen(factor):
    return jnp.repeat(factor, NB)[None, :]


def recover(field, slot_ids, live_counts, coupling, layer_inverse, interior_load):
    picked = field.reshape(field.shape[0], CASES, NB)[slot_ids]
    positions = jnp.arange(picked.shape[1], dtype=jnp.int32)
    live_mask = (positions[None, :] < live_counts[:, None]).astype(jnp.float32)
    picked = picked * live_mask[:, :, None, None]
    matrices = coupling.reshape(coupling.shape[0], coupling.shape[1], -1, NB)
    reduced = interior_load - jnp.einsum("snaq,sacq->scn", matrices, picked, precision=HIGHEST_MODE)
    return jnp.einsum("snm,scm->scn", layer_inverse, reduced, precision=HIGHEST_MODE)


def body(
    interface_load,
    schur_values,
    schur_columns,
    coupling,
    layer_inverse,
    interior_load,
    adjacency,
    live_counts,
):
    block_rows = interface_load.shape[0]
    members = lax.axis_size("member")
    region_rows = block_rows * members
    region_index = lax.axis_index("region")

    def triple_place(global_ids):
        within = global_ids % region_rows
        relative = global_ids // region_rows - region_index + 1
        return (within // block_rows * 3 + relative) * block_rows + within % block_rows

    def locate(global_ids):
        return triple_place(global_ids)

    local_columns = locate(schur_columns)

    def window(field):
        widened = extended(field, (("region", 0),), block_rows)
        return lax.all_gather(widened, "member", axis=0, tiled=True)

    def total(left, right):
        return lax.psum(case_partial(left, right), ("region", "member"))

    solution = jnp.zeros_like(interface_load)
    residual = interface_load
    direction = interface_load
    norm_now = total(residual, residual)
    kept_windows = []
    kept_steps = []
    for iteration in range(ITERS):
        spread = window(direction)
        image = apply_schur(schur_values, local_columns, spread)
        step_size = norm_now / total(direction, image)
        kept_windows.append(spread)
        kept_steps.append(step_size)
        solution = solution + widen(step_size) * direction
        residual = residual - widen(step_size) * image
        if iteration + 1 < ITERS:
            norm_next = total(residual, residual)
            direction = residual + widen(norm_next / norm_now) * direction
            norm_now = norm_next
    solution_window = window(solution)
    interior = recover(
        solution_window, locate(adjacency), live_counts, coupling, layer_inverse, interior_load
    )
    return (solution, residual, interior)


def solution(mesh):
    in_specs = (
        P(("region", "member"), None),
        P(("region", "member"), None, None),
        P(("region", "member"), None),
        P(("region", "member"), None, None),
        P(("region", "member"), None, None),
        P(("region", "member"), None, None),
        P(("region", "member"), None),
        P(("region", "member")),
    )
    out_specs = (
        P(("region", "member"), None),
        P(("region", "member"), None),
        P(("region", "member"), None, None),
    )
    return jax.shard_map(body, mesh=mesh, in_specs=in_specs, out_specs=out_specs, check_vma=False)
```

profile of v0, /device:TPU:1, one launch (start us, length us, event | category | flops | bytes accessed | tf_op | source)
XLA Modules:
  0.0 442.9 jit_solution(945504226411526324)
XLA Ops:
  7.2 4.6 %collective-permute-start = (f32[16,1024]{1,0:T(8,128)}, f32[16,1024]{1,0:T(8,128)S(1)}, u32[]{:S(2)}, u32[]{:S(2)}) collective-permute-start(f32[16,1024]{1,0:T(8,128)} %param.8), channel_id=1, source_target_pairs={{0,16},{16,32},{32,48},{48,64},{64,80},{80,96},{96,112},{1,17},{17... | collective-permute-start | bytes 196616 | tf_op jit(solution)/shard_map/ppermute | solution.py:19
  11.8 1.9 collective-permute-start.1
  13.8 3.9 collective-permute-done.1
  17.6 1.5 pad_maximum_fusion
  19.2 0.7 compare_select_fusion
  20.0 7.9 %reshape.62 = f32[16,16,64,64]{3,2,1,0:T(8,128)} reshape(f32[16,16,4096]{2,1,0:T(8,128)} %param.9) | data formatting | bytes 8388608 | tf_op jit(solution)/shard_map/reshape | solution.py:29
  27.9 40.8 %all-gather.4.cloned.1.call-done = f32[768,1024]{1,0:T(8,128)} async-done(((f32[48,1024]{1,0:T(8,128)}), f32[768,1024]{1,0:T(8,128)}) %all-gather.4.cloned.1.call-update) | async-done | bytes 3145744 | tf_op jit(solution)/shard_map/all_gather | solution.py:79
  68.7 2.4 copy.51
  71.0 5.2 %copy.52 = f32[768,16,64]{2,1,0:T(8,128)} copy(f32[768,16,64]{0,2,1:T(8,128)S(1)} %bitcast.26) | data formatting | bytes 6291456 | tf_op jit(solution)/shard_map/reshape | solution.py:28
  76.2 3.5 gather_fusion
  79.8 9.2 %convolution_bitcast_fusion.2 = f32[16,16,64]{2,1,0:T(8,128)S(1)} fusion(f32[16,16,16,64]{3,2,1,0:T(8,128)S(1)} %bitcast.30, f32[16,16,64,64]{3,2,1,0:T(8,128)} %reshape.62), kind=kOutput, calls=%fused_computation.5 | convolution fusion | flops 201326592 | bytes 5308416 | tf_op jit(solution)/shard_map/ikrq,ikcq->icr/dot_general | solution.py:30
  89.6 64.5 %all-reduce = (f32[16]{0:T(128)S(1)}, f32[16]{0:T(128)S(1)}) all-reduce(f32[16]{0:T(128)S(1)} %reduce_sum.51, f32[16]{0:T(128)S(1)} %reduce_sum.54), channel_id=1, replica_groups=mesh['region'=8,'member'=16] {'region','member'}, use_global_device_ids=true, to_apply=%region_2.3 | all-reduce | flops 32 | bytes 256 | tf_op jit(solution)/shard_map/psum | solution.py:82
  154.5 63.5 %psum.30 = f32[16]{0:T(128)S(1)} all-reduce(f32[16]{0:T(128)S(1)} %reduce_sum.72), channel_id=1, replica_groups=mesh['region'=8,'member'=16] {'region','member'}, use_global_device_ids=true, to_apply=%region_8.9 | all-reduce | flops 16 | bytes 128 | tf_op jit(solution)/shard_map/psum | solution.py:82
  218.2 2.3 collective-permute-start.2
  220.5 2.0 collective-permute-start.3
  222.5 3.6 collective-permute-done.3
  227.0 44.7 %all-gather.6.cloned.1.call-done = f32[768,1024]{1,0:T(8,128)} async-done(((f32[48,1024]{1,0:T(8,128)}), f32[768,1024]{1,0:T(8,128)}) %all-gather.6.cloned.1.call-update) | async-done | bytes 3145744 | tf_op jit(solution)/shard_map/all_gather | solution.py:79
  271.7 2.4 copy.53
  274.1 5.2 %copy.54 = f32[768,16,64]{2,1,0:T(8,128)} copy(f32[768,16,64]{0,2,1:T(8,128)S(1)} %bitcast.27) | data formatting | bytes 6291456 | tf_op jit(solution)/shard_map/reshape | solution.py:28
  279.3 3.5 gather_fusion.1
  282.9 9.2 %convolution_bitcast_fusion.1 = f32[16,16,64]{2,1,0:T(8,128)S(1)} fusion(f32[16,16,16,64]{3,2,1,0:T(8,128)S(1)} %bitcast.29, f32[16,16,64,64]{3,2,1,0:T(8,128)} %reshape.62), kind=kOutput, calls=%fused_computation.4 | convolution fusion | flops 201326592 | bytes 5308416 | tf_op jit(solution)/shard_map/ikrq,ikcq->icr/dot_general | solution.py:30
  292.4 64.5 %psum.31 = f32[16]{0:T(128)S(1)} all-reduce(f32[16]{0:T(128)S(1)} %reduce_sum.75), channel_id=1, replica_groups=mesh['region'=8,'member'=16] {'region','member'}, use_global_device_ids=true, to_apply=%region_11.12 | all-reduce | flops 16 | bytes 128 | tf_op jit(solution)/shard_map/psum | solution.py:82
  357.8 3.0 collective-permute-start.4
  360.8 1.9 collective-permute-start.5
  362.7 3.6 collective-permute-done.5
  367.2 5.5 %copy.57 = f32[2,1024,512]{1,2,0:T(8,128)} copy(f32[2,1024,512]{2,1,0:T(8,128)} %param.11) | data formatting | bytes 8388608 | tf_op args[3]
  372.8 38.9 %all-gather.8.cloned.1.call-done = f32[768,1024]{1,0:T(8,128)} async-done(((f32[48,1024]{1,0:T(8,128)}), f32[768,1024]{1,0:T(8,128)}) %all-gather.8.cloned.1.call-update) | async-done | bytes 3145744 | tf_op jit(solution)/shard_map/all_gather | solution.py:79
  411.6 2.4 copy.55
  414.0 5.1 %copy.56 = f32[768,16,64]{2,1,0:T(8,128)} copy(f32[768,16,64]{0,2,1:T(8,128)S(1)} %bitcast.28) | data formatting | bytes 6291456 | tf_op jit(solution)/shard_map/reshape | solution.py:43
  419.2 3.3 gather_fusion.2
  422.5 4.0 fusion
  426.5 9.9 %fusion.16 = f32[2,16,1024]{2,1,0:T(8,128)} fusion(f32[2,16,1024]{2,1,0:T(8,128)S(1)} %fusion, f32[2,1024,1024]{2,1,0:T(8,128)} %param.12), kind=kOutput, calls=%fused_computation.60 | convolution fusion | flops 402653184 | bytes 8650752 | tf_op jit(solution)/shard_map/snm,scm->scn/dot_general | solution.py:49
  (51 shorter events, 4.2 us)
Async XLA Ops:
  7.2 61.5 %all-gather.4.cloned.1.call-start = ((), (), s32[]{:S(2)}) async-start(), calls=%async_computation | async-start | bytes 3342336 | tf_op jit(solution)/shard_map/all_gather | solution.py:79
  7.2 6.5 %collective-permute-start = (f32[16,1024]{1,0:T(8,128)}, f32[16,1024]{1,0:T(8,128)S(1)}, u32[]{:S(2)}, u32[]{:S(2)}) collective-permute-start(f32[16,1024]{1,0:T(8,128)} %param.8), channel_id=1, source_target_pairs={{0,16},{16,32},{32,48},{48,64},{64,80},{80,96},{96,112},{1,17},{17... | collective-permute-start | bytes 196616 | tf_op jit(solution)/shard_map/ppermute | solution.py:19
  11.8 5.8 %collective-permute-start.1 = (f32[16,1024]{1,0:T(8,128)}, f32[16,1024]{1,0:T(8,128)S(1)}, u32[]{:S(2)}, u32[]{:S(2)}) collective-permute-start(f32[16,1024]{1,0:T(8,128)} %param.8), channel_id=1, source_target_pairs={{16,0},{32,16},{48,32},{64,48},{80,64},{96,80},{112,96},{17,1},{33... | collective-permute-start | bytes 196616 | tf_op jit(solution)/shard_map/ppermute | solution.py:22
  19.2 252.6 %all-gather.6.cloned.1.call-start = ((), (), s32[]{:S(2)}) async-start(), calls=%async_computation.1 | async-start | bytes 3342336 | tf_op jit(solution)/shard_map/all_gather | solution.py:79
  79.8 9.4 %copy-start = (f32[16,1024]{1,0:T(8,128)S(1)}, f32[16,1024]{1,0:T(8,128)}, u32[]{:S(2)}) copy-start(f32[16,1024]{1,0:T(8,128)} %param.8) | copy-start | bytes 196612
  218.2 4.3 collective-permute-start.2
  220.5 5.6 %collective-permute-start.3 = (f32[16,1024]{1,0:T(8,128)S(1)}, f32[16,1024]{1,0:T(8,128)S(1)}, u32[]{:S(2)}, u32[]{:S(2)}) collective-permute-start(f32[16,1024]{1,0:T(8,128)S(1)} %multiply_add_fusion.1), channel_id=1, source_target_pairs={{16,0},{32,16},{48,32},{64,48},{80,64},{96,80},{112,96},{17,1},{33... | collective-permute-start | bytes 196616 | tf_op jit(solution)/shard_map/ppermute | solution.py:22
  226.8 184.8 %all-gather.8.cloned.1.call-start = ((), (), s32[]{:S(2)}) async-start(), calls=%async_computation.2 | async-start | bytes 3342336 | tf_op jit(solution)/shard_map/all_gather | solution.py:79
  282.9 84.2 %copy-start.3 = (s32[2,8]{1,0:T(2,128)S(1)}, s32[2,8]{1,0:T(2,128)}, u32[]{:S(2)}) copy-start(s32[2,8]{1,0:T(2,128)} %param.14) | copy-start | bytes 196
  357.8 14.9 %copy-start.1 = (f32[16,1024]{1,0:T(8,128)}, f32[16,1024]{1,0:T(8,128)S(1)}, u32[]{:S(2)}) copy-start(f32[16,1024]{1,0:T(8,128)S(1)} %get-tuple-element.14) | copy-start | bytes 196612
  357.8 4.9 %collective-permute-start.4 = (f32[16,1024]{1,0:T(8,128)S(1)}, f32[16,1024]{1,0:T(8,128)S(1)}, u32[]{:S(2)}, u32[]{:S(2)}) collective-permute-start(f32[16,1024]{1,0:T(8,128)S(1)} %get-tuple-element.14), channel_id=1, source_target_pairs={{0,16},{16,32},{32,48},{48,64},{64,80},{80,96},{96,112},{1,17},{17... | collective-permute-start | bytes 196616 | tf_op jit(solution)/shard_map/ppermute | solution.py:19
  360.8 5.6 %collective-permute-start.5 = (f32[16,1024]{1,0:T(8,128)S(1)}, f32[16,1024]{1,0:T(8,128)S(1)}, u32[]{:S(2)}, u32[]{:S(2)}) collective-permute-start(f32[16,1024]{1,0:T(8,128)S(1)} %get-tuple-element.14), channel_id=1, source_target_pairs={{16,0},{32,16},{48,32},{64,48},{80,64},{96,80},{112,96},{17,1},{33... | collective-permute-start | bytes 196616 | tf_op jit(solution)/shard_map/ppermute | solution.py:22
  367.2 5.5 %copy-start.4 = (s32[2]{0:T(128)S(1)}, s32[2]{0:T(128)}, u32[]{:S(2)}) copy-start(s32[2]{0:T(128)} %param.15) | copy-start | bytes 28
  414.0 8.5 %copy-start.2 = (f32[2,16,1024]{2,1,0:T(8,128)S(1)}, f32[2,16,1024]{2,1,0:T(8,128)}, u32[]{:S(2)}) copy-start(f32[2,16,1024]{2,1,0:T(8,128)} %param.13) | copy-start | bytes 393220
Sparse Core Ops, SparseCore 0:
  19.3 49.3 all-gather.3
  226.9 44.7 all-gather.5
  367.2 44.3 all-gather.7
where the time goes:
time: 444 us; the launch traced here: 443 us
  blocking collectives  193 us (43%)
  waiting for transfers between devices  135 us (30%)
  local copies, waits for them, and re-layouts  47.6 us (11%)
  matrix products  32.4 us (7%)
  starting transfers between devices  16.1 us (4%)
  between operations  14 us (3%)
  other arithmetic  4.97 us (1%)
    psum x3, blocking collectives, total(): return lax.psum(case_partial(left, right), ('region', 'member'))  193 us
    all_gather x3, waiting for transfers between devices, window(): return lax.all_gather(widened, 'member', axis=0, tiled=True)  124 us
    dot_general x2, matrix products, apply_schur(): jnp.einsum('ikrq,ikcq->icr', matrices, blocks, precision=HIGHEST_MODE)  18.4 us
    ppermute x3, waiting for transfers between devices, extended(): lax.ppermute(lax.slice_in_dim(block, 0, width, axis=dim), axis, backward)  11.1 us
    reshape x2, local copies, waits for them, and re-layouts, apply_schur(): blocks = field.reshape(field.shape[0], CASES, NB)[column_ids]  10.4 us
    ppermute x3, starting transfers between devices, extended(): lax.ppermute(lax.slice_in_dim(block, block.shape[dim] - width, None, axis...  9.92 us
    dot_general x1, matrix products, recover(): jnp.einsum('snm,scm->scn', layer_inverse, reduced, precision=HIGHEST_MODE)  9.87 us
  transfers between devices with their start and end apart: 9, of which 6 were waited for; matrix products, arithmetic and copies ran while one was open for 3% of the time, Pallas kernels for 0%

commit v1 on v0

v1 whole, which is shorter than its diff:
```python
import jax
import jax.numpy as jnp
from jax import lax
from jax.experimental import pallas as pl
from jax.experimental.pallas import tpu as pltpu
from jax.sharding import PartitionSpec as P

NB = 64
CASES = 16
LANES = 128
AXES = ("y", "core", "x", "z")
SIZES = (4, 2, 4, 4)
ORDER = (0, 1, 3, 2)
WINDOW = 768
NT = (((1,), (1,)), ((), ()))

PLACES = [
    (y, c, x, z)
    for y in range(SIZES[0])
    for c in range(SIZES[1])
    for x in range(SIZES[2])
    for z in range(SIZES[3])
]


def flat(y, c, x, z):
    return ((y * SIZES[1] + c) * SIZES[2] + x) * SIZES[3] + z


def permute(value, target):
    pairs = []
    for place in PLACES:
        goal = target(*place)
        if goal is not None:
            pairs.append((flat(*place), flat(*goal)))
    return lax.ppermute(value, AXES, pairs)


def far(y, c, x, z):
    if c == 1:
        return (y + 1, 0, x, z) if y + 1 < SIZES[0] else None
    return (y - 1, 1, x, z) if y > 0 else None


def partner(y, c, x, z):
    return (y, 1 - c, x, z)


def along_first(step):
    return lambda y, c, x, z: (y, c, x, (z - step) % 4) if c == 0 else (y, c, (x - step) % 4, z)


def along_second(step):
    return lambda y, c, x, z: (y, c, (x - step) % 4, z) if c == 0 else (y, c, x, (z - step) % 4)


def exchange(own):
    line = [own] + [permute(own, along_first(k)) for k in ORDER[1:]]
    line = jnp.concatenate(line)
    plane = [line] + [permute(line, along_second(k)) for k in ORDER[1:]]
    others = [permute(piece, far) for piece in plane]
    pair = [permute(piece, partner) for piece in plane]
    return jnp.concatenate(plane + others + pair)


def locate(ids, region, x, z):
    goal = ids // 256
    member = ids % 256 // 16
    dx = (member // 4 - x) % 4
    dz = (member % 4 - z) % 4
    px = dx ^ (dx >> 1)
    pz = dz ^ (dz >> 1)
    odd = goal % 2 == 1
    first = jnp.where(odd, pz, px)
    second = jnp.where(odd, px, pz)
    group = jnp.where(goal == region, 0, jnp.where(goal == (region ^ 1), 2, 1))
    return ((group * 4 + first) * 4 + second) * 16 + ids % 16


def split(value):
    high = value.astype(jnp.bfloat16)
    low = (value - high.astype(jnp.float32)).astype(jnp.bfloat16)
    return high, low


def lane_ids(rows):
    return lax.broadcasted_iota(jnp.int32, (rows, LANES), 1)


def merge_halves(left, right):
    low_half = lane_ids(left.shape[0]) < NB
    first = jnp.where(low_half, left, pltpu.roll(right, NB, 1))
    second = jnp.where(low_half, pltpu.roll(left, NB, 1), right)
    return first, second


def prepare_kernel(values_ref, out_ref, rows_ref):
    lanes = lane_ids(8)
    subs = lax.broadcasted_iota(jnp.int32, (8, LANES), 0)
    for pair in range(32):
        cut = slice(pair * LANES, (pair + 1) * LANES)
        upper = values_ref[0, 0:8, cut]
        lower = values_ref[0, 8:16, cut]
        own = (subs == 0) & ((lanes == 2 * pair) | (lanes == NB + 2 * pair + 1))
        upper = jnp.where(own, upper - 2.0, upper)
        first, second = merge_halves(upper, lower)
        rows_ref[pl.ds(2 * pair, 8, stride=NB), :] = first
        rows_ref[pl.ds(2 * pair + 1, 8, stride=NB), :] = second
    for k in range(8):
        high, low = split(rows_ref[k * NB : (k + 1) * NB, :])
        out_ref[0, 0:NB, k * LANES : (k + 1) * LANES] = high
        out_ref[0, NB : 2 * NB, k * LANES : (k + 1) * LANES] = low


def prepare(values):
    rows = values.shape[0]
    return pl.pallas_call(
        prepare_kernel,
        grid=(rows,),
        in_specs=[pl.BlockSpec((1, 16, 4096), lambda i: (i, 0, 0))],
        out_specs=pl.BlockSpec((1, 128, 1024), lambda i: (i, 0, 0)),
        out_shape=jax.ShapeDtypeStruct((rows, 128, 1024), jnp.bfloat16),
        scratch_shapes=[pltpu.VMEM((512, LANES), jnp.float32)],
        compiler_params=pltpu.CompilerParams(vmem_limit_bytes=8 * 2**20),
        cost_estimate=pl.CostEstimate(flops=2**24, bytes_accessed=2**23, transcendentals=0),
        name="prepare",
    )(values)


def apply_rows(places_ref, window_ref, matrices_ref, x_ref, out_ref):
    low_half = lane_ids(8) < NB
    for row in range(16):
        for k in range(8):
            left = window_ref[places_ref[row * 16 + k]]
            right = window_ref[places_ref[row * 16 + k + 8]]
            high, low = split(jnp.concatenate(merge_halves(left, right)))
            x_ref[row % 2, 0:16, k * LANES : (k + 1) * LANES] = high
            x_ref[row % 2, 16:32, k * LANES : (k + 1) * LANES] = low
        product = lax.dot_general(
            x_ref[row % 2], matrices_ref[row], NT, preferred_element_type=jnp.float32
        )
        both = product[0:16] + product[16:32]
        both = both + pltpu.roll(both, NB, 1)
        out_ref[row] = jnp.where(low_half, both[0:8], both[8:16])


def first_kernel(places_ref, window_ref, matrices_ref, image_ref, x_ref):
    apply_rows(places_ref, window_ref, matrices_ref, x_ref, image_ref)


def second_kernel(
    places_ref, window_ref, matrices_ref, load_ref, image_ref, twice_ref, sums_ref, x_ref
):
    apply_rows(places_ref, window_ref, matrices_ref, x_ref, twice_ref)
    load, image, twice = load_ref[...], image_ref[...], twice_ref[...]
    lanes = lane_ids(8)
    low_half = lanes < NB
    packed = jnp.zeros((8, LANES), jnp.float32)
    products = (load * load, load * image, image * image, load * twice, image * twice)
    for place, product in enumerate(products):
        tile = jnp.sum(product, axis=0)
        left = jnp.sum(jnp.where(low_half, tile, 0.0), axis=1, keepdims=True)
        right = jnp.sum(jnp.where(low_half, 0.0, tile), axis=1, keepdims=True)
        packed = jnp.where(lanes == place, left, packed)
        packed = jnp.where(lanes == NB + place, right, packed)
    sums_ref[...] = packed


VMEM_SPEC = pl.BlockSpec(memory_space=pltpu.VMEM)
SMEM_SPEC = pl.BlockSpec(memory_space=pltpu.SMEM)
APPLY_COST = pl.CostEstimate(flops=2**27, bytes_accessed=2**23, transcendentals=0)


def apply_first(places, window, matrices):
    return pl.pallas_call(
        first_kernel,
        in_specs=[SMEM_SPEC, VMEM_SPEC, VMEM_SPEC],
        out_specs=VMEM_SPEC,
        out_shape=jax.ShapeDtypeStruct((16, 8, LANES), jnp.float32),
        scratch_shapes=[pltpu.VMEM((2, 32, 1024), jnp.bfloat16)],
        compiler_params=pltpu.CompilerParams(vmem_limit_bytes=16 * 2**20),
        cost_estimate=APPLY_COST,
        name="apply_first",
    )(places, window, matrices)


def apply_second(places, window, matrices, load, image):
    return pl.pallas_call(
        second_kernel,
        in_specs=[SMEM_SPEC] + [VMEM_SPEC] * 4,
        out_specs=[VMEM_SPEC] * 2,
        out_shape=[
            jax.ShapeDtypeStruct((16, 8, LANES), jnp.float32),
            jax.ShapeDtypeStruct((8, LANES), jnp.float32),
        ],
        scratch_shapes=[pltpu.VMEM((2, 32, 1024), jnp.bfloat16)],
        compiler_params=pltpu.CompilerParams(vmem_limit_bytes=16 * 2**20),
        cost_estimate=APPLY_COST,
        name="apply_second",
    )(places, window, matrices, load, image)


def couple_kernel(slots_ref, live_ref, first_ref, second_ref, coupling_ref, load_ref, out_ref, x_ref, rows_ref):
    sub = pl.program_id(0)

    @pl.when(pl.program_id(1) == 0)
    def _():
        for t in range(4):
            for which, ref in enumerate((first_ref, second_ref)):
                tiles = []
                for slot in (2 * t, 2 * t + 1):
                    tile = ref[slots_ref[sub * 8 + slot]]
                    tiles.append(jnp.where(slot < live_ref[sub], tile, 0.0))
                even, odd = merge_halves(*tiles)
                rows_ref[t, which, pl.ds(0, 8, stride=2), :] = even
                rows_ref[t, which, pl.ds(1, 8, stride=2), :] = odd
                high, low = split(rows_ref[t, which])
                x_ref[16 * which : 16 * which + 16, t * LANES : (t + 1) * LANES] = high
                x_ref[32 + 16 * which : 48 + 16 * which, t * LANES : (t + 1) * LANES] = low

    high, low = split(coupling_ref[0])
    main = lax.dot_general(x_ref[...], high, NT, preferred_element_type=jnp.float32)
    rest = lax.dot_general(x_ref[0:32], low, NT, preferred_element_type=jnp.float32)
    out_ref[0, 16:48, :] = main[0:32] + main[32:64] + rest
    out_ref[0, 0:16, :] = load_ref[0]


def couple(slots, live, first, second, coupling, load):
    cut = 512
    return pl.pallas_call(
        couple_kernel,
        grid=(2, 1024 // cut),
        in_specs=[
            SMEM_SPEC,
            SMEM_SPEC,
            VMEM_SPEC,
            VMEM_SPEC,
            pl.BlockSpec((1, cut, 512), lambda s, n: (s, n, 0)),
            pl.BlockSpec((1, 16, cut), lambda s, n: (s, 0, n)),
        ],
        out_specs=pl.BlockSpec((1, 48, cut), lambda s, n: (s, 0, n)),
        out_shape=jax.ShapeDtypeStruct((2, 48, 1024), jnp.float32),
        scratch_shapes=[pltpu.VMEM((64, 512), jnp.bfloat16), pltpu.VMEM((4, 2, 16, LANES), jnp.float32)],
        compiler_params=pltpu.CompilerParams(vmem_limit_bytes=16 * 2**20),
        cost_estimate=pl.CostEstimate(flops=2**28, bytes_accessed=2**22, transcendentals=0),
        name="couple",
    )(slots, live, first, second, coupling, load)


def layers_kernel(reduced_ref, inverse_ref, out_ref):
    top, bottom = split(reduced_ref[0])
    high, low = split(inverse_ref[0])
    main = lax.dot_general(
        jnp.concatenate([top, bottom]), high, NT, preferred_element_type=jnp.float32
    )
    rest = lax.dot_general(top, low, NT, preferred_element_type=jnp.float32)
    out_ref[0] = main[0:48] + main[48:96] + rest


def layers(reduced, inverse):
    cut = 256
    return pl.pallas_call(
        layers_kernel,
        grid=(2, 1024 // cut),
        in_specs=[
            pl.BlockSpec((1, 48, 1024), lambda s, n: (s, 0, 0)),
            pl.BlockSpec((1, cut, 1024), lambda s, n: (s, n, 0)),
        ],
        out_specs=pl.BlockSpec((1, 48, cut), lambda s, n: (s, 0, n)),
        out_shape=jax.ShapeDtypeStruct((2, 48, 1024), jnp.float32),
        compiler_params=pltpu.CompilerParams(vmem_limit_bytes=16 * 2**20),
        cost_estimate=pl.CostEstimate(flops=2**29, bytes_accessed=2**23, transcendentals=0),
        name="layers",
    )(reduced, inverse)


def finish_kernel(
    sums_ref, load_ref, image_ref, twice_ref, parts_ref, solution_ref, residual_ref, interior_ref, tiles_ref, cases_ref
):
    lanes = lane_ids(8)
    low_half = lanes < NB
    packed = jnp.sum(sums_ref[...], axis=0)

    def pick(place):
        left = jnp.sum(jnp.where(lanes == place, packed, 0.0), axis=1, keepdims=True)
        right = jnp.sum(jnp.where(lanes == NB + place, packed, 0.0), axis=1, keepdims=True)
        return jnp.where(low_half, left, right)

    uu, ue, ee, uf, ef = [pick(place) for place in range(5)]
    inner = 2.0 * uu + ue
    step = uu / inner
    along = ue / inner
    beta = step * (ee / inner) - along * along
    norm = beta * uu
    mix = along + beta
    length = mix * mix * uu - 2.0 * mix * step * ue + step * step * ee
    cross = mix * mix * ue - mix * step * (uf + ee) + step * step * ef
    last = norm / (2.0 * length + cross)
    on_load = step + last * mix
    on_image = -last * step
    rest_load = along - 2.0 * last * mix
    rest_image = -step - last * (mix - 2.0 * step)
    rest_twice = last * step

    rows = load_ref.shape[0]
    load, image, twice = load_ref[...], image_ref[...], twice_ref[...]
    for out_ref, value in (
        (solution_ref, on_load[None] * load + on_image[None] * image),
        (
            residual_ref,
            rest_load[None] * load + rest_image[None] * image + rest_twice[None] * twice,
        ),
    ):
        tiles_ref[...] = value.reshape(rows * 8, LANES)
        for s in range(8):
            out_ref[:, s * LANES : (s + 1) * LANES] = tiles_ref[pl.ds(s, rows, stride=8), :]
    for place, factor in enumerate((on_load, on_image)):
        for h in range(2):
            spread = jnp.broadcast_to(factor[:, h * NB : h * NB + 1], (8, LANES))
            cases_ref[place, pl.ds(h, 8, stride=2), :] = spread
    own, other = cases_ref[0][:, 0:1], cases_ref[1][:, 0:1]
    for sub in range(2):
        interior_ref[sub] = (
            parts_ref[sub, 0:16] - own * parts_ref[sub, 16:32] - other * parts_ref[sub, 32:48]
        )


def finish(sums, load, image, twice, parts):
    return pl.pallas_call(
        finish_kernel,
        in_specs=[VMEM_SPEC] * 5,
        out_specs=[VMEM_SPEC] * 3,
        out_shape=[
            jax.ShapeDtypeStruct((16, 1024), jnp.float32),
            jax.ShapeDtypeStruct((16, 1024), jnp.float32),
            jax.ShapeDtypeStruct((2, CASES, 1024), jnp.float32),
        ],
        scratch_shapes=[pltpu.VMEM((128, LANES), jnp.float32), pltpu.VMEM((2, 16, LANES), jnp.float32)],
        compiler_params=pltpu.CompilerParams(vmem_limit_bytes=8 * 2**20),
        name="finish",
    )(sums, load, image, twice, parts)


def to_all(value, axes, count):
    return lax.all_to_all(jnp.broadcast_to(value[None], (count,) + value.shape), axes, 0, 0)


def body(
    interface_load,
    schur_values,
    schur_columns,
    coupling,
    layer_inverse,
    interior_load,
    adjacency,
    live_counts,
):
    y, core, x, z = [lax.axis_index(axis) for axis in AXES]
    region = y * 2 + core
    places = locate(schur_columns, region, x, z).reshape(-1)
    slots = locate(adjacency, region, x, z).reshape(-1)
    load = interface_load.reshape(16, 8, LANES)
    matrices = prepare(schur_values)
    load_window = exchange(load)
    image = apply_first(places, load_window, matrices)
    image_window = exchange(image)
    twice, sums = apply_second(places, image_window, matrices, load, image)
    plane_sums = jnp.sum(to_all(sums, ("x", "z"), 16), axis=0)
    all_sums = to_all(plane_sums, ("y", "core"), 8)
    reduced = couple(slots, live_counts, load_window, image_window, coupling, interior_load)
    parts = layers(reduced, layer_inverse)
    return tuple(finish(all_sums, load, image, twice, parts))


def solution(mesh):
    grid = jax.sharding.Mesh(mesh.devices.reshape(SIZES), AXES)
    lead = AXES
    in_specs = (
        P(lead, None),
        P(lead, None, None),
        P(lead, None),
        P(lead, None, None),
        P(lead, None, None),
        P(lead, None, None),
        P(lead, None),
        P(lead),
    )
    out_specs = (P(lead, None), P(lead, None), P(lead, None, None))
    return jax.shard_map(body, mesh=grid, in_specs=in_specs, out_specs=out_specs, check_vma=False)
```

time: 444 us -> 109 us (0.25)
  blocking collectives: 193 us -> 0 us
  waiting for transfers between devices: 135 us -> 12.4 us
  starting transfers between devices: 16.1 us -> 58.3 us
  matrix products: 32.4 us -> 0 us
  local copies, waits for them, and re-layouts: 47.6 us -> 19.6 us
  Pallas kernels: 0 us -> 15.7 us
  between operations: 14 us -> 1.17 us
    psum x3 -> x0, blocking collectives: 193 us -> none  [total(): return lax.psum(case_partial(left, right), ('region', 'member'))]
    all_gather x3 -> x0, waiting for transfers between devices: 124 us -> none  [window(): return lax.all_gather(widened, 'member', axis=0, tiled=True)]
    ppermute x6 -> x28, starting transfers between devices: 15.8 us -> 50.2 us  [permute(): return lax.ppermute(value, AXES, pairs)]
    dot_general x4 -> x0, matrix products: 32.4 us -> none  [the longest x2 18.4 us: apply_schur(): jnp.einsum('ikrq,ikcq->icr', matrices, blocks, precision=HIGHEST_MODE)]
    reshape x6 -> x2, local copies, waits for them, and re-layouts: 23.7 us -> 0.17 us  [the longest x1 0.08 us: body(): slots = locate(adjacency, region, x, z).reshape(-1)]
    pallas_call x0 -> x6, Pallas kernels: none -> 15.7 us  [the longest x1 4.31 us: prepare(): pl.pallas_call(prepare_kernel, grid=(rows,), in_specs=[pl.BlockSpec((1, 1...]
    unnamed x11 -> x48, local copies, waits for them, and re-layouts: 5.48 us -> 17.4 us
    gather x3 -> x0, local copies, waits for them, and re-layouts: 10.4 us -> none  [the longest x2 7.07 us: apply_schur(): blocks = field.reshape(field.shape[0], CASES, NB)[column_ids]]
  transfers between devices with their start and end apart: 9 -> 30, of which waited for: 6 -> 6; matrix products, arithmetic and copies ran while one was open for 3% -> 6% of each run, Pallas kernels for 0% -> 10%
where the time goes in v1:
time: 109 us; the launch traced here: 108 us
  starting transfers between devices  58.3 us (53%)
  local copies, waits for them, and re-layouts  19.6 us (18%)
  Pallas kernels  15.7 us (14%)
  waiting for transfers between devices  12.4 us (11%)
  between operations  1.17 us (1%)
    ppermute x28, starting transfers between devices, permute(): return lax.ppermute(value, AXES, pairs)  50.2 us
    unnamed x48, local copies, waits for them, and re-layouts  17.4 us
    ppermute x28, waiting for transfers between devices, permute(): return lax.ppermute(value, AXES, pairs)  12.4 us
    all_to_all x2, starting transfers between devices, to_all(): lax.all_to_all(jnp.broadcast_to(value[None], (count,) + value.shape), axe...  8.05 us
    pallas_call x1, Pallas kernels, prepare(): pl.pallas_call(prepare_kernel, grid=(rows,), in_specs=[pl.BlockSpec((1, 1...  4.31 us
    pallas_call x1, Pallas kernels, layers(): pl.pallas_call(layers_kernel, grid=(2, 1024 // cut), in_specs=[pl.BlockSp...  3.6 us
    pallas_call x1, Pallas kernels, couple(): pl.pallas_call(couple_kernel, grid=(2, 1024 // cut), in_specs=[SMEM_SPEC,...  2.73 us
  transfers between devices with their start and end apart: 30, of which 6 were waited for; matrix products, arithmetic and copies ran while one was open for 6% of the time, Pallas kernels for 10%

profile of v1, /device:TPU:1, one launch (start us, length us, event | category | flops | bytes accessed | tf_op | source)
XLA Modules:
  0.0 108.0 jit_solution(15361041966407929877)
XLA Ops:
  1.5 3.4 %collective-permute-start = (f32[16,8,128]{2,1,0:T(8,128)S(1)}, f32[16,8,128]{2,1,0:T(8,128)S(1)}, u32[]{:S(2)}, u32[]{:S(2)}) collective-permute-start(f32[16,8,128]{2,1,0:T(8,128)S(1)} %bitcast.2), channel_id=1, source_target_pairs={{0,3},{1,0},{2,1},{3,2},{4,7},{5,4},{6,5},{7,6},{8,11},{9,8},{10,9... | collective-permute-start | bytes 196616 | tf_op jit(solution)/shard_map/ppermute | solution.py:36
  4.9 1.7 %collective-permute-start.2 = (f32[16,8,128]{2,1,0:T(8,128)S(1)}, f32[16,8,128]{2,1,0:T(8,128)S(1)}, u32[]{:S(2)}, u32[]{:S(2)}) collective-permute-start(f32[16,8,128]{2,1,0:T(8,128)S(1)} %bitcast.4), channel_id=1, source_target_pairs={{0,2},{1,3},{2,0},{3,1},{4,6},{5,7},{6,4},{7,5},{8,10},{9,11},{10,... | collective-permute-start | bytes 196616 | tf_op jit(solution)/shard_map/ppermute | solution.py:36
  7.9 2.0 %collective-permute-done.1 = f32[16,8,128]{2,1,0:T(8,128)S(1)} collective-permute-done((f32[16,8,128]{2,1,0:T(8,128)S(1)}, f32[16,8,128]{2,1,0:T(8,128)S(1)}, u32[]{:S(2)}, u32[]{:S(2)}) %collective-permute-start.1) | collective-permute-done | bytes 65568 | tf_op jit(solution)/shard_map/ppermute | solution.py:36
  11.2 3.8 %collective-permute-start.3 = (f32[64,8,128]{2,1,0:T(8,128)}, f32[64,8,128]{2,1,0:T(8,128)}, u32[]{:S(2)}, u32[]{:S(2)}) collective-permute-start(f32[64,8,128]{2,1,0:T(8,128)} %get-tuple-element.7), channel_id=1, source_target_pairs={{0,12},{1,13},{2,14},{3,15},{4,0},{5,1},{6,2},{7,3},{8,4},{9,5},{1... | collective-permute-start | bytes 786440 | tf_op jit(solution)/shard_map/ppermute | solution.py:36
  14.9 1.4 %collective-permute-start.5 = (f32[64,8,128]{2,1,0:T(8,128)}, f32[64,8,128]{2,1,0:T(8,128)}, u32[]{:S(2)}, u32[]{:S(2)}) collective-permute-start(f32[64,8,128]{2,1,0:T(8,128)} %get-tuple-element.7), channel_id=1, source_target_pairs={{0,8},{1,9},{2,10},{3,11},{4,12},{5,13},{6,14},{7,15},{8,0},{9,1},... | collective-permute-start | bytes 786440 | tf_op jit(solution)/shard_map/ppermute | solution.py:36
  17.2 2.2 %copy-done.3 = f32[16,16,4096]{2,1,0:T(8,128)S(1)} copy-done((f32[16,16,4096]{2,1,0:T(8,128)S(1)}, f32[16,16,4096]{2,1,0:T(8,128)}, u32[]{:S(2)}) %copy-start.3) | copy-done | bytes 4194328
  19.4 4.3 %prepare.1.matrices_ref = bf16[16,128,1024]{2,1,0:T(8,128)(2,1)S(1)} custom-call(f32[16,16,4096]{2,1,0:T(8,128)S(1)} %copy-done.3), custom_call_target="tpu_custom_call" | custom-call | flops 16777216 | bytes 8388608 | tf_op jit(solution)/shard_map/prepare/pallas_call | solution.py:117
  23.7 6.3 %collective-permute-start.6 = (f32[64,8,128]{2,1,0:T(8,128)}, f32[64,8,128]{2,1,0:T(8,128)S(1)}, u32[]{:S(2)}, u32[]{:S(2)}) collective-permute-start(f32[64,8,128]{2,1,0:T(8,128)} %get-tuple-element.7), channel_id=1, source_target_pairs={{16,32},{17,33},{18,34},{19,35},{20,36},{21,37},{22,38},{23,39},{2... | collective-permute-start | bytes 786440 | tf_op jit(solution)/shard_map/ppermute | solution.py:36
  30.1 3.6 %collective-permute-start.7 = (f32[64,8,128]{2,1,0:T(8,128)}, f32[64,8,128]{2,1,0:T(8,128)S(1)}, u32[]{:S(2)}, u32[]{:S(2)}) collective-permute-start(f32[64,8,128]{2,1,0:T(8,128)} %collective-permute-done.3), channel_id=1, source_target_pairs={{16,32},{17,33},{18,34},{19,35},{20,36},{21,37},{22,38},{23,39},{2... | collective-permute-start | bytes 786440 | tf_op jit(solution)/shard_map/ppermute | solution.py:36
  34.7 2.0 %collective-permute-start.8 = (f32[64,8,128]{2,1,0:T(8,128)}, f32[64,8,128]{2,1,0:T(8,128)S(1)}, u32[]{:S(2)}, u32[]{:S(2)}) collective-permute-start(f32[64,8,128]{2,1,0:T(8,128)} %collective-permute-done.4), channel_id=1, source_target_pairs={{16,32},{17,33},{18,34},{19,35},{20,36},{21,37},{22,38},{23,39},{2... | collective-permute-start | bytes 786440 | tf_op jit(solution)/shard_map/ppermute | solution.py:36
  37.7 3.6 %collective-permute-start.9 = (f32[64,8,128]{2,1,0:T(8,128)}, f32[64,8,128]{2,1,0:T(8,128)S(1)}, u32[]{:S(2)}, u32[]{:S(2)}) collective-permute-start(f32[64,8,128]{2,1,0:T(8,128)} %collective-permute-done.5), channel_id=1, source_target_pairs={{16,32},{17,33},{18,34},{19,35},{20,36},{21,37},{22,38},{23,39},{2... | collective-permute-start | bytes 786440 | tf_op jit(solution)/shard_map/ppermute | solution.py:36
  43.1 2.5 %collective-permute-done.9 = f32[64,8,128]{2,1,0:T(8,128)S(1)} collective-permute-done((f32[64,8,128]{2,1,0:T(8,128)}, f32[64,8,128]{2,1,0:T(8,128)S(1)}, u32[]{:S(2)}, u32[]{:S(2)}) %collective-permute-start.9) | collective-permute-done | bytes 262176 | tf_op jit(solution)/shard_map/ppermute | solution.py:36
  45.8 2.1 %apply_first.1.image_ref = f32[16,8,128]{2,1,0:T(8,128)S(1)} custom-call(s32[256]{0:T(256)S(1)} %reshape.17.places_ref, f32[768,8,128]{2,1,0:T(8,128)S(1)} %constant_dynamic-update-slice_fusion.4.window_ref.first_ref, bf16[16,128,1024]{2,1,0:T(8,128)(2,1)S(1)} %prepare.1.matrices_ref), custom_call_target="tpu_custom_call" | custom-call | flops 134217728 | bytes 8388608 | tf_op jit(solution)/shard_map/apply_first/pallas_call | solution.py:175
  49.5 1.7 %collective-permute-start.16 = (f32[16,8,128]{2,1,0:T(8,128)S(1)}, f32[16,8,128]{2,1,0:T(8,128)S(1)}, u32[]{:S(2)}, u32[]{:S(2)}) collective-permute-start(f32[16,8,128]{2,1,0:T(8,128)S(1)} %apply_first.1.image_ref), channel_id=1, source_target_pairs={{0,2},{1,3},{2,0},{3,1},{4,6},{5,7},{6,4},{7,5},{8,10},{9,11},{10,... | collective-permute-start | bytes 196616 | tf_op jit(solution)/shard_map/ppermute | solution.py:36
  51.2 1.9 %collective-permute-done.15 = f32[16,8,128]{2,1,0:T(8,128)S(1)} collective-permute-done((f32[16,8,128]{2,1,0:T(8,128)S(1)}, f32[16,8,128]{2,1,0:T(8,128)S(1)}, u32[]{:S(2)}, u32[]{:S(2)}) %collective-permute-start.15) | collective-permute-done | bytes 65568 | tf_op jit(solution)/shard_map/ppermute | solution.py:36
  53.1 1.0 collective-permute-done.16
  54.2 2.5 %collective-permute-start.17 = (f32[64,8,128]{2,1,0:T(8,128)S(1)}, f32[64,8,128]{2,1,0:T(8,128)S(1)}, u32[]{:S(2)}, u32[]{:S(2)}) collective-permute-start(f32[64,8,128]{2,1,0:T(8,128)S(1)} %pad_maximum_fusion), channel_id=1, source_target_pairs={{0,12},{1,13},{2,14},{3,15},{4,0},{5,1},{6,2},{7,3},{8,4},{9,5},{1... | collective-permute-start | bytes 786440 | tf_op jit(solution)/shard_map/ppermute | solution.py:36
  56.7 1.3 %collective-permute-start.19 = (f32[64,8,128]{2,1,0:T(8,128)S(1)}, f32[64,8,128]{2,1,0:T(8,128)S(1)}, u32[]{:S(2)}, u32[]{:S(2)}) collective-permute-start(f32[64,8,128]{2,1,0:T(8,128)S(1)} %pad_maximum_fusion), channel_id=1, source_target_pairs={{0,8},{1,9},{2,10},{3,11},{4,12},{5,13},{6,14},{7,15},{8,0},{9,1},... | collective-permute-start | bytes 786440 | tf_op jit(solution)/shard_map/ppermute | solution.py:36
  58.0 5.8 %collective-permute-start.20 = (f32[64,8,128]{2,1,0:T(8,128)S(1)}, f32[64,8,128]{2,1,0:T(8,128)S(1)}, u32[]{:S(2)}, u32[]{:S(2)}) collective-permute-start(f32[64,8,128]{2,1,0:T(8,128)S(1)} %pad_maximum_fusion), channel_id=1, source_target_pairs={{16,32},{17,33},{18,34},{19,35},{20,36},{21,37},{22,38},{23,39},{2... | collective-permute-start | bytes 786440 | tf_op jit(solution)/shard_map/ppermute | solution.py:36
  64.0 3.3 %collective-permute-start.21 = (f32[64,8,128]{2,1,0:T(8,128)S(1)}, f32[64,8,128]{2,1,0:T(8,128)S(1)}, u32[]{:S(2)}, u32[]{:S(2)}) collective-permute-start(f32[64,8,128]{2,1,0:T(8,128)S(1)} %collective-permute-done.17), channel_id=1, source_target_pairs={{16,32},{17,33},{18,34},{19,35},{20,36},{21,37},{22,38},{23,39},{2... | collective-permute-start | bytes 786440 | tf_op jit(solution)/shard_map/ppermute | solution.py:36
  67.3 4.7 %collective-permute-start.22 = (f32[64,8,128]{2,1,0:T(8,128)S(1)}, f32[64,8,128]{2,1,0:T(8,128)S(1)}, u32[]{:S(2)}, u32[]{:S(2)}) collective-permute-start(f32[64,8,128]{2,1,0:T(8,128)S(1)} %collective-permute-done.18), channel_id=1, source_target_pairs={{16,32},{17,33},{18,34},{19,35},{20,36},{21,37},{22,38},{23,39},{2... | collective-permute-start | bytes 786440 | tf_op jit(solution)/shard_map/ppermute | solution.py:36
  72.0 1.9 %collective-permute-start.23 = (f32[64,8,128]{2,1,0:T(8,128)S(1)}, f32[64,8,128]{2,1,0:T(8,128)S(1)}, u32[]{:S(2)}, u32[]{:S(2)}) collective-permute-start(f32[64,8,128]{2,1,0:T(8,128)S(1)} %collective-permute-done.19), channel_id=1, source_target_pairs={{16,32},{17,33},{18,34},{19,35},{20,36},{21,37},{22,38},{23,39},{2... | collective-permute-start | bytes 786440 | tf_op jit(solution)/shard_map/ppermute | solution.py:36
  74.7 1.3 %collective-permute-done.22 = f32[64,8,128]{2,1,0:T(8,128)S(1)} collective-permute-done((f32[64,8,128]{2,1,0:T(8,128)S(1)}, f32[64,8,128]{2,1,0:T(8,128)S(1)}, u32[]{:S(2)}, u32[]{:S(2)}) %collective-permute-start.22) | collective-permute-done | bytes 262176 | tf_op jit(solution)/shard_map/ppermute | solution.py:36
  76.0 3.7 %collective-permute-done.23 = f32[64,8,128]{2,1,0:T(8,128)S(1)} collective-permute-done((f32[64,8,128]{2,1,0:T(8,128)S(1)}, f32[64,8,128]{2,1,0:T(8,128)S(1)}, u32[]{:S(2)}, u32[]{:S(2)}) %collective-permute-start.23) | collective-permute-done | bytes 262176 | tf_op jit(solution)/shard_map/ppermute | solution.py:36
  79.9 2.1 %apply_second.1 = (f32[16,8,128]{2,1,0:T(8,128)S(1)}, f32[8,128]{1,0:T(8,128)S(1)}) custom-call(s32[256]{0:T(256)S(1)} %reshape.17.places_ref, f32[768,8,128]{2,1,0:T(8,128)S(1)} %constant_dynamic-update-slice_fusion.19.window_ref.second_ref, bf16[16,128,1024]{2,1,0:T(8,128)(2,1)S(1)} %prepare.1.matrices_ref, f32[16,8,128]{2,1,0:T(8,128)S(1)} %bitcast.6, ...), custom_call_target="tpu_custom_call" | custom-call | flops 134217728 | bytes 8388608 | tf_op jit(solution)/shard_map/apply_second/pallas_call | solution.py:188
  82.7 4.1 %all-to-all-start = ((f32[16,8,128]{2,1,0:T(8,128)}), f32[16,8,128]{2,1,0:T(8,128)S(1)}, u32[]{:S(2)}, u32[]{:S(2)}) async-start(f32[16,8,128]{2,1,0:T(8,128)} %broadcast_in_dim.29), calls=%async_computation | async-start | bytes 131072 | tf_op jit(solution)/shard_map/all_to_all | solution.py:345
  86.9 1.9 %copy-done.1 = f32[768,8,128]{2,1,0:T(8,128)S(1)} copy-done((f32[768,8,128]{2,1,0:T(8,128)S(1)}, f32[768,8,128]{2,1,0:T(8,128)}, u32[]{:S(2)}) %copy-start.1) | copy-done | bytes 3145752
  88.8 2.2 %copy-done.4 = f32[2,1024,512]{2,1,0:T(8,128)S(1)} copy-done((f32[2,1024,512]{2,1,0:T(8,128)S(1)}, f32[2,1024,512]{2,1,0:T(8,128)}, u32[]{:S(2)}) %copy-start.4) | copy-done | bytes 4194328
  91.0 2.7 %couple.1.reduced_ref = f32[2,48,1024]{2,1,0:T(8,128)S(1)} custom-call(s32[16]{0:T(128)S(1)} %reshape.19.slots_ref, s32[2]{0:T(128)S(1)} %copy-done.8, f32[768,8,128]{2,1,0:T(8,128)S(1)} %copy-done.1, f32[768,8,128]{2,1,0:T(8,128)S(1)} %constant_dynamic-update-slice_fusion.19.window_ref.second_ref, f32[2,1024,512]{2,1,0:T(8,128)S(1)} %copy-done.4, ...), custom_call_target="tpu_custom_call" | custom-call | flops 268435456 | bytes 4194304 | tf_op jit(solution)/shard_map/couple/pallas_call | solution.py:230
  95.1 3.9 %all-to-all-start.1 = ((f32[8,8,128]{2,1,0:T(8,128)}), f32[8,8,128]{2,1,0:T(8,128)S(1)}, u32[]{:S(2)}, u32[]{:S(2)}) async-start(f32[8,8,128]{2,1,0:T(8,128)} %broadcast_in_dim.30), calls=%async_computation.1 | async-start | bytes 65536 | tf_op jit(solution)/shard_map/all_to_all | solution.py:345
  99.1 3.4 %copy-done.2 = f32[2,1024,1024]{2,1,0:T(8,128)S(1)} copy-done((f32[2,1024,1024]{2,1,0:T(8,128)S(1)}, f32[2,1024,1024]{2,1,0:T(8,128)}, u32[]{:S(2)}) %copy-start.2) | copy-done | bytes 8388632
  103.5 3.6 %layers.1.parts_ref = f32[2,48,1024]{2,1,0:T(8,128)S(1)} custom-call(f32[2,48,1024]{2,1,0:T(8,128)S(1)} %copy-done.6, f32[2,1024,1024]{2,1,0:T(8,128)S(1)} %copy-done.2), custom_call_target="tpu_custom_call" | custom-call | flops 536870912 | bytes 8388608 | tf_op jit(solution)/shard_map/layers/pallas_call | solution.py:262
  (93 shorter events, 15.0 us)
Async XLA Ops:
  1.5 5.7 %collective-permute-start = (f32[16,8,128]{2,1,0:T(8,128)S(1)}, f32[16,8,128]{2,1,0:T(8,128)S(1)}, u32[]{:S(2)}, u32[]{:S(2)}) collective-permute-start(f32[16,8,128]{2,1,0:T(8,128)S(1)} %bitcast.2), channel_id=1, source_target_pairs={{0,3},{1,0},{2,1},{3,2},{4,7},{5,4},{6,5},{7,6},{8,11},{9,8},{10,9... | collective-permute-start | bytes 196616 | tf_op jit(solution)/shard_map/ppermute | solution.py:36
  4.9 5.0 %collective-permute-start.1 = (f32[16,8,128]{2,1,0:T(8,128)S(1)}, f32[16,8,128]{2,1,0:T(8,128)S(1)}, u32[]{:S(2)}, u32[]{:S(2)}) collective-permute-start(f32[16,8,128]{2,1,0:T(8,128)S(1)} %bitcast.3), channel_id=1, source_target_pairs={{0,1},{1,2},{2,3},{3,0},{4,5},{5,6},{6,7},{7,4},{8,9},{9,10},{10,1... | collective-permute-start | bytes 196616 | tf_op jit(solution)/shard_map/ppermute | solution.py:36
  4.9 5.7 %collective-permute-start.2 = (f32[16,8,128]{2,1,0:T(8,128)S(1)}, f32[16,8,128]{2,1,0:T(8,128)S(1)}, u32[]{:S(2)}, u32[]{:S(2)}) collective-permute-start(f32[16,8,128]{2,1,0:T(8,128)S(1)} %bitcast.4), channel_id=1, source_target_pairs={{0,2},{1,3},{2,0},{3,1},{4,6},{5,7},{6,4},{7,5},{8,10},{9,11},{10,... | collective-permute-start | bytes 196616 | tf_op jit(solution)/shard_map/ppermute | solution.py:36
  11.2 19.0 %collective-permute-start.3 = (f32[64,8,128]{2,1,0:T(8,128)}, f32[64,8,128]{2,1,0:T(8,128)}, u32[]{:S(2)}, u32[]{:S(2)}) collective-permute-start(f32[64,8,128]{2,1,0:T(8,128)} %get-tuple-element.7), channel_id=1, source_target_pairs={{0,12},{1,13},{2,14},{3,15},{4,0},{5,1},{6,2},{7,3},{8,4},{9,5},{1... | collective-permute-start | bytes 786440 | tf_op jit(solution)/shard_map/ppermute | solution.py:36
  14.9 19.8 %collective-permute-start.4 = (f32[64,8,128]{2,1,0:T(8,128)}, f32[64,8,128]{2,1,0:T(8,128)}, u32[]{:S(2)}, u32[]{:S(2)}) collective-permute-start(f32[64,8,128]{2,1,0:T(8,128)} %get-tuple-element.7), channel_id=1, source_target_pairs={{0,4},{1,5},{2,6},{3,7},{4,8},{5,9},{6,10},{7,11},{8,12},{9,13},{1... | collective-permute-start | bytes 786440 | tf_op jit(solution)/shard_map/ppermute | solution.py:36
  14.9 22.8 %collective-permute-start.5 = (f32[64,8,128]{2,1,0:T(8,128)}, f32[64,8,128]{2,1,0:T(8,128)}, u32[]{:S(2)}, u32[]{:S(2)}) collective-permute-start(f32[64,8,128]{2,1,0:T(8,128)} %get-tuple-element.7), channel_id=1, source_target_pairs={{0,8},{1,9},{2,10},{3,11},{4,12},{5,13},{6,14},{7,15},{8,0},{9,1},... | collective-permute-start | bytes 786440 | tf_op jit(solution)/shard_map/ppermute | solution.py:36
  23.7 18.6 %collective-permute-start.6 = (f32[64,8,128]{2,1,0:T(8,128)}, f32[64,8,128]{2,1,0:T(8,128)S(1)}, u32[]{:S(2)}, u32[]{:S(2)}) collective-permute-start(f32[64,8,128]{2,1,0:T(8,128)} %get-tuple-element.7), channel_id=1, source_target_pairs={{16,32},{17,33},{18,34},{19,35},{20,36},{21,37},{22,38},{23,39},{2... | collective-permute-start | bytes 786440 | tf_op jit(solution)/shard_map/ppermute | solution.py:36
  30.0 15.6 %collective-permute-start.10 = (f32[64,8,128]{2,1,0:T(8,128)}, f32[64,8,128]{2,1,0:T(8,128)S(1)}, u32[]{:S(2)}, u32[]{:S(2)}) collective-permute-start(f32[64,8,128]{2,1,0:T(8,128)} %get-tuple-element.7), channel_id=1, source_target_pairs={{0,16},{1,17},{2,18},{3,19},{4,20},{5,21},{6,22},{7,23},{8,24},{9,... | collective-permute-start | bytes 786440 | tf_op jit(solution)/shard_map/ppermute | solution.py:36
  30.1 12.3 %collective-permute-start.7 = (f32[64,8,128]{2,1,0:T(8,128)}, f32[64,8,128]{2,1,0:T(8,128)S(1)}, u32[]{:S(2)}, u32[]{:S(2)}) collective-permute-start(f32[64,8,128]{2,1,0:T(8,128)} %collective-permute-done.3), channel_id=1, source_target_pairs={{16,32},{17,33},{18,34},{19,35},{20,36},{21,37},{22,38},{23,39},{2... | collective-permute-start | bytes 786440 | tf_op jit(solution)/shard_map/ppermute | solution.py:36
  34.7 8.3 %collective-permute-start.8 = (f32[64,8,128]{2,1,0:T(8,128)}, f32[64,8,128]{2,1,0:T(8,128)S(1)}, u32[]{:S(2)}, u32[]{:S(2)}) collective-permute-start(f32[64,8,128]{2,1,0:T(8,128)} %collective-permute-done.4), channel_id=1, source_target_pairs={{16,32},{17,33},{18,34},{19,35},{20,36},{21,37},{22,38},{23,39},{2... | collective-permute-start | bytes 786440 | tf_op jit(solution)/shard_map/ppermute | solution.py:36
  37.7 7.9 %collective-permute-start.9 = (f32[64,8,128]{2,1,0:T(8,128)}, f32[64,8,128]{2,1,0:T(8,128)S(1)}, u32[]{:S(2)}, u32[]{:S(2)}) collective-permute-start(f32[64,8,128]{2,1,0:T(8,128)} %collective-permute-done.5), channel_id=1, source_target_pairs={{16,32},{17,33},{18,34},{19,35},{20,36},{21,37},{22,38},{23,39},{2... | collective-permute-start | bytes 786440 | tf_op jit(solution)/shard_map/ppermute | solution.py:36
  42.3 3.4 %collective-permute-start.11 = (f32[64,8,128]{2,1,0:T(8,128)}, f32[64,8,128]{2,1,0:T(8,128)S(1)}, u32[]{:S(2)}, u32[]{:S(2)}) collective-permute-start(f32[64,8,128]{2,1,0:T(8,128)} %collective-permute-done.3), channel_id=1, source_target_pairs={{0,16},{1,17},{2,18},{3,19},{4,20},{5,21},{6,22},{7,23},{8,24},{9,... | collective-permute-start | bytes 786440 | tf_op jit(solution)/shard_map/ppermute | solution.py:36
  42.4 3.3 %collective-permute-start.12 = (f32[64,8,128]{2,1,0:T(8,128)}, f32[64,8,128]{2,1,0:T(8,128)S(1)}, u32[]{:S(2)}, u32[]{:S(2)}) collective-permute-start(f32[64,8,128]{2,1,0:T(8,128)} %collective-permute-done.4), channel_id=1, source_target_pairs={{0,16},{1,17},{2,18},{3,19},{4,20},{5,21},{6,22},{7,23},{8,24},{9,... | collective-permute-start | bytes 786440 | tf_op jit(solution)/shard_map/ppermute | solution.py:36
  43.0 2.7 %collective-permute-start.13 = (f32[64,8,128]{2,1,0:T(8,128)}, f32[64,8,128]{2,1,0:T(8,128)S(1)}, u32[]{:S(2)}, u32[]{:S(2)}) collective-permute-start(f32[64,8,128]{2,1,0:T(8,128)} %collective-permute-done.5), channel_id=1, source_target_pairs={{0,16},{1,17},{2,18},{3,19},{4,20},{5,21},{6,22},{7,23},{8,24},{9,... | collective-permute-start | bytes 786440 | tf_op jit(solution)/shard_map/ppermute | solution.py:36
  47.8 3.4 %collective-permute-start.14 = (f32[16,8,128]{2,1,0:T(8,128)S(1)}, f32[16,8,128]{2,1,0:T(8,128)S(1)}, u32[]{:S(2)}, u32[]{:S(2)}) collective-permute-start(f32[16,8,128]{2,1,0:T(8,128)S(1)} %apply_first.1.image_ref), channel_id=1, source_target_pairs={{0,3},{1,0},{2,1},{3,2},{4,7},{5,4},{6,5},{7,6},{8,11},{9,8},{10,9... | collective-permute-start | bytes 196616 | tf_op jit(solution)/shard_map/ppermute | solution.py:36
  48.8 4.3 %collective-permute-start.15 = (f32[16,8,128]{2,1,0:T(8,128)S(1)}, f32[16,8,128]{2,1,0:T(8,128)S(1)}, u32[]{:S(2)}, u32[]{:S(2)}) collective-permute-start(f32[16,8,128]{2,1,0:T(8,128)S(1)} %apply_first.1.image_ref), channel_id=1, source_target_pairs={{0,1},{1,2},{2,3},{3,0},{4,5},{5,6},{6,7},{7,4},{8,9},{9,10},{10,1... | collective-permute-start | bytes 196616 | tf_op jit(solution)/shard_map/ppermute | solution.py:36
  49.5 4.6 %collective-permute-start.16 = (f32[16,8,128]{2,1,0:T(8,128)S(1)}, f32[16,8,128]{2,1,0:T(8,128)S(1)}, u32[]{:S(2)}, u32[]{:S(2)}) collective-permute-start(f32[16,8,128]{2,1,0:T(8,128)S(1)} %apply_first.1.image_ref), channel_id=1, source_target_pairs={{0,2},{1,3},{2,0},{3,1},{4,6},{5,7},{6,4},{7,5},{8,10},{9,11},{10,... | collective-permute-start | bytes 196616 | tf_op jit(solution)/shard_map/ppermute | solution.py:36
  54.2 9.8 %collective-permute-start.17 = (f32[64,8,128]{2,1,0:T(8,128)S(1)}, f32[64,8,128]{2,1,0:T(8,128)S(1)}, u32[]{:S(2)}, u32[]{:S(2)}) collective-permute-start(f32[64,8,128]{2,1,0:T(8,128)S(1)} %pad_maximum_fusion), channel_id=1, source_target_pairs={{0,12},{1,13},{2,14},{3,15},{4,0},{5,1},{6,2},{7,3},{8,4},{9,5},{1... | collective-permute-start | bytes 786440 | tf_op jit(solution)/shard_map/ppermute | solution.py:36
  56.7 10.6 %collective-permute-start.18 = (f32[64,8,128]{2,1,0:T(8,128)S(1)}, f32[64,8,128]{2,1,0:T(8,128)S(1)}, u32[]{:S(2)}, u32[]{:S(2)}) collective-permute-start(f32[64,8,128]{2,1,0:T(8,128)S(1)} %pad_maximum_fusion), channel_id=1, source_target_pairs={{0,4},{1,5},{2,6},{3,7},{4,8},{5,9},{6,10},{7,11},{8,12},{9,13},{1... | collective-permute-start | bytes 786440 | tf_op jit(solution)/shard_map/ppermute | solution.py:36
  56.7 15.3 %collective-permute-start.19 = (f32[64,8,128]{2,1,0:T(8,128)S(1)}, f32[64,8,128]{2,1,0:T(8,128)S(1)}, u32[]{:S(2)}, u32[]{:S(2)}) collective-permute-start(f32[64,8,128]{2,1,0:T(8,128)S(1)} %pad_maximum_fusion), channel_id=1, source_target_pairs={{0,8},{1,9},{2,10},{3,11},{4,12},{5,13},{6,14},{7,15},{8,0},{9,1},... | collective-permute-start | bytes 786440 | tf_op jit(solution)/shard_map/ppermute | solution.py:36
  58.0 16.0 %collective-permute-start.20 = (f32[64,8,128]{2,1,0:T(8,128)S(1)}, f32[64,8,128]{2,1,0:T(8,128)S(1)}, u32[]{:S(2)}, u32[]{:S(2)}) collective-permute-start(f32[64,8,128]{2,1,0:T(8,128)S(1)} %pad_maximum_fusion), channel_id=1, source_target_pairs={{16,32},{17,33},{18,34},{19,35},{20,36},{21,37},{22,38},{23,39},{2... | collective-permute-start | bytes 786440 | tf_op jit(solution)/shard_map/ppermute | solution.py:36
  63.8 15.9 %collective-permute-start.24 = (f32[64,8,128]{2,1,0:T(8,128)S(1)}, f32[64,8,128]{2,1,0:T(8,128)S(1)}, u32[]{:S(2)}, u32[]{:S(2)}) collective-permute-start(f32[64,8,128]{2,1,0:T(8,128)S(1)} %pad_maximum_fusion), channel_id=1, source_target_pairs={{0,16},{1,17},{2,18},{3,19},{4,20},{5,21},{6,22},{7,23},{8,24},{9,... | collective-permute-start | bytes 786440 | tf_op jit(solution)/shard_map/ppermute | solution.py:36
  64.0 10.1 %collective-permute-start.21 = (f32[64,8,128]{2,1,0:T(8,128)S(1)}, f32[64,8,128]{2,1,0:T(8,128)S(1)}, u32[]{:S(2)}, u32[]{:S(2)}) collective-permute-start(f32[64,8,128]{2,1,0:T(8,128)S(1)} %collective-permute-done.17), channel_id=1, source_target_pairs={{16,32},{17,33},{18,34},{19,35},{20,36},{21,37},{22,38},{23,39},{2... | collective-permute-start | bytes 786440 | tf_op jit(solution)/shard_map/ppermute | solution.py:36
  67.3 8.7 %collective-permute-start.22 = (f32[64,8,128]{2,1,0:T(8,128)S(1)}, f32[64,8,128]{2,1,0:T(8,128)S(1)}, u32[]{:S(2)}, u32[]{:S(2)}) collective-permute-start(f32[64,8,128]{2,1,0:T(8,128)S(1)} %collective-permute-done.18), channel_id=1, source_target_pairs={{16,32},{17,33},{18,34},{19,35},{20,36},{21,37},{22,38},{23,39},{2... | collective-permute-start | bytes 786440 | tf_op jit(solution)/shard_map/ppermute | solution.py:36
  72.0 7.7 %collective-permute-start.23 = (f32[64,8,128]{2,1,0:T(8,128)S(1)}, f32[64,8,128]{2,1,0:T(8,128)S(1)}, u32[]{:S(2)}, u32[]{:S(2)}) collective-permute-start(f32[64,8,128]{2,1,0:T(8,128)S(1)} %collective-permute-done.19), channel_id=1, source_target_pairs={{16,32},{17,33},{18,34},{19,35},{20,36},{21,37},{22,38},{23,39},{2... | collective-permute-start | bytes 786440 | tf_op jit(solution)/shard_map/ppermute | solution.py:36
  74.0 5.8 %collective-permute-start.25 = (f32[64,8,128]{2,1,0:T(8,128)S(1)}, f32[64,8,128]{2,1,0:T(8,128)S(1)}, u32[]{:S(2)}, u32[]{:S(2)}) collective-permute-start(f32[64,8,128]{2,1,0:T(8,128)S(1)} %collective-permute-done.17), channel_id=1, source_target_pairs={{0,16},{1,17},{2,18},{3,19},{4,20},{5,21},{6,22},{7,23},{8,24},{9,... | collective-permute-start | bytes 786440 | tf_op jit(solution)/shard_map/ppermute | solution.py:36
  74.1 5.7 %collective-permute-start.26 = (f32[64,8,128]{2,1,0:T(8,128)S(1)}, f32[64,8,128]{2,1,0:T(8,128)S(1)}, u32[]{:S(2)}, u32[]{:S(2)}) collective-permute-start(f32[64,8,128]{2,1,0:T(8,128)S(1)} %collective-permute-done.18), channel_id=1, source_target_pairs={{0,16},{1,17},{2,18},{3,19},{4,20},{5,21},{6,22},{7,23},{8,24},{9,... | collective-permute-start | bytes 786440 | tf_op jit(solution)/shard_map/ppermute | solution.py:36
  76.0 3.8 %collective-permute-start.27 = (f32[64,8,128]{2,1,0:T(8,128)S(1)}, f32[64,8,128]{2,1,0:T(8,128)S(1)}, u32[]{:S(2)}, u32[]{:S(2)}) collective-permute-start(f32[64,8,128]{2,1,0:T(8,128)S(1)} %collective-permute-done.19), channel_id=1, source_target_pairs={{0,16},{1,17},{2,18},{3,19},{4,20},{5,21},{6,22},{7,23},{8,24},{9,... | collective-permute-start | bytes 786440 | tf_op jit(solution)/shard_map/ppermute | solution.py:36
  79.9 7.0 %copy-start.7 = (f32[2,16,1024]{2,1,0:T(8,128)S(1)}, f32[2,16,1024]{2,1,0:T(8,128)}, u32[]{:S(2)}) copy-start(f32[2,16,1024]{2,1,0:T(8,128)} %load_ref.1) | copy-start | bytes 393220
  79.9 7.0 %copy-start.8 = (s32[2]{0:T(128)S(1)}, s32[2]{0:T(128)}, u32[]{:S(2)}) copy-start(s32[2]{0:T(128)} %live_ref.1) | copy-start | bytes 28
  82.7 11.8 %all-to-all-start = ((f32[16,8,128]{2,1,0:T(8,128)}), f32[16,8,128]{2,1,0:T(8,128)S(1)}, u32[]{:S(2)}, u32[]{:S(2)}) async-start(f32[16,8,128]{2,1,0:T(8,128)} %broadcast_in_dim.29), calls=%async_computation | async-start | bytes 131072 | tf_op jit(solution)/shard_map/all_to_all | solution.py:345
  95.1 11.9 %all-to-all-start.1 = ((f32[8,8,128]{2,1,0:T(8,128)}), f32[8,8,128]{2,1,0:T(8,128)S(1)}, u32[]{:S(2)}, u32[]{:S(2)}) async-start(f32[8,8,128]{2,1,0:T(8,128)} %broadcast_in_dim.30), calls=%async_computation.1 | async-start | bytes 65536 | tf_op jit(solution)/shard_map/all_to_all | solution.py:345
  (8 other events, 20.4 us)

commit v2 on v1

v2 whole, which is shorter than its diff:
```python
import jax
import jax.numpy as jnp
from jax import lax
from jax.experimental import pallas as pl
from jax.experimental.pallas import tpu as pltpu
from jax.sharding import PartitionSpec as P

NB = 64
CASES = 16
LANES = 128
AXES = ("y", "core", "x", "z")
SIZES = (4, 2, 4, 4)
ORDER = (0, 1, 3, 2)
WINDOW = 768
CHIPS = 64
NT = (((1,), (1,)), ((), ()))
VMEM_SPEC = pl.BlockSpec(memory_space=pltpu.VMEM)
SMEM_SPEC = pl.BlockSpec(memory_space=pltpu.SMEM)
ANY_SPEC = pl.BlockSpec(memory_space=pl.ANY)

PLACES = [
    (y, c, x, z)
    for y in range(SIZES[0])
    for c in range(SIZES[1])
    for x in range(SIZES[2])
    for z in range(SIZES[3])
]


def flat(y, c, x, z):
    return ((y * SIZES[1] + c) * SIZES[2] + x) * SIZES[3] + z


def permute(value, target):
    pairs = []
    for place in PLACES:
        goal = target(*place)
        if goal is not None:
            pairs.append((flat(*place), flat(*goal)))
    return lax.ppermute(value, AXES, pairs)


def far(y, c, x, z):
    if c == 1:
        return (y + 1, 0, x, z) if y + 1 < SIZES[0] else None
    return (y - 1, 1, x, z) if y > 0 else None


def partner(y, c, x, z):
    return (y, 1 - c, x, z)


def along_first(step):
    return lambda y, c, x, z: (y, c, x, (z - step) % 4) if c == 0 else (y, c, (x - step) % 4, z)


def along_second(step):
    return lambda y, c, x, z: (y, c, (x - step) % 4, z) if c == 0 else (y, c, x, (z - step) % 4)


def exchange(own, beside):
    line = jnp.stack([own] + [permute(own, along_first(k)) for k in ORDER[1:]])
    near_other = permute(line, far)
    rest = jnp.stack([permute(line, along_second(k)) for k in ORDER[1:]])
    plane = jnp.concatenate([line[None], rest])
    rest_other = permute(rest, far)
    pair = permute(plane, partner)
    results = beside(rest)
    window = jnp.concatenate([plane, near_other[None], rest_other, pair])
    return window.reshape(WINDOW, 8, LANES), results


def locate(ids, region, x, z):
    goal = ids // 256
    member = ids % 256 // 16
    dx = (member // 4 - x) % 4
    dz = (member % 4 - z) % 4
    px = dx ^ (dx >> 1)
    pz = dz ^ (dz >> 1)
    place = jnp.where(goal % 2 == 1, pz * 4 + px, px * 4 + pz)
    group = jnp.where(goal == region, 0, jnp.where(goal == (region ^ 1), 2, 1))
    return (group * 16 + place) * 16 + ids % 16


def split(value):
    high = value.astype(jnp.bfloat16)
    low = (value - high.astype(jnp.float32)).astype(jnp.bfloat16)
    return high, low


def lane_ids(rows):
    return lax.broadcasted_iota(jnp.int32, (rows, LANES), 1)


def merge_halves(left, right):
    low_half = lane_ids(left.shape[0]) < NB
    first = jnp.where(low_half, left, pltpu.roll(right, NB, 1))
    second = jnp.where(low_half, pltpu.roll(left, NB, 1), right)
    return first, second


def prepare_kernel(values_ref, ready_ref, out_ref):
    lanes = lane_ids(8)
    subs = lax.broadcasted_iota(jnp.int32, (8, LANES), 0)
    for group in range(4):
        rows = []
        for pair in range(8 * group, 8 * group + 8):
            cut = slice(pair * LANES, (pair + 1) * LANES)
            upper = values_ref[0, 0:8, cut]
            lower = values_ref[0, 8:16, cut]
            own = (subs == 0) & ((lanes == 2 * pair) | (lanes == NB + 2 * pair + 1))
            upper = jnp.where(own, upper - 2.0, upper)
            rows.extend(merge_halves(upper, lower))
        tiles = jnp.transpose(jnp.stack(rows), (1, 0, 2))
        for k in range(8):
            high, low = split(tiles[k])
            out_ref[0, 16 * group : 16 * group + 16, k * LANES : (k + 1) * LANES] = high
            out_ref[0, NB + 16 * group : NB + 16 * group + 16, k * LANES : (k + 1) * LANES] = low


def prepare(values, ready):
    return pl.pallas_call(
        prepare_kernel,
        grid=(16,),
        in_specs=[pl.BlockSpec((1, 16, 4096), lambda i: (i, 0, 0)), ANY_SPEC],
        out_specs=pl.BlockSpec((1, 128, 1024), lambda i: (i, 0, 0)),
        out_shape=jax.ShapeDtypeStruct((16, 128, 1024), jnp.bfloat16),
        compiler_params=pltpu.CompilerParams(vmem_limit_bytes=8 * 2**20),
        cost_estimate=pl.CostEstimate(flops=2**24, bytes_accessed=2**23, transcendentals=0),
        name="prepare",
    )(values, ready)


def halve_kernel(
    inverse_ref, coupling_ref, load_ref, ready_ref, inverse_out_ref, coupling_out_ref, base_ref, l_ref
):
    sub = pl.program_id(0)
    size = inverse_ref.shape[1]
    rows = pl.ds(pl.multiple_of(pl.program_id(1) * size, size), size)

    @pl.when(pl.program_id(1) == 0)
    def _():
        l_ref[0:16], l_ref[16:32] = split(load_ref[0])

    coupling_out_ref[sub, 0, rows, :], coupling_out_ref[sub, 1, rows, :] = split(coupling_ref[0])
    high, low = split(inverse_ref[0])
    inverse_out_ref[sub, 0, rows, :], inverse_out_ref[sub, 1, rows, :] = high, low
    main = lax.dot_general(l_ref[...], high, NT, preferred_element_type=jnp.float32)
    rest = lax.dot_general(l_ref[0:16], low, NT, preferred_element_type=jnp.float32)
    base_ref[sub, :, rows] = main[0:16] + main[16:32] + rest


def halve(inverse, coupling, load, ready):
    cut = 256
    return pl.pallas_call(
        halve_kernel,
        grid=(2, 1024 // cut),
        in_specs=[
            pl.BlockSpec((1, cut, 1024), lambda s, n: (s, n, 0)),
            pl.BlockSpec((1, cut, 512), lambda s, n: (s, n, 0)),
            pl.BlockSpec((1, CASES, 1024), lambda s, n: (s, 0, 0)),
            ANY_SPEC,
        ],
        out_specs=[VMEM_SPEC] * 3,
        out_shape=[
            jax.ShapeDtypeStruct((2, 2, 1024, 1024), jnp.bfloat16),
            jax.ShapeDtypeStruct((2, 2, 1024, 512), jnp.bfloat16),
            jax.ShapeDtypeStruct((2, CASES, 1024), jnp.float32),
        ],
        scratch_shapes=[pltpu.VMEM((32, 1024), jnp.bfloat16)],
        compiler_params=pltpu.CompilerParams(vmem_limit_bytes=20 * 2**20),
        cost_estimate=pl.CostEstimate(flops=2**27, bytes_accessed=3 * 2**23, transcendentals=0),
        name="halve",
    )(inverse, coupling, load, ready)


def apply_rows(places_ref, window_ref, matrices_ref, x_ref, out_ref):
    low_half = lane_ids(8) < NB
    for row in range(16):
        for k in range(8):
            left = window_ref[places_ref[row * 16 + k]]
            right = window_ref[places_ref[row * 16 + k + 8]]
            high, low = split(jnp.concatenate(merge_halves(left, right)))
            x_ref[row % 2, 0:16, k * LANES : (k + 1) * LANES] = high
            x_ref[row % 2, 16:32, k * LANES : (k + 1) * LANES] = low
        product = lax.dot_general(
            x_ref[row % 2], matrices_ref[row], NT, preferred_element_type=jnp.float32
        )
        both = product[0:16] + product[16:32]
        both = both + pltpu.roll(both, NB, 1)
        out_ref[row] = jnp.where(low_half, both[0:8], both[8:16])


def pick_slots(slots_ref, live_ref, window_ref, picked_ref):
    for sub in range(2):
        for t in range(4):
            tiles = []
            for slot in (2 * t, 2 * t + 1):
                tile = window_ref[slots_ref[sub * 8 + slot]]
                tiles.append(jnp.where(slot < live_ref[sub], tile, 0.0))
            even, odd = merge_halves(*tiles)
            picked_ref[sub, t, pl.ds(0, 8, stride=2), :] = even
            picked_ref[sub, t, pl.ds(1, 8, stride=2), :] = odd


def first_kernel(
    places_ref, slots_ref, live_ref, window_ref, matrices_ref, halves_ref, image_ref, picked_ref, x_ref
):
    apply_rows(places_ref, window_ref, matrices_ref, x_ref, image_ref)
    pick_slots(slots_ref, live_ref, window_ref, picked_ref)


def second_kernel(
    places_ref,
    slots_ref,
    live_ref,
    window_ref,
    matrices_ref,
    load_ref,
    image_ref,
    folded_ref,
    twice_ref,
    sums_ref,
    parts_ref,
    x_ref,
    picked_ref,
    p_ref,
):
    apply_rows(places_ref, window_ref, matrices_ref, x_ref, twice_ref)
    load, image, twice = load_ref[...], image_ref[...], twice_ref[...]
    lanes = lane_ids(8)
    low_half = lanes < NB
    packed = jnp.zeros((8, LANES), jnp.float32)
    products = (load * load, load * image, image * image, load * twice, image * twice)
    for place, product in enumerate(products):
        tile = jnp.sum(product, axis=0)
        left = jnp.sum(jnp.where(low_half, tile, 0.0), axis=1, keepdims=True)
        right = jnp.sum(jnp.where(low_half, 0.0, tile), axis=1, keepdims=True)
        packed = jnp.where(lanes == place, left, packed)
        packed = jnp.where(lanes == NB + place, right, packed)
    sums_ref[...] = jnp.broadcast_to(packed[None], sums_ref.shape)
    pick_slots(slots_ref, live_ref, window_ref, picked_ref)
    for sub in range(2):
        for t in range(4):
            cut = slice(t * LANES, (t + 1) * LANES)
            p_ref[sub, 0:16, cut], p_ref[sub, 16:32, cut] = split(picked_ref[sub, t])
        main = lax.dot_general(p_ref[sub], folded_ref[sub, 0], NT, preferred_element_type=jnp.float32)
        rest = lax.dot_general(
            p_ref[sub, 0:16], folded_ref[sub, 1], NT, preferred_element_type=jnp.float32
        )
        parts_ref[sub] = main[0:16] + main[16:32] + rest


APPLY_COST = pl.CostEstimate(flops=2**27, bytes_accessed=2**23, transcendentals=0)
TILES = jax.ShapeDtypeStruct((16, 8, LANES), jnp.float32)
PICKED = jax.ShapeDtypeStruct((2, 4, 16, LANES), jnp.float32)


def apply_first(places, slots, live, window, matrices, halves):
    return pl.pallas_call(
        first_kernel,
        in_specs=[SMEM_SPEC] * 3 + [VMEM_SPEC] * 3,
        out_specs=[VMEM_SPEC] * 2,
        out_shape=[TILES, PICKED],
        scratch_shapes=[pltpu.VMEM((2, 32, 1024), jnp.bfloat16)],
        compiler_params=pltpu.CompilerParams(vmem_limit_bytes=6 * 2**20),
        cost_estimate=APPLY_COST,
        name="apply_first",
    )(places, slots, live, window, matrices, halves)


def apply_second(places, slots, live, window, matrices, load, image, folded):
    return pl.pallas_call(
        second_kernel,
        in_specs=[SMEM_SPEC] * 3 + [VMEM_SPEC] * 5,
        out_specs=[VMEM_SPEC] * 3,
        out_shape=[
            TILES,
            jax.ShapeDtypeStruct((CHIPS, 8, LANES), jnp.float32),
            jax.ShapeDtypeStruct((2, CASES, 1024), jnp.float32),
        ],
        scratch_shapes=[
            pltpu.VMEM((2, 32, 1024), jnp.bfloat16),
            pltpu.VMEM((2, 4, 16, LANES), jnp.float32),
            pltpu.VMEM((2, 32, 512), jnp.bfloat16),
        ],
        compiler_params=pltpu.CompilerParams(vmem_limit_bytes=8 * 2**20),
        cost_estimate=APPLY_COST,
        name="apply_second",
    )(places, slots, live, window, matrices, load, image, folded)


def fold_kernel(inverse_ref, coupling_ref, picked_ref, ready_ref, folded_ref, parts_ref, p_ref):
    cut = 256
    for sub in range(2):
        for t in range(4):
            lanes = slice(t * LANES, (t + 1) * LANES)
            p_ref[sub, 0:16, lanes], p_ref[sub, 16:32, lanes] = split(picked_ref[sub, t])

    @pl.loop(0, 2)
    def _(sub):
        for n in range(1024 // cut):
            rows = slice(n * cut, (n + 1) * cut)
            high, low = inverse_ref[sub, 0, rows], inverse_ref[sub, 1, rows]
            term = (
                jnp.dot(high, coupling_ref[sub, 0], preferred_element_type=jnp.float32)
                + jnp.dot(high, coupling_ref[sub, 1], preferred_element_type=jnp.float32)
                + jnp.dot(low, coupling_ref[sub, 0], preferred_element_type=jnp.float32)
            )
            high, low = split(term)
            folded_ref[sub, 0, rows], folded_ref[sub, 1, rows] = high, low
            main = lax.dot_general(p_ref[sub], high, NT, preferred_element_type=jnp.float32)
            rest = lax.dot_general(p_ref[sub, 0:16], low, NT, preferred_element_type=jnp.float32)
            parts_ref[sub, :, rows] = main[0:16] + main[16:32] + rest


def fold(inverse, coupling, picked, ready):
    return pl.pallas_call(
        fold_kernel,
        in_specs=[VMEM_SPEC] * 3 + [ANY_SPEC],
        out_specs=[VMEM_SPEC] * 2,
        out_shape=[
            jax.ShapeDtypeStruct((2, 2, 1024, 512), jnp.bfloat16),
            jax.ShapeDtypeStruct((2, CASES, 1024), jnp.float32),
        ],
        scratch_shapes=[pltpu.VMEM((2, 32, 512), jnp.bfloat16)],
        compiler_params=pltpu.CompilerParams(vmem_limit_bytes=10 * 2**20),
        cost_estimate=pl.CostEstimate(flops=2**33, bytes_accessed=2**24, transcendentals=0),
        name="fold",
    )(inverse, coupling, picked, ready)


def finish_kernel(
    sums_ref, others_ref, load_ref, image_ref, twice_ref, base_ref, parts_ref, more_ref, solution_ref, residual_ref, interior_ref, tiles_ref, cases_ref
):
    lanes = lane_ids(8)
    low_half = lanes < NB
    packed = sums_ref[...] + others_ref[...]

    def pick(place):
        left = jnp.sum(jnp.where(lanes == place, packed, 0.0), axis=1, keepdims=True)
        right = jnp.sum(jnp.where(lanes == NB + place, packed, 0.0), axis=1, keepdims=True)
        return jnp.where(low_half, left, right)

    uu, ue, ee, uf, ef = [pick(place) for place in range(5)]
    inner = 2.0 * uu + ue
    step = uu / inner
    along = ue / inner
    beta = step * (ee / inner) - along * along
    norm = beta * uu
    mix = along + beta
    length = mix * mix * uu - 2.0 * mix * step * ue + step * step * ee
    cross = mix * mix * ue - mix * step * (uf + ee) + step * step * ef
    last = norm / (2.0 * length + cross)
    on_load = step + last * mix
    on_image = -last * step
    rest_load = along - 2.0 * last * mix
    rest_image = -step - last * (mix - 2.0 * step)
    rest_twice = last * step

    rows = load_ref.shape[0]
    load, image, twice = load_ref[...], image_ref[...], twice_ref[...]
    for out_ref, value in (
        (solution_ref, on_load[None] * load + on_image[None] * image),
        (
            residual_ref,
            rest_load[None] * load + rest_image[None] * image + rest_twice[None] * twice,
        ),
    ):
        tiles_ref[...] = value.reshape(rows * 8, LANES)
        for s in range(8):
            out_ref[:, s * LANES : (s + 1) * LANES] = tiles_ref[pl.ds(s, rows, stride=8), :]
    for place, factor in enumerate((on_load, on_image)):
        for h in range(2):
            spread = jnp.broadcast_to(factor[:, h * NB : h * NB + 1], (8, LANES))
            cases_ref[place, pl.ds(h, 8, stride=2), :] = spread
    own, other = cases_ref[0][:, 0:1], cases_ref[1][:, 0:1]
    for sub in range(2):
        interior_ref[sub] = (
            base_ref[sub] - own * parts_ref[sub] - other * more_ref[sub]
        )


def finish(sums, others, load, image, twice, base, parts, more):
    return pl.pallas_call(
        finish_kernel,
        in_specs=[VMEM_SPEC] * 8,
        out_specs=[VMEM_SPEC] * 3,
        out_shape=[
            jax.ShapeDtypeStruct((16, 1024), jnp.float32),
            jax.ShapeDtypeStruct((16, 1024), jnp.float32),
            jax.ShapeDtypeStruct((2, CASES, 1024), jnp.float32),
        ],
        scratch_shapes=[pltpu.VMEM((128, LANES), jnp.float32), pltpu.VMEM((2, 16, LANES), jnp.float32)],
        compiler_params=pltpu.CompilerParams(vmem_limit_bytes=8 * 2**20),
        name="finish",
    )(sums, others, load, image, twice, base, parts, more)


def body(
    interface_load,
    schur_values,
    schur_columns,
    coupling,
    layer_inverse,
    interior_load,
    adjacency,
    live_counts,
):
    y, core, x, z = [lax.axis_index(axis) for axis in AXES]
    region = y * 2 + core
    places = locate(schur_columns, region, x, z).reshape(-1)
    slots = locate(adjacency, region, x, z).reshape(-1)
    load = interface_load.reshape(16, 8, LANES)
    load_window, (matrices, (inverse, couplings, base)) = exchange(
        load,
        lambda ready: (
            prepare(schur_values, ready),
            halve(layer_inverse, coupling, interior_load, ready),
        ),
    )
    image, picked = apply_first(places, slots, live_counts, load_window, matrices, inverse)
    image_window, (folded, parts) = exchange(
        image, lambda ready: fold(inverse, couplings, picked, ready)
    )
    twice, sums, more = apply_second(
        places, slots, live_counts, image_window, matrices, load, image, folded
    )
    sums = jnp.sum(lax.all_to_all(sums, ("y", "x", "z"), 0, 0), axis=0)
    return tuple(finish(sums, permute(sums, partner), load, image, twice, base, parts, more))


def solution(mesh):
    grid = jax.sharding.Mesh(mesh.devices.reshape(SIZES), AXES)
    lead = AXES
    in_specs = (
        P(lead, None),
        P(lead, None, None),
        P(lead, None),
        P(lead, None, None),
        P(lead, None, None),
        P(lead, None, None),
        P(lead, None),
        P(lead),
    )
    out_specs = (P(lead, None), P(lead, None), P(lead, None, None))
    return jax.shard_map(body, mesh=grid, in_specs=in_specs, out_specs=out_specs, check_vma=False)
```

time: 109 us -> 98.3 us (0.902)
  blocking collectives: 0 us -> 16.3 us
  local copies, waits for them, and re-layouts: 19.6 us -> 5.3 us
  starting transfers between devices: 58.3 us -> 46.8 us
  waiting for transfers between devices: 12.4 us -> 4.09 us
  Pallas kernels: 15.7 us -> 22.6 us
  other arithmetic: 0.82 us -> 1.93 us
    all_to_all x0 -> x1, blocking collectives: none -> 16.3 us  [body(): sums = jnp.sum(lax.all_to_all(sums, ('y', 'x', 'z'), 0, 0), axis=0)]
    unnamed x48 -> x21, local copies, waits for them, and re-layouts: 17.4 us -> 4.95 us
    ppermute x28 -> x19, waiting for transfers between devices: 12.4 us -> 4.09 us  [permute(): return lax.ppermute(value, AXES, pairs)]
    all_to_all x2 -> x0, starting transfers between devices: 8.05 us -> none  [to_all(): lax.all_to_all(jnp.broadcast_to(value[None], (count,) + value.shape), axe...]
    pallas_call x6, Pallas kernels: 15.7 us -> 22.6 us  [the longest x1 9.19 us: fold(): pl.pallas_call(fold_kernel, in_specs=[VMEM_SPEC] * 3 + [ANY_SPEC], out_sp...]
    ppermute x28 -> x19, starting transfers between devices: 50.2 us -> 46.8 us  [permute(): return lax.ppermute(value, AXES, pairs)]
    broadcast_in_dim x2 -> x0, local copies, waits for them, and re-layouts: 1.28 us -> none  [to_all(): jnp.broadcast_to(value[None], (count,) + value.shape)]
  transfers between devices with their start and end apart: 30 -> 19, of which waited for: 6 -> 6; matrix products, arithmetic and copies ran while one was open for 6% -> 2% of each run, Pallas kernels for 10% -> 17%
where the time goes in v2:
time: 98.3 us; the launch traced here: 97.9 us
  starting transfers between devices  46.8 us (48%)
  Pallas kernels  22.6 us (23%)
  blocking collectives  16.3 us (17%)
  local copies, waits for them, and re-layouts  5.3 us (5%)
  waiting for transfers between devices  4.09 us (4%)
  other arithmetic  1.93 us (2%)
    ppermute x19, starting transfers between devices, permute(): return lax.ppermute(value, AXES, pairs)  46.8 us
    all_to_all x1, blocking collectives, body(): sums = jnp.sum(lax.all_to_all(sums, ('y', 'x', 'z'), 0, 0), axis=0)  16.3 us
    pallas_call x1, Pallas kernels, fold(): pl.pallas_call(fold_kernel, in_specs=[VMEM_SPEC] * 3 + [ANY_SPEC], out_sp...  9.19 us
    unnamed x21, local copies, waits for them, and re-layouts  4.95 us
    pallas_call x1, Pallas kernels, halve(): pl.pallas_call(halve_kernel, grid=(2, 1024 // cut), in_specs=[pl.BlockSpe...  4.4 us
    ppermute x19, waiting for transfers between devices, permute(): return lax.ppermute(value, AXES, pairs)  4.09 us
    pallas_call x1, Pallas kernels, apply_second(): pl.pallas_call(second_kernel, in_specs=[SMEM_SPEC] * 3 + [VMEM_SPEC] * 5,...  3.13 us
    pallas_call x1, Pallas kernels, prepare(): pl.pallas_call(prepare_kernel, grid=(16,), in_specs=[pl.BlockSpec((1, 16,...  2.88 us
  transfers between devices with their start and end apart: 19, of which 6 were waited for; matrix products, arithmetic and copies ran while one was open for 2% of the time, Pallas kernels for 17%

profile of v2, /device:TPU:1, one launch (start us, length us, event | category | flops | bytes accessed | tf_op | source)
XLA Modules:
  0.0 97.9 jit_solution(6520981705226177777)
XLA Ops:
  0.6 0.9 copy.11
  1.5 3.7 %collective-permute-start.2 = (f32[16,8,128]{2,1,0:T(8,128)S(1)}, f32[16,8,128]{2,1,0:T(8,128)S(1)}, u32[]{:S(2)}, u32[]{:S(2)}) collective-permute-start(f32[16,8,128]{2,1,0:T(8,128)S(1)} %bitcast.38), channel_id=1, source_target_pairs={{0,2},{1,3},{2,0},{3,1},{4,6},{5,7},{6,4},{7,5},{8,10},{9,11},{10,... | collective-permute-start | bytes 196616 | tf_op jit(solution)/shard_map/ppermute | solution.py:40
  5.5 2.4 %collective-permute-start = (f32[16,8,128]{2,1,0:T(8,128)S(1)}, f32[16,8,128]{2,1,0:T(8,128)S(1)}, u32[]{:S(2)}, u32[]{:S(2)}) collective-permute-start(f32[16,8,128]{2,1,0:T(8,128)S(1)} %bitcast.40), channel_id=1, source_target_pairs={{0,3},{1,0},{2,1},{3,2},{4,7},{5,4},{6,5},{7,6},{8,11},{9,8},{10,9... | collective-permute-start | bytes 196616 | tf_op jit(solution)/shard_map/ppermute | solution.py:40
  7.8 0.7 fusion.13
  8.6 0.8 collective-permute-done.1
  9.5 3.7 %collective-permute-start.5 = (f32[4,16,8,128]{3,2,1,0:T(8,128)S(1)}, f32[4,16,8,128]{3,2,1,0:T(8,128)S(1)}, u32[]{:S(2)}, u32[]{:S(2)}) collective-permute-start(f32[4,16,8,128]{3,2,1,0:T(8,128)S(1)} %get-tuple-element.26), channel_id=1, source_target_pairs={{0,8},{1,9},{2,10},{3,11},{4,12},{5,13},{6,14},{7,15},{8,0},{9,1},... | collective-permute-start | bytes 786440 | tf_op jit(solution)/shard_map/ppermute | solution.py:40
  13.2 0.7 collective-permute-start.4
  13.9 1.9 %collective-permute-start.3 = (f32[4,16,8,128]{3,2,1,0:T(8,128)S(1)}, f32[4,16,8,128]{3,2,1,0:T(8,128)S(1)}, u32[]{:S(2)}, u32[]{:S(2)}) collective-permute-start(f32[4,16,8,128]{3,2,1,0:T(8,128)S(1)} %get-tuple-element.26), channel_id=1, source_target_pairs={{0,12},{1,13},{2,14},{3,15},{4,0},{5,1},{6,2},{7,3},{8,4},{9,5},{1... | collective-permute-start | bytes 786440 | tf_op jit(solution)/shard_map/ppermute | solution.py:40
  15.9 0.7 fusion.7
  16.7 6.3 %collective-permute-start.6 = (f32[4,16,8,128]{3,2,1,0:T(8,128)S(1)}, f32[4,16,8,128]{3,2,1,0:T(8,128)S(1)}, u32[]{:S(2)}, u32[]{:S(2)}) collective-permute-start(f32[4,16,8,128]{3,2,1,0:T(8,128)S(1)} %get-tuple-element.26), channel_id=1, source_target_pairs={{16,32},{17,33},{18,34},{19,35},{20,36},{21,37},{22,38},{23,39},{2... | collective-permute-start | bytes 786440 | tf_op jit(solution)/shard_map/ppermute | solution.py:40
  23.2 3.4 %collective-permute-start.7 = (f32[3,4,16,8,128]{4,3,2,1,0:T(8,128)S(1)}, f32[3,4,16,8,128]{4,3,2,1,0:T(8,128)S(1)}, u32[]{:S(2)}, u32[]{:S(2)}) collective-permute-start(f32[3,4,16,8,128]{4,3,2,1,0:T(8,128)S(1)} %pad_maximum_fusion.2.ready_ref), channel_id=1, source_target_pairs={{16,32},{17,33},{18,34},{19,35},{20,36},{21,37},{22,38},{23,39},{2... | collective-permute-start | bytes 2359304 | tf_op jit(solution)/shard_map/ppermute | solution.py:40
  26.7 2.9 %prepare.1.matrices_ref = bf16[16,128,1024]{2,1,0:T(8,128)(2,1)S(1)} custom-call(f32[16,16,4096]{2,1,0:T(8,128)S(1)} %copy-done.2, f32[3,4,16,8,128]{4,3,2,1,0:T(8,128)S(1)} %pad_maximum_fusion.2.ready_ref), custom_call_target="tpu_custom_call" | custom-call | flops 16777216 | bytes 8388608 | tf_op jit(solution)/shard_map/prepare/pallas_call | solution.py:122
  29.7 3.4 %copy-done = f32[2,1024,1024]{2,1,0:T(8,128)S(1)} copy-done((f32[2,1024,1024]{2,1,0:T(8,128)S(1)}, f32[2,1024,1024]{2,1,0:T(8,128)}, u32[]{:S(2)}) %copy-start) | copy-done | bytes 8388632
  33.0 4.4 %halve.1 = (bf16[2,2,1024,1024]{3,2,1,0:T(8,128)(2,1)S(1)}, bf16[2,2,1024,512]{3,2,1,0:T(8,128)(2,1)S(1)}, f32[2,16,1024]{2,1,0:T(8,128)S(1)}) custom-call(f32[2,1024,1024]{2,1,0:T(8,128)S(1)} %copy-done, f32[2,1024,512]{2,1,0:T(8,128)S(1)} %copy-done.1, f32[2,16,1024]{2,1,0:T(8,128)S(1)} %copy-done.3, f32[3,4,16,8,128]{4,3,2,1,0:T(8,128)S(1)} %pad_maximum_fusion.2.ready_ref), custom_call_target="tpu_custom_call" | custom-call | flops 134217728 | bytes 25165824 | tf_op jit(solution)/shard_map/halve/pallas_call | solution.py:155
  37.7 0.4 copy-done.4
  38.1 2.1 %apply_first.1 = (f32[16,8,128]{2,1,0:T(8,128)S(1)}, f32[2,4,16,128]{3,2,1,0:T(8,128)S(1)}) custom-call(s32[256]{0:T(256)S(1)} %reshape.21.places_ref, s32[16]{0:T(128)S(1)} %reshape.22.slots_ref, s32[2]{0:T(128)S(1)} %copy-done.4, f32[768,8,128]{2,1,0:T(8,128)S(1)} %bitcast.36, bf16[16,128,1024]{2,1,0:T(8,128)(2,1)S(1)} %prepare.1.matrices_ref, ...), custom_call_target="tpu_custom_call" | custom-call | flops 134217728 | bytes 8388608 | tf_op jit(solution)/shard_map/apply_first/pallas_call | solution.py:260
  40.2 1.9 %collective-permute-start.11 = (f32[16,8,128]{2,1,0:T(8,128)S(1)}, f32[16,8,128]{2,1,0:T(8,128)S(1)}, u32[]{:S(2)}, u32[]{:S(2)}) collective-permute-start(f32[16,8,128]{2,1,0:T(8,128)S(1)} %get-tuple-element.14.image_ref), channel_id=1, source_target_pairs={{0,2},{1,3},{2,0},{3,1},{4,6},{5,7},{6,4},{7,5},{8,10},{9,11},{10,... | collective-permute-start | bytes 196616 | tf_op jit(solution)/shard_map/ppermute | solution.py:40
  42.1 1.6 %collective-permute-start.10 = (f32[16,8,128]{2,1,0:T(8,128)S(1)}, f32[16,8,128]{2,1,0:T(8,128)S(1)}, u32[]{:S(2)}, u32[]{:S(2)}) collective-permute-start(f32[16,8,128]{2,1,0:T(8,128)S(1)} %get-tuple-element.14.image_ref), channel_id=1, source_target_pairs={{0,1},{1,2},{2,3},{3,0},{4,5},{5,6},{6,7},{7,4},{8,9},{9,10},{10,1... | collective-permute-start | bytes 196616 | tf_op jit(solution)/shard_map/ppermute | solution.py:40
  43.6 1.1 %collective-permute-start.9 = (f32[16,8,128]{2,1,0:T(8,128)S(1)}, f32[16,8,128]{2,1,0:T(8,128)S(1)}, u32[]{:S(2)}, u32[]{:S(2)}) collective-permute-start(f32[16,8,128]{2,1,0:T(8,128)S(1)} %get-tuple-element.14.image_ref), channel_id=1, source_target_pairs={{0,3},{1,0},{2,1},{3,2},{4,7},{5,4},{6,5},{7,6},{8,11},{9,8},{10,9... | collective-permute-start | bytes 196616 | tf_op jit(solution)/shard_map/ppermute | solution.py:40
  44.9 1.8 %collective-permute-done.10 = f32[16,8,128]{2,1,0:T(8,128)S(1)} collective-permute-done((f32[16,8,128]{2,1,0:T(8,128)S(1)}, f32[16,8,128]{2,1,0:T(8,128)S(1)}, u32[]{:S(2)}, u32[]{:S(2)}) %collective-permute-start.10) | collective-permute-done | bytes 65568 | tf_op jit(solution)/shard_map/ppermute | solution.py:40
  46.7 0.4 collective-permute-done.9
  47.1 1.3 %collective-permute-start.14 = (f32[4,16,8,128]{3,2,1,0:T(8,128)S(1)}, f32[4,16,8,128]{3,2,1,0:T(8,128)S(1)}, u32[]{:S(2)}, u32[]{:S(2)}) collective-permute-start(f32[4,16,8,128]{3,2,1,0:T(8,128)S(1)} %get-tuple-element.24), channel_id=1, source_target_pairs={{0,8},{1,9},{2,10},{3,11},{4,12},{5,13},{6,14},{7,15},{8,0},{9,1},... | collective-permute-start | bytes 786440 | tf_op jit(solution)/shard_map/ppermute | solution.py:40
  48.4 2.3 %collective-permute-start.13 = (f32[4,16,8,128]{3,2,1,0:T(8,128)S(1)}, f32[4,16,8,128]{3,2,1,0:T(8,128)S(1)}, u32[]{:S(2)}, u32[]{:S(2)}) collective-permute-start(f32[4,16,8,128]{3,2,1,0:T(8,128)S(1)} %get-tuple-element.24), channel_id=1, source_target_pairs={{0,4},{1,5},{2,6},{3,7},{4,8},{5,9},{6,10},{7,11},{8,12},{9,13},{1... | collective-permute-start | bytes 786440 | tf_op jit(solution)/shard_map/ppermute | solution.py:40
  50.7 0.3 collective-permute-start.12
  51.0 6.6 %collective-permute-start.15 = (f32[4,16,8,128]{3,2,1,0:T(8,128)S(1)}, f32[4,16,8,128]{3,2,1,0:T(8,128)S(1)}, u32[]{:S(2)}, u32[]{:S(2)}) collective-permute-start(f32[4,16,8,128]{3,2,1,0:T(8,128)S(1)} %get-tuple-element.24), channel_id=1, source_target_pairs={{16,32},{17,33},{18,34},{19,35},{20,36},{21,37},{22,38},{23,39},{2... | collective-permute-start | bytes 786440 | tf_op jit(solution)/shard_map/ppermute | solution.py:40
  57.9 5.7 %collective-permute-start.16 = (f32[3,4,16,8,128]{4,3,2,1,0:T(8,128)S(1)}, f32[3,4,16,8,128]{4,3,2,1,0:T(8,128)S(1)}, u32[]{:S(2)}, u32[]{:S(2)}) collective-permute-start(f32[3,4,16,8,128]{4,3,2,1,0:T(8,128)S(1)} %pad_maximum_fusion.3.ready_ref), channel_id=1, source_target_pairs={{16,32},{17,33},{18,34},{19,35},{20,36},{21,37},{22,38},{23,39},{2... | collective-permute-start | bytes 2359304 | tf_op jit(solution)/shard_map/ppermute | solution.py:40
  64.0 9.2 %fold.1 = (bf16[2,2,1024,512]{3,2,1,0:T(8,128)(2,1)S(1)}, f32[2,16,1024]{2,1,0:T(8,128)S(1)}) custom-call(bf16[2,2,1024,1024]{3,2,1,0:T(8,128)(2,1)S(1)} %get-tuple-element.13.halves_ref.inverse_ref, bf16[2,2,1024,512]{3,2,1,0:T(8,128)(2,1)S(1)} %get-tuple-element.15.coupling_ref, f32[2,4,16,128]{3,2,1,0:T(8,128)S(1)} %get-tuple-element.16.picked_ref, ...), custom_call_target="tpu_custom_call" | custom-call | flops 8589934592 | bytes 16777216 | tf_op jit(solution)/shard_map/fold/pallas_call | solution.py:318
  73.4 3.1 %apply_second.1 = (f32[16,8,128]{2,1,0:T(8,128)S(1)}, f32[64,8,128]{2,1,0:T(8,128)S(1)}, f32[2,16,1024]{2,1,0:T(8,128)S(1)}) custom-call(s32[256]{0:T(256)S(1)} %reshape.21.places_ref, s32[16]{0:T(128)S(1)} %reshape.22.slots_ref, s32[2]{0:T(128)S(1)} %copy-done.4, f32[768,8,128]{2,1,0:T(8,128)S(1)} %bitcast.37, ...), custom_call_target="tpu_custom_call" | custom-call | flops 134217728 | bytes 8388608 | tf_op jit(solution)/shard_map/apply_second/pallas_call | solution.py:273
  76.6 16.3 %all_to_all.5 = f32[64,8,128]{2,1,0:T(8,128)S(1)} all-to-all(f32[64,8,128]{2,1,0:T(8,128)S(1)} %get-tuple-element.18), channel_id=1, replica_groups=mesh['y'=4,'core'=2,'x'=4,'z'=4] {'y','x','z'}, dimensions={0} | all-to-all | bytes 524288 | tf_op jit(solution)/shard_map/all_to_all | solution.py:429
  92.9 3.3 %collective-permute-start.18 = (f32[8,128]{1,0:T(8,128)S(1)}, f32[8,128]{1,0:T(8,128)S(1)}, u32[]{:S(2)}, u32[]{:S(2)}) collective-permute-start(f32[8,128]{1,0:T(8,128)S(1)} %reduce_sum.9.sums_ref), channel_id=1, source_target_pairs={{0,16},{1,17},{2,18},{3,19},{4,20},{5,21},{6,22},{7,23},{8,24},{9,... | collective-permute-start | bytes 12296 | tf_op jit(solution)/shard_map/ppermute | solution.py:40
  96.2 0.8 collective-permute-done.18.others_ref
  97.0 0.9 finish.1
  (49 shorter events, 2.1 us)
Async XLA Ops:
  1.5 7.1 %collective-permute-start.2 = (f32[16,8,128]{2,1,0:T(8,128)S(1)}, f32[16,8,128]{2,1,0:T(8,128)S(1)}, u32[]{:S(2)}, u32[]{:S(2)}) collective-permute-start(f32[16,8,128]{2,1,0:T(8,128)S(1)} %bitcast.38), channel_id=1, source_target_pairs={{0,2},{1,3},{2,0},{3,1},{4,6},{5,7},{6,4},{7,5},{8,10},{9,11},{10,... | collective-permute-start | bytes 196616 | tf_op jit(solution)/shard_map/ppermute | solution.py:40
  5.1 4.3 %collective-permute-start.1 = (f32[16,8,128]{2,1,0:T(8,128)S(1)}, f32[16,8,128]{2,1,0:T(8,128)S(1)}, u32[]{:S(2)}, u32[]{:S(2)}) collective-permute-start(f32[16,8,128]{2,1,0:T(8,128)S(1)} %bitcast.39), channel_id=1, source_target_pairs={{0,1},{1,2},{2,3},{3,0},{4,5},{5,6},{6,7},{7,4},{8,9},{9,10},{10,1... | collective-permute-start | bytes 196616 | tf_op jit(solution)/shard_map/ppermute | solution.py:40
  5.5 4.0 %collective-permute-start = (f32[16,8,128]{2,1,0:T(8,128)S(1)}, f32[16,8,128]{2,1,0:T(8,128)S(1)}, u32[]{:S(2)}, u32[]{:S(2)}) collective-permute-start(f32[16,8,128]{2,1,0:T(8,128)S(1)} %bitcast.40), channel_id=1, source_target_pairs={{0,3},{1,0},{2,1},{3,2},{4,7},{5,4},{6,5},{7,6},{8,11},{9,8},{10,9... | collective-permute-start | bytes 196616 | tf_op jit(solution)/shard_map/ppermute | solution.py:40
  9.5 13.5 %collective-permute-start.5 = (f32[4,16,8,128]{3,2,1,0:T(8,128)S(1)}, f32[4,16,8,128]{3,2,1,0:T(8,128)S(1)}, u32[]{:S(2)}, u32[]{:S(2)}) collective-permute-start(f32[4,16,8,128]{3,2,1,0:T(8,128)S(1)} %get-tuple-element.26), channel_id=1, source_target_pairs={{0,8},{1,9},{2,10},{3,11},{4,12},{5,13},{6,14},{7,15},{8,0},{9,1},... | collective-permute-start | bytes 786440 | tf_op jit(solution)/shard_map/ppermute | solution.py:40
  13.2 9.8 %collective-permute-start.4 = (f32[4,16,8,128]{3,2,1,0:T(8,128)S(1)}, f32[4,16,8,128]{3,2,1,0:T(8,128)S(1)}, u32[]{:S(2)}, u32[]{:S(2)}) collective-permute-start(f32[4,16,8,128]{3,2,1,0:T(8,128)S(1)} %get-tuple-element.26), channel_id=1, source_target_pairs={{0,4},{1,5},{2,6},{3,7},{4,8},{5,9},{6,10},{7,11},{8,12},{9,13},{1... | collective-permute-start | bytes 786440 | tf_op jit(solution)/shard_map/ppermute | solution.py:40
  13.9 9.1 %collective-permute-start.3 = (f32[4,16,8,128]{3,2,1,0:T(8,128)S(1)}, f32[4,16,8,128]{3,2,1,0:T(8,128)S(1)}, u32[]{:S(2)}, u32[]{:S(2)}) collective-permute-start(f32[4,16,8,128]{3,2,1,0:T(8,128)S(1)} %get-tuple-element.26), channel_id=1, source_target_pairs={{0,12},{1,13},{2,14},{3,15},{4,0},{5,1},{6,2},{7,3},{8,4},{9,5},{1... | collective-permute-start | bytes 786440 | tf_op jit(solution)/shard_map/ppermute | solution.py:40
  16.7 10.0 %copy-start.2 = (f32[16,16,4096]{2,1,0:T(8,128)S(1)}, f32[16,16,4096]{2,1,0:T(8,128)}, u32[]{:S(2)}) copy-start(f32[16,16,4096]{2,1,0:T(8,128)} %values_ref.1) | copy-start | bytes 12582916
  16.7 20.8 %collective-permute-start.6 = (f32[4,16,8,128]{3,2,1,0:T(8,128)S(1)}, f32[4,16,8,128]{3,2,1,0:T(8,128)S(1)}, u32[]{:S(2)}, u32[]{:S(2)}) collective-permute-start(f32[4,16,8,128]{3,2,1,0:T(8,128)S(1)} %get-tuple-element.26), channel_id=1, source_target_pairs={{16,32},{17,33},{18,34},{19,35},{20,36},{21,37},{22,38},{23,39},{2... | collective-permute-start | bytes 786440 | tf_op jit(solution)/shard_map/ppermute | solution.py:40
  23.2 14.3 %collective-permute-start.7 = (f32[3,4,16,8,128]{4,3,2,1,0:T(8,128)S(1)}, f32[3,4,16,8,128]{4,3,2,1,0:T(8,128)S(1)}, u32[]{:S(2)}, u32[]{:S(2)}) collective-permute-start(f32[3,4,16,8,128]{4,3,2,1,0:T(8,128)S(1)} %pad_maximum_fusion.2.ready_ref), channel_id=1, source_target_pairs={{16,32},{17,33},{18,34},{19,35},{20,36},{21,37},{22,38},{23,39},{2... | collective-permute-start | bytes 2359304 | tf_op jit(solution)/shard_map/ppermute | solution.py:40
  26.6 11.0 %collective-permute-start.8 = (f32[4,4,16,8,128]{4,3,2,1,0:T(8,128)S(1)}, f32[4,4,16,8,128]{4,3,2,1,0:T(8,128)S(1)}, u32[]{:S(2)}, u32[]{:S(2)}) collective-permute-start(f32[4,4,16,8,128]{4,3,2,1,0:T(8,128)S(1)} %pad_maximum_fusion), channel_id=1, source_target_pairs={{0,16},{1,17},{2,18},{3,19},{4,20},{5,21},{6,22},{7,23},{8,24},{9,... | collective-permute-start | bytes 3145736 | tf_op jit(solution)/shard_map/ppermute | solution.py:40
  26.7 2.9 %copy-start.1 = (f32[2,1024,512]{2,1,0:T(8,128)S(1)}, f32[2,1024,512]{2,1,0:T(8,128)}, u32[]{:S(2)}) copy-start(f32[2,1024,512]{2,1,0:T(8,128)} %coupling_ref.1) | copy-start | bytes 12582916
  26.7 2.9 %copy-start.3 = (f32[2,16,1024]{2,1,0:T(8,128)S(1)}, f32[2,16,1024]{2,1,0:T(8,128)}, u32[]{:S(2)}) copy-start(f32[2,16,1024]{2,1,0:T(8,128)} %load_ref.1) | copy-start | bytes 393220
  29.6 3.4 %copy-start = (f32[2,1024,1024]{2,1,0:T(8,128)S(1)}, f32[2,1024,1024]{2,1,0:T(8,128)}, u32[]{:S(2)}) copy-start(f32[2,1024,1024]{2,1,0:T(8,128)} %inverse_ref.1) | copy-start | bytes 25165828
  37.4 0.7 copy-start.4
  40.2 4.7 %collective-permute-start.11 = (f32[16,8,128]{2,1,0:T(8,128)S(1)}, f32[16,8,128]{2,1,0:T(8,128)S(1)}, u32[]{:S(2)}, u32[]{:S(2)}) collective-permute-start(f32[16,8,128]{2,1,0:T(8,128)S(1)} %get-tuple-element.14.image_ref), channel_id=1, source_target_pairs={{0,2},{1,3},{2,0},{3,1},{4,6},{5,7},{6,4},{7,5},{8,10},{9,11},{10,... | collective-permute-start | bytes 196616 | tf_op jit(solution)/shard_map/ppermute | solution.py:40
  42.1 4.6 %collective-permute-start.10 = (f32[16,8,128]{2,1,0:T(8,128)S(1)}, f32[16,8,128]{2,1,0:T(8,128)S(1)}, u32[]{:S(2)}, u32[]{:S(2)}) collective-permute-start(f32[16,8,128]{2,1,0:T(8,128)S(1)} %get-tuple-element.14.image_ref), channel_id=1, source_target_pairs={{0,1},{1,2},{2,3},{3,0},{4,5},{5,6},{6,7},{7,4},{8,9},{9,10},{10,1... | collective-permute-start | bytes 196616 | tf_op jit(solution)/shard_map/ppermute | solution.py:40
  43.6 3.4 %collective-permute-start.9 = (f32[16,8,128]{2,1,0:T(8,128)S(1)}, f32[16,8,128]{2,1,0:T(8,128)S(1)}, u32[]{:S(2)}, u32[]{:S(2)}) collective-permute-start(f32[16,8,128]{2,1,0:T(8,128)S(1)} %get-tuple-element.14.image_ref), channel_id=1, source_target_pairs={{0,3},{1,0},{2,1},{3,2},{4,7},{5,4},{6,5},{7,6},{8,11},{9,8},{10,9... | collective-permute-start | bytes 196616 | tf_op jit(solution)/shard_map/ppermute | solution.py:40
  47.1 10.6 %collective-permute-start.14 = (f32[4,16,8,128]{3,2,1,0:T(8,128)S(1)}, f32[4,16,8,128]{3,2,1,0:T(8,128)S(1)}, u32[]{:S(2)}, u32[]{:S(2)}) collective-permute-start(f32[4,16,8,128]{3,2,1,0:T(8,128)S(1)} %get-tuple-element.24), channel_id=1, source_target_pairs={{0,8},{1,9},{2,10},{3,11},{4,12},{5,13},{6,14},{7,15},{8,0},{9,1},... | collective-permute-start | bytes 786440 | tf_op jit(solution)/shard_map/ppermute | solution.py:40
  48.4 9.3 %collective-permute-start.13 = (f32[4,16,8,128]{3,2,1,0:T(8,128)S(1)}, f32[4,16,8,128]{3,2,1,0:T(8,128)S(1)}, u32[]{:S(2)}, u32[]{:S(2)}) collective-permute-start(f32[4,16,8,128]{3,2,1,0:T(8,128)S(1)} %get-tuple-element.24), channel_id=1, source_target_pairs={{0,4},{1,5},{2,6},{3,7},{4,8},{5,9},{6,10},{7,11},{8,12},{9,13},{1... | collective-permute-start | bytes 786440 | tf_op jit(solution)/shard_map/ppermute | solution.py:40
  50.7 7.0 %collective-permute-start.12 = (f32[4,16,8,128]{3,2,1,0:T(8,128)S(1)}, f32[4,16,8,128]{3,2,1,0:T(8,128)S(1)}, u32[]{:S(2)}, u32[]{:S(2)}) collective-permute-start(f32[4,16,8,128]{3,2,1,0:T(8,128)S(1)} %get-tuple-element.24), channel_id=1, source_target_pairs={{0,12},{1,13},{2,14},{3,15},{4,0},{5,1},{6,2},{7,3},{8,4},{9,5},{1... | collective-permute-start | bytes 786440 | tf_op jit(solution)/shard_map/ppermute | solution.py:40
  51.0 12.9 %collective-permute-start.15 = (f32[4,16,8,128]{3,2,1,0:T(8,128)S(1)}, f32[4,16,8,128]{3,2,1,0:T(8,128)S(1)}, u32[]{:S(2)}, u32[]{:S(2)}) collective-permute-start(f32[4,16,8,128]{3,2,1,0:T(8,128)S(1)} %get-tuple-element.24), channel_id=1, source_target_pairs={{16,32},{17,33},{18,34},{19,35},{20,36},{21,37},{22,38},{23,39},{2... | collective-permute-start | bytes 786440 | tf_op jit(solution)/shard_map/ppermute | solution.py:40
  57.9 15.4 %collective-permute-start.16 = (f32[3,4,16,8,128]{4,3,2,1,0:T(8,128)S(1)}, f32[3,4,16,8,128]{4,3,2,1,0:T(8,128)S(1)}, u32[]{:S(2)}, u32[]{:S(2)}) collective-permute-start(f32[3,4,16,8,128]{4,3,2,1,0:T(8,128)S(1)} %pad_maximum_fusion.3.ready_ref), channel_id=1, source_target_pairs={{16,32},{17,33},{18,34},{19,35},{20,36},{21,37},{22,38},{23,39},{2... | collective-permute-start | bytes 2359304 | tf_op jit(solution)/shard_map/ppermute | solution.py:40
  63.6 9.7 %collective-permute-start.17 = (f32[4,4,16,8,128]{4,3,2,1,0:T(8,128)S(1)}, f32[4,4,16,8,128]{4,3,2,1,0:T(8,128)S(1)}, u32[]{:S(2)}, u32[]{:S(2)}) collective-permute-start(f32[4,4,16,8,128]{4,3,2,1,0:T(8,128)S(1)} %pad_maximum_fusion.1), channel_id=1, source_target_pairs={{0,16},{1,17},{2,18},{3,19},{4,20},{5,21},{6,22},{7,23},{8,24},{9,... | collective-permute-start | bytes 3145736 | tf_op jit(solution)/shard_map/ppermute | solution.py:40
  92.9 4.1 %collective-permute-start.18 = (f32[8,128]{1,0:T(8,128)S(1)}, f32[8,128]{1,0:T(8,128)S(1)}, u32[]{:S(2)}, u32[]{:S(2)}) collective-permute-start(f32[8,128]{1,0:T(8,128)S(1)} %reduce_sum.9.sums_ref), channel_id=1, source_target_pairs={{0,16},{1,17},{2,18},{3,19},{4,20},{5,21},{6,22},{7,23},{8,24},{9,... | collective-permute-start | bytes 12296 | tf_op jit(solution)/shard_map/ppermute | solution.py:40

commit v3 on v2

--- a/solution.py
+++ b/solution.py
@@ -131,26 +131,15 @@
     )(values, ready)
 
 
-def halve_kernel(
-    inverse_ref, coupling_ref, load_ref, ready_ref, inverse_out_ref, coupling_out_ref, base_ref, l_ref
-):
+def halve_kernel(inverse_ref, coupling_ref, ready_ref, inverse_out_ref, coupling_out_ref):
     sub = pl.program_id(0)
     size = inverse_ref.shape[1]
     rows = pl.ds(pl.multiple_of(pl.program_id(1) * size, size), size)
-
-    @pl.when(pl.program_id(1) == 0)
-    def _():
-        l_ref[0:16], l_ref[16:32] = split(load_ref[0])
-
-    coupling_out_ref[sub, 0, rows, :], coupling_out_ref[sub, 1, rows, :] = split(coupling_ref[0])
-    high, low = split(inverse_ref[0])
-    inverse_out_ref[sub, 0, rows, :], inverse_out_ref[sub, 1, rows, :] = high, low
-    main = lax.dot_general(l_ref[...], high, NT, preferred_element_type=jnp.float32)
-    rest = lax.dot_general(l_ref[0:16], low, NT, preferred_element_type=jnp.float32)
-    base_ref[sub, :, rows] = main[0:16] + main[16:32] + rest
-
-
-def halve(inverse, coupling, load, ready):
+    for ref, out_ref in ((inverse_ref, inverse_out_ref), (coupling_ref, coupling_out_ref)):
+        out_ref[sub, 0, rows, :], out_ref[sub, 1, rows, :] = split(ref[0])
+
+
+def halve(inverse, coupling, ready):
     cut = 256
     return pl.pallas_call(
         halve_kernel,
@@ -158,20 +147,17 @@
         in_specs=[
             pl.BlockSpec((1, cut, 1024), lambda s, n: (s, n, 0)),
             pl.BlockSpec((1, cut, 512), lambda s, n: (s, n, 0)),
-            pl.BlockSpec((1, CASES, 1024), lambda s, n: (s, 0, 0)),
             ANY_SPEC,
         ],
-        out_specs=[VMEM_SPEC] * 3,
+        out_specs=[VMEM_SPEC] * 2,
         out_shape=[
             jax.ShapeDtypeStruct((2, 2, 1024, 1024), jnp.bfloat16),
             jax.ShapeDtypeStruct((2, 2, 1024, 512), jnp.bfloat16),
-            jax.ShapeDtypeStruct((2, CASES, 1024), jnp.float32),
-        ],
-        scratch_shapes=[pltpu.VMEM((32, 1024), jnp.bfloat16)],
+        ],
         compiler_params=pltpu.CompilerParams(vmem_limit_bytes=20 * 2**20),
-        cost_estimate=pl.CostEstimate(flops=2**27, bytes_accessed=3 * 2**23, transcendentals=0),
+        cost_estimate=pl.CostEstimate(flops=2**24, bytes_accessed=3 * 2**23, transcendentals=0),
         name="halve",
-    )(inverse, coupling, load, ready)
+    )(inverse, coupling, ready)
 
 
 def apply_rows(places_ref, window_ref, matrices_ref, x_ref, out_ref):
@@ -219,6 +205,7 @@
     load_ref,
     image_ref,
     folded_ref,
+    first_ref,
     twice_ref,
     sums_ref,
     parts_ref,
@@ -241,14 +228,17 @@
     sums_ref[...] = jnp.broadcast_to(packed[None], sums_ref.shape)
     pick_slots(slots_ref, live_ref, window_ref, picked_ref)
     for sub in range(2):
-        for t in range(4):
-            cut = slice(t * LANES, (t + 1) * LANES)
-            p_ref[sub, 0:16, cut], p_ref[sub, 16:32, cut] = split(picked_ref[sub, t])
+        for which, ref in enumerate((first_ref, picked_ref)):
+            for t in range(4):
+                cut = slice(t * LANES, (t + 1) * LANES)
+                high, low = split(ref[sub, t])
+                p_ref[sub, 16 * which : 16 * which + 16, cut] = high
+                p_ref[sub, 32 + 16 * which : 48 + 16 * which, cut] = low
         main = lax.dot_general(p_ref[sub], folded_ref[sub, 0], NT, preferred_element_type=jnp.float32)
         rest = lax.dot_general(
-            p_ref[sub, 0:16], folded_ref[sub, 1], NT, preferred_element_type=jnp.float32
+            p_ref[sub, 0:32], folded_ref[sub, 1], NT, preferred_element_type=jnp.float32
         )
-        parts_ref[sub] = main[0:16] + main[16:32] + rest
+        parts_ref[sub] = main[0:32] + main[32:64] + rest
 
 
 APPLY_COST = pl.CostEstimate(flops=2**27, bytes_accessed=2**23, transcendentals=0)
@@ -269,52 +259,48 @@
     )(places, slots, live, window, matrices, halves)
 
 
-def apply_second(places, slots, live, window, matrices, load, image, folded):
+def apply_second(places, slots, live, window, matrices, load, image, folded, first):
     return pl.pallas_call(
         second_kernel,
-        in_specs=[SMEM_SPEC] * 3 + [VMEM_SPEC] * 5,
+        in_specs=[SMEM_SPEC] * 3 + [VMEM_SPEC] * 6,
         out_specs=[VMEM_SPEC] * 3,
         out_shape=[
             TILES,
             jax.ShapeDtypeStruct((CHIPS, 8, LANES), jnp.float32),
-            jax.ShapeDtypeStruct((2, CASES, 1024), jnp.float32),
+            jax.ShapeDtypeStruct((2, 32, 1024), jnp.float32),
         ],
         scratch_shapes=[
             pltpu.VMEM((2, 32, 1024), jnp.bfloat16),
             pltpu.VMEM((2, 4, 16, LANES), jnp.float32),
-            pltpu.VMEM((2, 32, 512), jnp.bfloat16),
+            pltpu.VMEM((2, 64, 512), jnp.bfloat16),
         ],
         compiler_params=pltpu.CompilerParams(vmem_limit_bytes=8 * 2**20),
         cost_estimate=APPLY_COST,
         name="apply_second",
-    )(places, slots, live, window, matrices, load, image, folded)
-
-
-def fold_kernel(inverse_ref, coupling_ref, picked_ref, ready_ref, folded_ref, parts_ref, p_ref):
+    )(places, slots, live, window, matrices, load, image, folded, first)
+
+
+def fold_kernel(inverse_ref, coupling_ref, load_ref, ready_ref, folded_ref, base_ref, l_ref):
     cut = 256
     for sub in range(2):
-        for t in range(4):
-            lanes = slice(t * LANES, (t + 1) * LANES)
-            p_ref[sub, 0:16, lanes], p_ref[sub, 16:32, lanes] = split(picked_ref[sub, t])
+        l_ref[sub, 0:16], l_ref[sub, 16:32] = split(load_ref[sub])
 
     @pl.loop(0, 2)
     def _(sub):
         for n in range(1024 // cut):
             rows = slice(n * cut, (n + 1) * cut)
             high, low = inverse_ref[sub, 0, rows], inverse_ref[sub, 1, rows]
-            term = (
+            folded_ref[sub, 0, rows], folded_ref[sub, 1, rows] = split(
                 jnp.dot(high, coupling_ref[sub, 0], preferred_element_type=jnp.float32)
                 + jnp.dot(high, coupling_ref[sub, 1], preferred_element_type=jnp.float32)
                 + jnp.dot(low, coupling_ref[sub, 0], preferred_element_type=jnp.float32)
             )
-            high, low = split(term)
-            folded_ref[sub, 0, rows], folded_ref[sub, 1, rows] = high, low
-            main = lax.dot_general(p_ref[sub], high, NT, preferred_element_type=jnp.float32)
-            rest = lax.dot_general(p_ref[sub, 0:16], low, NT, preferred_element_type=jnp.float32)
-            parts_ref[sub, :, rows] = main[0:16] + main[16:32] + rest
-
-
-def fold(inverse, coupling, picked, ready):
+            main = lax.dot_general(l_ref[sub], high, NT, preferred_element_type=jnp.float32)
+            rest = lax.dot_general(l_ref[sub, 0:16], low, NT, preferred_element_type=jnp.float32)
+            base_ref[sub, :, rows] = main[0:16] + main[16:32] + rest
+
+
+def fold(inverse, coupling, load, ready):
     return pl.pallas_call(
         fold_kernel,
         in_specs=[VMEM_SPEC] * 3 + [ANY_SPEC],
@@ -323,15 +309,15 @@
             jax.ShapeDtypeStruct((2, 2, 1024, 512), jnp.bfloat16),
             jax.ShapeDtypeStruct((2, CASES, 1024), jnp.float32),
         ],
-        scratch_shapes=[pltpu.VMEM((2, 32, 512), jnp.bfloat16)],
+        scratch_shapes=[pltpu.VMEM((2, 32, 1024), jnp.bfloat16)],
         compiler_params=pltpu.CompilerParams(vmem_limit_bytes=10 * 2**20),
         cost_estimate=pl.CostEstimate(flops=2**33, bytes_accessed=2**24, transcendentals=0),
         name="fold",
-    )(inverse, coupling, picked, ready)
+    )(inverse, coupling, load, ready)
 
 
 def finish_kernel(
-    sums_ref, others_ref, load_ref, image_ref, twice_ref, base_ref, parts_ref, more_ref, solution_ref, residual_ref, interior_ref, tiles_ref, cases_ref
+    sums_ref, others_ref, load_ref, image_ref, twice_ref, base_ref, parts_ref, solution_ref, residual_ref, interior_ref, tiles_ref, cases_ref
 ):
     lanes = lane_ids(8)
     low_half = lanes < NB
@@ -377,14 +363,14 @@
     own, other = cases_ref[0][:, 0:1], cases_ref[1][:, 0:1]
     for sub in range(2):
         interior_ref[sub] = (
-            base_ref[sub] - own * parts_ref[sub] - other * more_ref[sub]
+            base_ref[sub] - own * parts_ref[sub, 0:16] - other * parts_ref[sub, 16:32]
         )
 
 
-def finish(sums, others, load, image, twice, base, parts, more):
+def finish(sums, others, load, image, twice, base, parts):
     return pl.pallas_call(
         finish_kernel,
-        in_specs=[VMEM_SPEC] * 8,
+        in_specs=[VMEM_SPEC] * 7,
         out_specs=[VMEM_SPEC] * 3,
         out_shape=[
             jax.ShapeDtypeStruct((16, 1024), jnp.float32),
@@ -394,7 +380,7 @@
         scratch_shapes=[pltpu.VMEM((128, LANES), jnp.float32), pltpu.VMEM((2, 16, LANES), jnp.float32)],
         compiler_params=pltpu.CompilerParams(vmem_limit_bytes=8 * 2**20),
         name="finish",
-    )(sums, others, load, image, twice, base, parts, more)
+    )(sums, others, load, image, twice, base, parts)
 
 
 def body(
@@ -412,22 +398,18 @@
     places = locate(schur_columns, region, x, z).reshape(-1)
     slots = locate(adjacency, region, x, z).reshape(-1)
     load = interface_load.reshape(16, 8, LANES)
-    load_window, (matrices, (inverse, couplings, base)) = exchange(
-        load,
-        lambda ready: (
-            prepare(schur_values, ready),
-            halve(layer_inverse, coupling, interior_load, ready),
-        ),
+    load_window, (matrices, (inverse, couplings)) = exchange(
+        load, lambda ready: (prepare(schur_values, ready), halve(layer_inverse, coupling, ready))
     )
     image, picked = apply_first(places, slots, live_counts, load_window, matrices, inverse)
-    image_window, (folded, parts) = exchange(
-        image, lambda ready: fold(inverse, couplings, picked, ready)
+    image_window, (folded, base) = exchange(
+        image, lambda ready: fold(inverse, couplings, interior_load, ready)
     )
-    twice, sums, more = apply_second(
-        places, slots, live_counts, image_window, matrices, load, image, folded
+    twice, sums, parts = apply_second(
+        places, slots, live_counts, image_window, matrices, load, image, folded, picked
     )
     sums = jnp.sum(lax.all_to_all(sums, ("y", "x", "z"), 0, 0), axis=0)
-    return tuple(finish(sums, permute(sums, partner), load, image, twice, base, parts, more))
+    return tuple(finish(sums, permute(sums, partner), load, image, twice, base, parts))
 
 
 def solution(mesh):

time: 98.3 us -> 97.1 us (0.988)
  Pallas kernels: 22.6 us -> 20 us
  blocking collectives: 16.3 us -> 17.8 us
  waiting for transfers between devices: 4.09 us -> 5.46 us
  starting transfers between devices: 46.8 us -> 45.7 us
    pallas_call x1, Pallas kernels: 4.4 us -> 1.98 us  [halve(): pl.pallas_call(halve_kernel, grid=(2, 1024 // cut), in_specs=[pl.BlockSpe...]
    all_to_all x1, blocking collectives: 16.3 us -> 17.8 us  [body(): sums = jnp.sum(lax.all_to_all(sums, ('y', 'x', 'z'), 0, 0), axis=0)]
    ppermute x19, waiting for transfers between devices: 4.09 us -> 5.46 us  [permute(): return lax.ppermute(value, AXES, pairs)]
    ppermute x19, starting transfers between devices: 46.8 us -> 45.7 us  [permute(): return lax.ppermute(value, AXES, pairs)]
  transfers between devices with their start and end apart: 19 -> 19, of which waited for: 6 -> 7; matrix products, arithmetic and copies ran while one was open for 2% -> 2% of each run, Pallas kernels for 17% -> 14%
where the time goes in v3:
time: 97.1 us; the launch traced here: 96.8 us
  starting transfers between devices  45.7 us (47%)
  Pallas kernels  20 us (21%)
  blocking collectives  17.8 us (18%)
  waiting for transfers between devices  5.46 us (6%)
  local copies, waits for them, and re-layouts  4.88 us (5%)
  other arithmetic  1.89 us (2%)
  between operations  1.02 us (1%)
    ppermute x19, starting transfers between devices, permute(): return lax.ppermute(value, AXES, pairs)  45.7 us
    all_to_all x1, blocking collectives, body(): sums = jnp.sum(lax.all_to_all(sums, ('y', 'x', 'z'), 0, 0), axis=0)  17.8 us
    pallas_call x1, Pallas kernels, fold(): pl.pallas_call(fold_kernel, in_specs=[VMEM_SPEC] * 3 + [ANY_SPEC], out_sp...  8.92 us
    ppermute x19, waiting for transfers between devices, permute(): return lax.ppermute(value, AXES, pairs)  5.46 us
    unnamed x21, local copies, waits for them, and re-layouts  4.53 us
    pallas_call x1, Pallas kernels, apply_second(): pl.pallas_call(second_kernel, in_specs=[SMEM_SPEC] * 3 + [VMEM_SPEC] * 6,...  3.23 us
    pallas_call x1, Pallas kernels, prepare(): pl.pallas_call(prepare_kernel, grid=(16,), in_specs=[pl.BlockSpec((1, 16,...  2.88 us
    pallas_call x1, Pallas kernels, apply_first(): pl.pallas_call(first_kernel, in_specs=[SMEM_SPEC] * 3 + [VMEM_SPEC] * 3,...  2.08 us
  transfers between devices with their start and end apart: 19, of which 7 were waited for; matrix products, arithmetic and copies ran while one was open for 2% of the time, Pallas kernels for 14%

profile of v3, /device:TPU:1, one launch (start us, length us, event | category | flops | bytes accessed | tf_op | source)
XLA Modules:
  0.0 96.8 jit_solution(12722814779423556601)
XLA Ops:
  0.6 0.9 copy.11
  1.5 3.7 %collective-permute-start.2 = (f32[16,8,128]{2,1,0:T(8,128)S(1)}, f32[16,8,128]{2,1,0:T(8,128)S(1)}, u32[]{:S(2)}, u32[]{:S(2)}) collective-permute-start(f32[16,8,128]{2,1,0:T(8,128)S(1)} %bitcast.38), channel_id=1, source_target_pairs={{0,2},{1,3},{2,0},{3,1},{4,6},{5,7},{6,4},{7,5},{8,10},{9,11},{10,... | collective-permute-start | bytes 196616 | tf_op jit(solution)/shard_map/ppermute | solution.py:40
  5.5 2.4 %collective-permute-start = (f32[16,8,128]{2,1,0:T(8,128)S(1)}, f32[16,8,128]{2,1,0:T(8,128)S(1)}, u32[]{:S(2)}, u32[]{:S(2)}) collective-permute-start(f32[16,8,128]{2,1,0:T(8,128)S(1)} %bitcast.40), channel_id=1, source_target_pairs={{0,3},{1,0},{2,1},{3,2},{4,7},{5,4},{6,5},{7,6},{8,11},{9,8},{10,9... | collective-permute-start | bytes 196616 | tf_op jit(solution)/shard_map/ppermute | solution.py:40
  7.8 0.7 fusion.13
  8.6 0.8 collective-permute-done.1
  9.5 3.7 %collective-permute-start.5 = (f32[4,16,8,128]{3,2,1,0:T(8,128)S(1)}, f32[4,16,8,128]{3,2,1,0:T(8,128)S(1)}, u32[]{:S(2)}, u32[]{:S(2)}) collective-permute-start(f32[4,16,8,128]{3,2,1,0:T(8,128)S(1)} %get-tuple-element.24), channel_id=1, source_target_pairs={{0,8},{1,9},{2,10},{3,11},{4,12},{5,13},{6,14},{7,15},{8,0},{9,1},... | collective-permute-start | bytes 786440 | tf_op jit(solution)/shard_map/ppermute | solution.py:40
  13.2 0.7 collective-permute-start.4
  13.9 1.9 %collective-permute-start.3 = (f32[4,16,8,128]{3,2,1,0:T(8,128)S(1)}, f32[4,16,8,128]{3,2,1,0:T(8,128)S(1)}, u32[]{:S(2)}, u32[]{:S(2)}) collective-permute-start(f32[4,16,8,128]{3,2,1,0:T(8,128)S(1)} %get-tuple-element.24), channel_id=1, source_target_pairs={{0,12},{1,13},{2,14},{3,15},{4,0},{5,1},{6,2},{7,3},{8,4},{9,5},{1... | collective-permute-start | bytes 786440 | tf_op jit(solution)/shard_map/ppermute | solution.py:40
  15.9 0.7 fusion.7
  16.7 6.3 %collective-permute-start.6 = (f32[4,16,8,128]{3,2,1,0:T(8,128)S(1)}, f32[4,16,8,128]{3,2,1,0:T(8,128)S(1)}, u32[]{:S(2)}, u32[]{:S(2)}) collective-permute-start(f32[4,16,8,128]{3,2,1,0:T(8,128)S(1)} %get-tuple-element.24), channel_id=1, source_target_pairs={{16,32},{17,33},{18,34},{19,35},{20,36},{21,37},{22,38},{23,39},{2... | collective-permute-start | bytes 786440 | tf_op jit(solution)/shard_map/ppermute | solution.py:40
  23.2 3.4 %collective-permute-start.7 = (f32[3,4,16,8,128]{4,3,2,1,0:T(8,128)S(1)}, f32[3,4,16,8,128]{4,3,2,1,0:T(8,128)S(1)}, u32[]{:S(2)}, u32[]{:S(2)}) collective-permute-start(f32[3,4,16,8,128]{4,3,2,1,0:T(8,128)S(1)} %pad_maximum_fusion.2.ready_ref), channel_id=1, source_target_pairs={{16,32},{17,33},{18,34},{19,35},{20,36},{21,37},{22,38},{23,39},{2... | collective-permute-start | bytes 2359304 | tf_op jit(solution)/shard_map/ppermute | solution.py:40
  26.7 2.9 %prepare.1.matrices_ref = bf16[16,128,1024]{2,1,0:T(8,128)(2,1)S(1)} custom-call(f32[16,16,4096]{2,1,0:T(8,128)S(1)} %copy-done.2, f32[3,4,16,8,128]{4,3,2,1,0:T(8,128)S(1)} %pad_maximum_fusion.2.ready_ref), custom_call_target="tpu_custom_call" | custom-call | flops 16777216 | bytes 8388608 | tf_op jit(solution)/shard_map/prepare/pallas_call | solution.py:122
  29.6 3.4 %copy-done = f32[2,1024,1024]{2,1,0:T(8,128)S(1)} copy-done((f32[2,1024,1024]{2,1,0:T(8,128)S(1)}, f32[2,1024,1024]{2,1,0:T(8,128)}, u32[]{:S(2)}) %copy-start) | copy-done | bytes 8388632
  33.0 2.0 %halve.1 = (bf16[2,2,1024,1024]{3,2,1,0:T(8,128)(2,1)S(1)}, bf16[2,2,1024,512]{3,2,1,0:T(8,128)(2,1)S(1)}) custom-call(f32[2,1024,1024]{2,1,0:T(8,128)S(1)} %copy-done, f32[2,1024,512]{2,1,0:T(8,128)S(1)} %copy-done.1, f32[3,4,16,8,128]{4,3,2,1,0:T(8,128)S(1)} %pad_maximum_fusion.2.ready_ref), custom_call_target="tpu_custom_call" | custom-call | flops 16777216 | bytes 25165824 | tf_op jit(solution)/shard_map/halve/pallas_call | solution.py:144
  35.1 1.4 %collective-permute-done.7 = f32[3,4,16,8,128]{4,3,2,1,0:T(8,128)S(1)} collective-permute-done((f32[3,4,16,8,128]{4,3,2,1,0:T(8,128)S(1)}, f32[3,4,16,8,128]{4,3,2,1,0:T(8,128)S(1)}, u32[]{:S(2)}, u32[]{:S(2)}) %collective-permute-start.7) | collective-permute-done | bytes 786464 | tf_op jit(solution)/shard_map/ppermute | solution.py:40
  36.7 2.1 %apply_first.1 = (f32[16,8,128]{2,1,0:T(8,128)S(1)}, f32[2,4,16,128]{3,2,1,0:T(8,128)S(1)}) custom-call(s32[256]{0:T(256)S(1)} %reshape.21.places_ref, s32[16]{0:T(128)S(1)} %reshape.22.slots_ref, s32[2]{0:T(128)S(1)} %copy-done.3, f32[768,8,128]{2,1,0:T(8,128)S(1)} %bitcast.36, bf16[16,128,1024]{2,1,0:T(8,128)(2,1)S(1)} %prepare.1.matrices_ref, ...), custom_call_target="tpu_custom_call" | custom-call | flops 134217728 | bytes 8388608 | tf_op jit(solution)/shard_map/apply_first/pallas_call | solution.py:250
  38.8 1.6 %collective-permute-start.11 = (f32[16,8,128]{2,1,0:T(8,128)S(1)}, f32[16,8,128]{2,1,0:T(8,128)S(1)}, u32[]{:S(2)}, u32[]{:S(2)}) collective-permute-start(f32[16,8,128]{2,1,0:T(8,128)S(1)} %get-tuple-element.13.image_ref), channel_id=1, source_target_pairs={{0,2},{1,3},{2,0},{3,1},{4,6},{5,7},{6,4},{7,5},{8,10},{9,11},{10,... | collective-permute-start | bytes 196616 | tf_op jit(solution)/shard_map/ppermute | solution.py:40
  40.4 1.6 %collective-permute-start.10 = (f32[16,8,128]{2,1,0:T(8,128)S(1)}, f32[16,8,128]{2,1,0:T(8,128)S(1)}, u32[]{:S(2)}, u32[]{:S(2)}) collective-permute-start(f32[16,8,128]{2,1,0:T(8,128)S(1)} %get-tuple-element.13.image_ref), channel_id=1, source_target_pairs={{0,1},{1,2},{2,3},{3,0},{4,5},{5,6},{6,7},{7,4},{8,9},{9,10},{10,1... | collective-permute-start | bytes 196616 | tf_op jit(solution)/shard_map/ppermute | solution.py:40
  41.9 1.1 %collective-permute-start.9 = (f32[16,8,128]{2,1,0:T(8,128)S(1)}, f32[16,8,128]{2,1,0:T(8,128)S(1)}, u32[]{:S(2)}, u32[]{:S(2)}) collective-permute-start(f32[16,8,128]{2,1,0:T(8,128)S(1)} %get-tuple-element.13.image_ref), channel_id=1, source_target_pairs={{0,3},{1,0},{2,1},{3,2},{4,7},{5,4},{6,5},{7,6},{8,11},{9,8},{10,9... | collective-permute-start | bytes 196616 | tf_op jit(solution)/shard_map/ppermute | solution.py:40
  43.0 0.6 collective-permute-done.11
  43.7 1.2 %collective-permute-done.10 = f32[16,8,128]{2,1,0:T(8,128)S(1)} collective-permute-done((f32[16,8,128]{2,1,0:T(8,128)S(1)}, f32[16,8,128]{2,1,0:T(8,128)S(1)}, u32[]{:S(2)}, u32[]{:S(2)}) %collective-permute-start.10) | collective-permute-done | bytes 65568 | tf_op jit(solution)/shard_map/ppermute | solution.py:40
  45.1 1.5 %collective-permute-start.14 = (f32[4,16,8,128]{3,2,1,0:T(8,128)S(1)}, f32[4,16,8,128]{3,2,1,0:T(8,128)S(1)}, u32[]{:S(2)}, u32[]{:S(2)}) collective-permute-start(f32[4,16,8,128]{3,2,1,0:T(8,128)S(1)} %get-tuple-element.22), channel_id=1, source_target_pairs={{0,8},{1,9},{2,10},{3,11},{4,12},{5,13},{6,14},{7,15},{8,0},{9,1},... | collective-permute-start | bytes 786440 | tf_op jit(solution)/shard_map/ppermute | solution.py:40
  46.6 2.1 %collective-permute-start.13 = (f32[4,16,8,128]{3,2,1,0:T(8,128)S(1)}, f32[4,16,8,128]{3,2,1,0:T(8,128)S(1)}, u32[]{:S(2)}, u32[]{:S(2)}) collective-permute-start(f32[4,16,8,128]{3,2,1,0:T(8,128)S(1)} %get-tuple-element.22), channel_id=1, source_target_pairs={{0,4},{1,5},{2,6},{3,7},{4,8},{5,9},{6,10},{7,11},{8,12},{9,13},{1... | collective-permute-start | bytes 786440 | tf_op jit(solution)/shard_map/ppermute | solution.py:40
  48.7 0.6 collective-permute-start.12
  49.3 6.7 %collective-permute-start.15 = (f32[4,16,8,128]{3,2,1,0:T(8,128)S(1)}, f32[4,16,8,128]{3,2,1,0:T(8,128)S(1)}, u32[]{:S(2)}, u32[]{:S(2)}) collective-permute-start(f32[4,16,8,128]{3,2,1,0:T(8,128)S(1)} %get-tuple-element.22), channel_id=1, source_target_pairs={{16,32},{17,33},{18,34},{19,35},{20,36},{21,37},{22,38},{23,39},{2... | collective-permute-start | bytes 786440 | tf_op jit(solution)/shard_map/ppermute | solution.py:40
  56.2 5.7 %collective-permute-start.16 = (f32[3,4,16,8,128]{4,3,2,1,0:T(8,128)S(1)}, f32[3,4,16,8,128]{4,3,2,1,0:T(8,128)S(1)}, u32[]{:S(2)}, u32[]{:S(2)}) collective-permute-start(f32[3,4,16,8,128]{4,3,2,1,0:T(8,128)S(1)} %pad_maximum_fusion.3.ready_ref), channel_id=1, source_target_pairs={{16,32},{17,33},{18,34},{19,35},{20,36},{21,37},{22,38},{23,39},{2... | collective-permute-start | bytes 2359304 | tf_op jit(solution)/shard_map/ppermute | solution.py:40
  62.3 8.9 %fold.1 = (bf16[2,2,1024,512]{3,2,1,0:T(8,128)(2,1)S(1)}, f32[2,16,1024]{2,1,0:T(8,128)S(1)}) custom-call(bf16[2,2,1024,1024]{3,2,1,0:T(8,128)(2,1)S(1)} %get-tuple-element.12.halves_ref.inverse_ref, bf16[2,2,1024,512]{3,2,1,0:T(8,128)(2,1)S(1)} %get-tuple-element.14.coupling_ref, f32[2,16,1024]{2,1,0:T(8,128)S(1)} %copy-done.4, ...), custom_call_target="tpu_custom_call" | custom-call | flops 8589934592 | bytes 16777216 | tf_op jit(solution)/shard_map/fold/pallas_call | solution.py:304
  71.7 3.2 %apply_second.1 = (f32[16,8,128]{2,1,0:T(8,128)S(1)}, f32[64,8,128]{2,1,0:T(8,128)S(1)}, f32[2,32,1024]{2,1,0:T(8,128)S(1)}) custom-call(s32[256]{0:T(256)S(1)} %reshape.21.places_ref, s32[16]{0:T(128)S(1)} %reshape.22.slots_ref, s32[2]{0:T(128)S(1)} %copy-done.3, f32[768,8,128]{2,1,0:T(8,128)S(1)} %bitcast.37, ...), custom_call_target="tpu_custom_call" | custom-call | flops 134217728 | bytes 8388608 | tf_op jit(solution)/shard_map/apply_second/pallas_call | solution.py:263
  75.0 17.8 %all_to_all.5 = f32[64,8,128]{2,1,0:T(8,128)S(1)} all-to-all(f32[64,8,128]{2,1,0:T(8,128)S(1)} %get-tuple-element.17), channel_id=1, replica_groups=mesh['y'=4,'core'=2,'x'=4,'z'=4] {'y','x','z'}, dimensions={0} | all-to-all | bytes 524288 | tf_op jit(solution)/shard_map/all_to_all | solution.py:411
  92.9 2.2 %collective-permute-start.18 = (f32[8,128]{1,0:T(8,128)S(1)}, f32[8,128]{1,0:T(8,128)S(1)}, u32[]{:S(2)}, u32[]{:S(2)}) collective-permute-start(f32[8,128]{1,0:T(8,128)S(1)} %reduce_sum.9.sums_ref), channel_id=1, source_target_pairs={{0,16},{1,17},{2,18},{3,19},{4,20},{5,21},{6,22},{7,23},{8,24},{9,... | collective-permute-start | bytes 12296 | tf_op jit(solution)/shard_map/ppermute | solution.py:40
  95.0 0.8 collective-permute-done.18.others_ref
  95.8 0.9 finish.1
  (49 shorter events, 2.3 us)
Async XLA Ops:
  1.5 7.1 %collective-permute-start.2 = (f32[16,8,128]{2,1,0:T(8,128)S(1)}, f32[16,8,128]{2,1,0:T(8,128)S(1)}, u32[]{:S(2)}, u32[]{:S(2)}) collective-permute-start(f32[16,8,128]{2,1,0:T(8,128)S(1)} %bitcast.38), channel_id=1, source_target_pairs={{0,2},{1,3},{2,0},{3,1},{4,6},{5,7},{6,4},{7,5},{8,10},{9,11},{10,... | collective-permute-start | bytes 196616 | tf_op jit(solution)/shard_map/ppermute | solution.py:40
  5.1 4.3 %collective-permute-start.1 = (f32[16,8,128]{2,1,0:T(8,128)S(1)}, f32[16,8,128]{2,1,0:T(8,128)S(1)}, u32[]{:S(2)}, u32[]{:S(2)}) collective-permute-start(f32[16,8,128]{2,1,0:T(8,128)S(1)} %bitcast.39), channel_id=1, source_target_pairs={{0,1},{1,2},{2,3},{3,0},{4,5},{5,6},{6,7},{7,4},{8,9},{9,10},{10,1... | collective-permute-start | bytes 196616 | tf_op jit(solution)/shard_map/ppermute | solution.py:40
  5.5 4.0 %collective-permute-start = (f32[16,8,128]{2,1,0:T(8,128)S(1)}, f32[16,8,128]{2,1,0:T(8,128)S(1)}, u32[]{:S(2)}, u32[]{:S(2)}) collective-permute-start(f32[16,8,128]{2,1,0:T(8,128)S(1)} %bitcast.40), channel_id=1, source_target_pairs={{0,3},{1,0},{2,1},{3,2},{4,7},{5,4},{6,5},{7,6},{8,11},{9,8},{10,9... | collective-permute-start | bytes 196616 | tf_op jit(solution)/shard_map/ppermute | solution.py:40
  9.5 13.5 %collective-permute-start.5 = (f32[4,16,8,128]{3,2,1,0:T(8,128)S(1)}, f32[4,16,8,128]{3,2,1,0:T(8,128)S(1)}, u32[]{:S(2)}, u32[]{:S(2)}) collective-permute-start(f32[4,16,8,128]{3,2,1,0:T(8,128)S(1)} %get-tuple-element.24), channel_id=1, source_target_pairs={{0,8},{1,9},{2,10},{3,11},{4,12},{5,13},{6,14},{7,15},{8,0},{9,1},... | collective-permute-start | bytes 786440 | tf_op jit(solution)/shard_map/ppermute | solution.py:40
  13.2 9.8 %collective-permute-start.4 = (f32[4,16,8,128]{3,2,1,0:T(8,128)S(1)}, f32[4,16,8,128]{3,2,1,0:T(8,128)S(1)}, u32[]{:S(2)}, u32[]{:S(2)}) collective-permute-start(f32[4,16,8,128]{3,2,1,0:T(8,128)S(1)} %get-tuple-element.24), channel_id=1, source_target_pairs={{0,4},{1,5},{2,6},{3,7},{4,8},{5,9},{6,10},{7,11},{8,12},{9,13},{1... | collective-permute-start | bytes 786440 | tf_op jit(solution)/shard_map/ppermute | solution.py:40
  13.9 9.1 %collective-permute-start.3 = (f32[4,16,8,128]{3,2,1,0:T(8,128)S(1)}, f32[4,16,8,128]{3,2,1,0:T(8,128)S(1)}, u32[]{:S(2)}, u32[]{:S(2)}) collective-permute-start(f32[4,16,8,128]{3,2,1,0:T(8,128)S(1)} %get-tuple-element.24), channel_id=1, source_target_pairs={{0,12},{1,13},{2,14},{3,15},{4,0},{5,1},{6,2},{7,3},{8,4},{9,5},{1... | collective-permute-start | bytes 786440 | tf_op jit(solution)/shard_map/ppermute | solution.py:40
  16.7 10.0 %copy-start.2 = (f32[16,16,4096]{2,1,0:T(8,128)S(1)}, f32[16,16,4096]{2,1,0:T(8,128)}, u32[]{:S(2)}) copy-start(f32[16,16,4096]{2,1,0:T(8,128)} %values_ref.1) | copy-start | bytes 12582916
  16.7 18.4 %collective-permute-start.6 = (f32[4,16,8,128]{3,2,1,0:T(8,128)S(1)}, f32[4,16,8,128]{3,2,1,0:T(8,128)S(1)}, u32[]{:S(2)}, u32[]{:S(2)}) collective-permute-start(f32[4,16,8,128]{3,2,1,0:T(8,128)S(1)} %get-tuple-element.24), channel_id=1, source_target_pairs={{16,32},{17,33},{18,34},{19,35},{20,36},{21,37},{22,38},{23,39},{2... | collective-permute-start | bytes 786440 | tf_op jit(solution)/shard_map/ppermute | solution.py:40
  23.2 13.3 %collective-permute-start.7 = (f32[3,4,16,8,128]{4,3,2,1,0:T(8,128)S(1)}, f32[3,4,16,8,128]{4,3,2,1,0:T(8,128)S(1)}, u32[]{:S(2)}, u32[]{:S(2)}) collective-permute-start(f32[3,4,16,8,128]{4,3,2,1,0:T(8,128)S(1)} %pad_maximum_fusion.2.ready_ref), channel_id=1, source_target_pairs={{16,32},{17,33},{18,34},{19,35},{20,36},{21,37},{22,38},{23,39},{2... | collective-permute-start | bytes 2359304 | tf_op jit(solution)/shard_map/ppermute | solution.py:40
  26.6 10.0 %collective-permute-start.8 = (f32[4,4,16,8,128]{4,3,2,1,0:T(8,128)S(1)}, f32[4,4,16,8,128]{4,3,2,1,0:T(8,128)S(1)}, u32[]{:S(2)}, u32[]{:S(2)}) collective-permute-start(f32[4,4,16,8,128]{4,3,2,1,0:T(8,128)S(1)} %pad_maximum_fusion), channel_id=1, source_target_pairs={{0,16},{1,17},{2,18},{3,19},{4,20},{5,21},{6,22},{7,23},{8,24},{9,... | collective-permute-start | bytes 3145736 | tf_op jit(solution)/shard_map/ppermute | solution.py:40
  26.7 2.9 %copy-start.1 = (f32[2,1024,512]{2,1,0:T(8,128)S(1)}, f32[2,1024,512]{2,1,0:T(8,128)}, u32[]{:S(2)}) copy-start(f32[2,1024,512]{2,1,0:T(8,128)} %coupling_ref.1) | copy-start | bytes 12582916
  29.6 3.4 %copy-start = (f32[2,1024,1024]{2,1,0:T(8,128)S(1)}, f32[2,1024,1024]{2,1,0:T(8,128)}, u32[]{:S(2)}) copy-start(f32[2,1024,1024]{2,1,0:T(8,128)} %inverse_ref.1) | copy-start | bytes 25165828
  35.0 1.7 %copy-start.3 = (s32[2]{0:T(128)S(1)}, s32[2]{0:T(128)}, u32[]{:S(2)}) copy-start(s32[2]{0:T(128)} %live_ref.3) | copy-start | bytes 28
  38.8 4.9 %collective-permute-start.11 = (f32[16,8,128]{2,1,0:T(8,128)S(1)}, f32[16,8,128]{2,1,0:T(8,128)S(1)}, u32[]{:S(2)}, u32[]{:S(2)}) collective-permute-start(f32[16,8,128]{2,1,0:T(8,128)S(1)} %get-tuple-element.13.image_ref), channel_id=1, source_target_pairs={{0,2},{1,3},{2,0},{3,1},{4,6},{5,7},{6,4},{7,5},{8,10},{9,11},{10,... | collective-permute-start | bytes 196616 | tf_op jit(solution)/shard_map/ppermute | solution.py:40
  40.4 4.5 %collective-permute-start.10 = (f32[16,8,128]{2,1,0:T(8,128)S(1)}, f32[16,8,128]{2,1,0:T(8,128)S(1)}, u32[]{:S(2)}, u32[]{:S(2)}) collective-permute-start(f32[16,8,128]{2,1,0:T(8,128)S(1)} %get-tuple-element.13.image_ref), channel_id=1, source_target_pairs={{0,1},{1,2},{2,3},{3,0},{4,5},{5,6},{6,7},{7,4},{8,9},{9,10},{10,1... | collective-permute-start | bytes 196616 | tf_op jit(solution)/shard_map/ppermute | solution.py:40
  41.9 3.1 %collective-permute-start.9 = (f32[16,8,128]{2,1,0:T(8,128)S(1)}, f32[16,8,128]{2,1,0:T(8,128)S(1)}, u32[]{:S(2)}, u32[]{:S(2)}) collective-permute-start(f32[16,8,128]{2,1,0:T(8,128)S(1)} %get-tuple-element.13.image_ref), channel_id=1, source_target_pairs={{0,3},{1,0},{2,1},{3,2},{4,7},{5,4},{6,5},{7,6},{8,11},{9,8},{10,9... | collective-permute-start | bytes 196616 | tf_op jit(solution)/shard_map/ppermute | solution.py:40
  45.1 17.2 %copy-start.4 = (f32[2,16,1024]{2,1,0:T(8,128)S(1)}, f32[2,16,1024]{2,1,0:T(8,128)}, u32[]{:S(2)}) copy-start(f32[2,16,1024]{2,1,0:T(8,128)} %load_ref.1) | copy-start | bytes 393220
  45.1 10.9 %collective-permute-start.14 = (f32[4,16,8,128]{3,2,1,0:T(8,128)S(1)}, f32[4,16,8,128]{3,2,1,0:T(8,128)S(1)}, u32[]{:S(2)}, u32[]{:S(2)}) collective-permute-start(f32[4,16,8,128]{3,2,1,0:T(8,128)S(1)} %get-tuple-element.22), channel_id=1, source_target_pairs={{0,8},{1,9},{2,10},{3,11},{4,12},{5,13},{6,14},{7,15},{8,0},{9,1},... | collective-permute-start | bytes 786440 | tf_op jit(solution)/shard_map/ppermute | solution.py:40
  46.6 9.4 %collective-permute-start.13 = (f32[4,16,8,128]{3,2,1,0:T(8,128)S(1)}, f32[4,16,8,128]{3,2,1,0:T(8,128)S(1)}, u32[]{:S(2)}, u32[]{:S(2)}) collective-permute-start(f32[4,16,8,128]{3,2,1,0:T(8,128)S(1)} %get-tuple-element.22), channel_id=1, source_target_pairs={{0,4},{1,5},{2,6},{3,7},{4,8},{5,9},{6,10},{7,11},{8,12},{9,13},{1... | collective-permute-start | bytes 786440 | tf_op jit(solution)/shard_map/ppermute | solution.py:40
  48.7 7.3 %collective-permute-start.12 = (f32[4,16,8,128]{3,2,1,0:T(8,128)S(1)}, f32[4,16,8,128]{3,2,1,0:T(8,128)S(1)}, u32[]{:S(2)}, u32[]{:S(2)}) collective-permute-start(f32[4,16,8,128]{3,2,1,0:T(8,128)S(1)} %get-tuple-element.22), channel_id=1, source_target_pairs={{0,12},{1,13},{2,14},{3,15},{4,0},{5,1},{6,2},{7,3},{8,4},{9,5},{1... | collective-permute-start | bytes 786440 | tf_op jit(solution)/shard_map/ppermute | solution.py:40
  49.3 12.9 %collective-permute-start.15 = (f32[4,16,8,128]{3,2,1,0:T(8,128)S(1)}, f32[4,16,8,128]{3,2,1,0:T(8,128)S(1)}, u32[]{:S(2)}, u32[]{:S(2)}) collective-permute-start(f32[4,16,8,128]{3,2,1,0:T(8,128)S(1)} %get-tuple-element.22), channel_id=1, source_target_pairs={{16,32},{17,33},{18,34},{19,35},{20,36},{21,37},{22,38},{23,39},{2... | collective-permute-start | bytes 786440 | tf_op jit(solution)/shard_map/ppermute | solution.py:40
  56.2 15.4 %collective-permute-start.16 = (f32[3,4,16,8,128]{4,3,2,1,0:T(8,128)S(1)}, f32[3,4,16,8,128]{4,3,2,1,0:T(8,128)S(1)}, u32[]{:S(2)}, u32[]{:S(2)}) collective-permute-start(f32[3,4,16,8,128]{4,3,2,1,0:T(8,128)S(1)} %pad_maximum_fusion.3.ready_ref), channel_id=1, source_target_pairs={{16,32},{17,33},{18,34},{19,35},{20,36},{21,37},{22,38},{23,39},{2... | collective-permute-start | bytes 2359304 | tf_op jit(solution)/shard_map/ppermute | solution.py:40
  61.9 9.7 %collective-permute-start.17 = (f32[4,4,16,8,128]{4,3,2,1,0:T(8,128)S(1)}, f32[4,4,16,8,128]{4,3,2,1,0:T(8,128)S(1)}, u32[]{:S(2)}, u32[]{:S(2)}) collective-permute-start(f32[4,4,16,8,128]{4,3,2,1,0:T(8,128)S(1)} %pad_maximum_fusion.1), channel_id=1, source_target_pairs={{0,16},{1,17},{2,18},{3,19},{4,20},{5,21},{6,22},{7,23},{8,24},{9,... | collective-permute-start | bytes 3145736 | tf_op jit(solution)/shard_map/ppermute | solution.py:40
  92.9 3.0 %collective-permute-start.18 = (f32[8,128]{1,0:T(8,128)S(1)}, f32[8,128]{1,0:T(8,128)S(1)}, u32[]{:S(2)}, u32[]{:S(2)}) collective-permute-start(f32[8,128]{1,0:T(8,128)S(1)} %reduce_sum.9.sums_ref), channel_id=1, source_target_pairs={{0,16},{1,17},{2,18},{3,19},{4,20},{5,21},{6,22},{7,23},{8,24},{9,... | collective-permute-start | bytes 12296 | tf_op jit(solution)/shard_map/ppermute | solution.py:40

commit v4 on v3

--- a/solution.py
+++ b/solution.py
@@ -86,6 +86,16 @@
     high = value.astype(jnp.bfloat16)
     low = (value - high.astype(jnp.float32)).astype(jnp.bfloat16)
     return high, low
+
+
+def times(rows, high, low):
+    count = rows.shape[0]
+    top, bottom = split(rows)
+    main = lax.dot_general(
+        jnp.concatenate([top, bottom]), high, NT, preferred_element_type=jnp.float32
+    )
+    rest = lax.dot_general(top, low, NT, preferred_element_type=jnp.float32)
+    return main[:count] + main[count:] + rest
 
 
 def lane_ids(rows):
@@ -131,15 +141,21 @@
     )(values, ready)
 
 
-def halve_kernel(inverse_ref, coupling_ref, ready_ref, inverse_out_ref, coupling_out_ref):
+def halve_kernel(
+    inverse_ref, coupling_ref, load_ref, ready_ref, inverse_out_ref, coupling_out_ref, base_ref
+):
     sub = pl.program_id(0)
     size = inverse_ref.shape[1]
     rows = pl.ds(pl.multiple_of(pl.program_id(1) * size, size), size)
     for ref, out_ref in ((inverse_ref, inverse_out_ref), (coupling_ref, coupling_out_ref)):
         out_ref[sub, 0, rows, :], out_ref[sub, 1, rows, :] = split(ref[0])
 
-
-def halve(inverse, coupling, ready):
+    @pl.when(sub == 0)
+    def _():
+        base_ref[:, rows] = times(load_ref[0], *split(inverse_ref[0]))
+
+
+def halve(inverse, coupling, load, ready):
     cut = 256
     return pl.pallas_call(
         halve_kernel,
@@ -147,17 +163,19 @@
         in_specs=[
             pl.BlockSpec((1, cut, 1024), lambda s, n: (s, n, 0)),
             pl.BlockSpec((1, cut, 512), lambda s, n: (s, n, 0)),
+            VMEM_SPEC,
             ANY_SPEC,
         ],
-        out_specs=[VMEM_SPEC] * 2,
+        out_specs=[VMEM_SPEC] * 3,
         out_shape=[
             jax.ShapeDtypeStruct((2, 2, 1024, 1024), jnp.bfloat16),
             jax.ShapeDtypeStruct((2, 2, 1024, 512), jnp.bfloat16),
+            jax.ShapeDtypeStruct((CASES, 1024), jnp.float32),
         ],
         compiler_params=pltpu.CompilerParams(vmem_limit_bytes=20 * 2**20),
         cost_estimate=pl.CostEstimate(flops=2**24, bytes_accessed=3 * 2**23, transcendentals=0),
         name="halve",
-    )(inverse, coupling, ready)
+    )(inverse, coupling, load, ready)
 
 
 def apply_rows(places_ref, window_ref, matrices_ref, x_ref, out_ref):
@@ -280,10 +298,9 @@
     )(places, slots, live, window, matrices, load, image, folded, first)
 
 
-def fold_kernel(inverse_ref, coupling_ref, load_ref, ready_ref, folded_ref, base_ref, l_ref):
+def fold_kernel(inverse_ref, coupling_ref, load_ref, ready_ref, folded_ref, base_ref):
     cut = 256
-    for sub in range(2):
-        l_ref[sub, 0:16], l_ref[sub, 16:32] = split(load_ref[sub])
+    base_ref[...] = times(load_ref[1], inverse_ref[1, 0], inverse_ref[1, 1])
 
     @pl.loop(0, 2)
     def _(sub):
@@ -295,9 +312,6 @@
                 + jnp.dot(high, coupling_ref[sub, 1], preferred_element_type=jnp.float32)
                 + jnp.dot(low, coupling_ref[sub, 0], preferred_element_type=jnp.float32)
             )
-            main = lax.dot_general(l_ref[sub], high, NT, preferred_element_type=jnp.float32)
-            rest = lax.dot_general(l_ref[sub, 0:16], low, NT, preferred_element_type=jnp.float32)
-            base_ref[sub, :, rows] = main[0:16] + main[16:32] + rest
 
 
 def fold(inverse, coupling, load, ready):
@@ -307,9 +321,8 @@
         out_specs=[VMEM_SPEC] * 2,
         out_shape=[
             jax.ShapeDtypeStruct((2, 2, 1024, 512), jnp.bfloat16),
-            jax.ShapeDtypeStruct((2, CASES, 1024), jnp.float32),
-        ],
-        scratch_shapes=[pltpu.VMEM((2, 32, 1024), jnp.bfloat16)],
+            jax.ShapeDtypeStruct((CASES, 1024), jnp.float32),
+        ],
         compiler_params=pltpu.CompilerParams(vmem_limit_bytes=10 * 2**20),
         cost_estimate=pl.CostEstimate(flops=2**33, bytes_accessed=2**24, transcendentals=0),
         name="fold",
@@ -317,7 +330,7 @@
 
 
 def finish_kernel(
-    sums_ref, others_ref, load_ref, image_ref, twice_ref, base_ref, parts_ref, solution_ref, residual_ref, interior_ref, tiles_ref, cases_ref
+    sums_ref, others_ref, load_ref, image_ref, twice_ref, base0_ref, base1_ref, parts_ref, solution_ref, residual_ref, interior_ref, tiles_ref, cases_ref
 ):
     lanes = lane_ids(8)
     low_half = lanes < NB
@@ -361,16 +374,16 @@
             spread = jnp.broadcast_to(factor[:, h * NB : h * NB + 1], (8, LANES))
             cases_ref[place, pl.ds(h, 8, stride=2), :] = spread
     own, other = cases_ref[0][:, 0:1], cases_ref[1][:, 0:1]
-    for sub in range(2):
+    for sub, base_ref in enumerate((base0_ref, base1_ref)):
         interior_ref[sub] = (
-            base_ref[sub] - own * parts_ref[sub, 0:16] - other * parts_ref[sub, 16:32]
+            base_ref[...] - own * parts_ref[sub, 0:16] - other * parts_ref[sub, 16:32]
         )
 
 
-def finish(sums, others, load, image, twice, base, parts):
+def finish(sums, others, load, image, twice, base0, base1, parts):
     return pl.pallas_call(
         finish_kernel,
-        in_specs=[VMEM_SPEC] * 7,
+        in_specs=[VMEM_SPEC] * 8,
         out_specs=[VMEM_SPEC] * 3,
         out_shape=[
             jax.ShapeDtypeStruct((16, 1024), jnp.float32),
@@ -380,7 +393,7 @@
         scratch_shapes=[pltpu.VMEM((128, LANES), jnp.float32), pltpu.VMEM((2, 16, LANES), jnp.float32)],
         compiler_params=pltpu.CompilerParams(vmem_limit_bytes=8 * 2**20),
         name="finish",
-    )(sums, others, load, image, twice, base, parts)
+    )(sums, others, load, image, twice, base0, base1, parts)
 
 
 def body(
@@ -398,18 +411,22 @@
     places = locate(schur_columns, region, x, z).reshape(-1)
     slots = locate(adjacency, region, x, z).reshape(-1)
     load = interface_load.reshape(16, 8, LANES)
-    load_window, (matrices, (inverse, couplings)) = exchange(
-        load, lambda ready: (prepare(schur_values, ready), halve(layer_inverse, coupling, ready))
+    load_window, (matrices, (inverse, couplings, base0)) = exchange(
+        load,
+        lambda ready: (
+            prepare(schur_values, ready),
+            halve(layer_inverse, coupling, interior_load, ready),
+        ),
     )
     image, picked = apply_first(places, slots, live_counts, load_window, matrices, inverse)
-    image_window, (folded, base) = exchange(
+    image_window, (folded, base1) = exchange(
         image, lambda ready: fold(inverse, couplings, interior_load, ready)
     )
     twice, sums, parts = apply_second(
         places, slots, live_counts, image_window, matrices, load, image, folded, picked
     )
     sums = jnp.sum(lax.all_to_all(sums, ("y", "x", "z"), 0, 0), axis=0)
-    return tuple(finish(sums, permute(sums, partner), load, image, twice, base, parts))
+    return tuple(finish(sums, permute(sums, partner), load, image, twice, base0, base1, parts))
 
 
 def solution(mesh):

time: 97.1 us -> 97.5 us (level)
    pallas_call x1, Pallas kernels: 1.98 us -> 3.52 us  [halve(): pl.pallas_call(halve_kernel, grid=(2, 1024 // cut), in_specs=[pl.BlockSpe...]
  transfers between devices with their start and end apart: 19 -> 19, of which waited for: 7 -> 6; matrix products, arithmetic and copies ran while one was open for 2% -> 2% of each run, Pallas kernels for 14% -> 15%
where the time goes in v4:
time: 97.5 us; the launch traced here: 97.1 us
  starting transfers between devices  46 us (47%)
  Pallas kernels  20.7 us (21%)
  blocking collectives  17.1 us (18%)
  local copies, waits for them, and re-layouts  5.27 us (5%)
  waiting for transfers between devices  5.18 us (5%)
  other arithmetic  1.89 us (2%)
  between operations  1.02 us (1%)
    ppermute x19, starting transfers between devices, permute(): return lax.ppermute(value, AXES, pairs)  46 us
    all_to_all x1, blocking collectives, body(): sums = jnp.sum(lax.all_to_all(sums, ('y', 'x', 'z'), 0, 0), axis=0)  17.1 us
    pallas_call x1, Pallas kernels, fold(): pl.pallas_call(fold_kernel, in_specs=[VMEM_SPEC] * 3 + [ANY_SPEC], out_sp...  8.08 us
    ppermute x19, waiting for transfers between devices, permute(): return lax.ppermute(value, AXES, pairs)  5.18 us
    unnamed x21, local copies, waits for them, and re-layouts  4.92 us
    pallas_call x1, Pallas kernels, halve(): pl.pallas_call(halve_kernel, grid=(2, 1024 // cut), in_specs=[pl.BlockSpe...  3.52 us
    pallas_call x1, Pallas kernels, apply_second(): pl.pallas_call(second_kernel, in_specs=[SMEM_SPEC] * 3 + [VMEM_SPEC] * 6,...  3.23 us
    pallas_call x1, Pallas kernels, prepare(): pl.pallas_call(prepare_kernel, grid=(16,), in_specs=[pl.BlockSpec((1, 16,...  2.88 us
  transfers between devices with their start and end apart: 19, of which 6 were waited for; matrix products, arithmetic and copies ran while one was open for 2% of the time, Pallas kernels for 15%

profile of v4, /device:TPU:1, one launch (start us, length us, event | category | flops | bytes accessed | tf_op | source)
XLA Modules:
  0.0 97.1 jit_solution(13140845689711830252)
XLA Ops:
  0.6 0.9 copy.11
  1.5 3.7 %collective-permute-start.2 = (f32[16,8,128]{2,1,0:T(8,128)S(1)}, f32[16,8,128]{2,1,0:T(8,128)S(1)}, u32[]{:S(2)}, u32[]{:S(2)}) collective-permute-start(f32[16,8,128]{2,1,0:T(8,128)S(1)} %bitcast.38), channel_id=1, source_target_pairs={{0,2},{1,3},{2,0},{3,1},{4,6},{5,7},{6,4},{7,5},{8,10},{9,11},{10,... | collective-permute-start | bytes 196616 | tf_op jit(solution)/shard_map/ppermute | solution.py:40
  5.5 2.4 %collective-permute-start = (f32[16,8,128]{2,1,0:T(8,128)S(1)}, f32[16,8,128]{2,1,0:T(8,128)S(1)}, u32[]{:S(2)}, u32[]{:S(2)}) collective-permute-start(f32[16,8,128]{2,1,0:T(8,128)S(1)} %bitcast.40), channel_id=1, source_target_pairs={{0,3},{1,0},{2,1},{3,2},{4,7},{5,4},{6,5},{7,6},{8,11},{9,8},{10,9... | collective-permute-start | bytes 196616 | tf_op jit(solution)/shard_map/ppermute | solution.py:40
  7.8 0.7 fusion.13
  8.6 0.8 collective-permute-done.1
  9.5 3.7 %collective-permute-start.5 = (f32[4,16,8,128]{3,2,1,0:T(8,128)S(1)}, f32[4,16,8,128]{3,2,1,0:T(8,128)S(1)}, u32[]{:S(2)}, u32[]{:S(2)}) collective-permute-start(f32[4,16,8,128]{3,2,1,0:T(8,128)S(1)} %get-tuple-element.26), channel_id=1, source_target_pairs={{0,8},{1,9},{2,10},{3,11},{4,12},{5,13},{6,14},{7,15},{8,0},{9,1},... | collective-permute-start | bytes 786440 | tf_op jit(solution)/shard_map/ppermute | solution.py:40
  13.2 0.7 collective-permute-start.4
  13.9 1.9 %collective-permute-start.3 = (f32[4,16,8,128]{3,2,1,0:T(8,128)S(1)}, f32[4,16,8,128]{3,2,1,0:T(8,128)S(1)}, u32[]{:S(2)}, u32[]{:S(2)}) collective-permute-start(f32[4,16,8,128]{3,2,1,0:T(8,128)S(1)} %get-tuple-element.26), channel_id=1, source_target_pairs={{0,12},{1,13},{2,14},{3,15},{4,0},{5,1},{6,2},{7,3},{8,4},{9,5},{1... | collective-permute-start | bytes 786440 | tf_op jit(solution)/shard_map/ppermute | solution.py:40
  15.9 0.7 fusion.7
  16.7 6.3 %collective-permute-start.6 = (f32[4,16,8,128]{3,2,1,0:T(8,128)S(1)}, f32[4,16,8,128]{3,2,1,0:T(8,128)S(1)}, u32[]{:S(2)}, u32[]{:S(2)}) collective-permute-start(f32[4,16,8,128]{3,2,1,0:T(8,128)S(1)} %get-tuple-element.26), channel_id=1, source_target_pairs={{16,32},{17,33},{18,34},{19,35},{20,36},{21,37},{22,38},{23,39},{2... | collective-permute-start | bytes 786440 | tf_op jit(solution)/shard_map/ppermute | solution.py:40
  23.2 3.4 %collective-permute-start.7 = (f32[3,4,16,8,128]{4,3,2,1,0:T(8,128)S(1)}, f32[3,4,16,8,128]{4,3,2,1,0:T(8,128)S(1)}, u32[]{:S(2)}, u32[]{:S(2)}) collective-permute-start(f32[3,4,16,8,128]{4,3,2,1,0:T(8,128)S(1)} %pad_maximum_fusion.2.ready_ref), channel_id=1, source_target_pairs={{16,32},{17,33},{18,34},{19,35},{20,36},{21,37},{22,38},{23,39},{2... | collective-permute-start | bytes 2359304 | tf_op jit(solution)/shard_map/ppermute | solution.py:40
  26.7 2.9 %prepare.1.matrices_ref = bf16[16,128,1024]{2,1,0:T(8,128)(2,1)S(1)} custom-call(f32[16,16,4096]{2,1,0:T(8,128)S(1)} %copy-done.2, f32[3,4,16,8,128]{4,3,2,1,0:T(8,128)S(1)} %pad_maximum_fusion.2.ready_ref), custom_call_target="tpu_custom_call" | custom-call | flops 16777216 | bytes 8388608 | tf_op jit(solution)/shard_map/prepare/pallas_call | solution.py:132
  29.7 3.4 %copy-done = f32[2,1024,1024]{2,1,0:T(8,128)S(1)} copy-done((f32[2,1024,1024]{2,1,0:T(8,128)S(1)}, f32[2,1024,1024]{2,1,0:T(8,128)}, u32[]{:S(2)}) %copy-start) | copy-done | bytes 8388632
  33.0 3.5 %halve.1 = (bf16[2,2,1024,1024]{3,2,1,0:T(8,128)(2,1)S(1)}, bf16[2,2,1024,512]{3,2,1,0:T(8,128)(2,1)S(1)}, f32[16,1024]{1,0:T(8,128)S(1)}) custom-call(f32[2,1024,1024]{2,1,0:T(8,128)S(1)} %copy-done, f32[2,1024,512]{2,1,0:T(8,128)S(1)} %copy-done.1, f32[2,16,1024]{2,1,0:T(8,128)S(1)} %copy-done.3, f32[3,4,16,8,128]{4,3,2,1,0:T(8,128)S(1)} %pad_maximum_fusion.2.ready_ref), custom_call_target="tpu_custom_call" | custom-call | flops 16777216 | bytes 25165824 | tf_op jit(solution)/shard_map/halve/pallas_call | solution.py:160
  36.8 0.4 copy-done.4
  37.2 2.1 %apply_first.1 = (f32[16,8,128]{2,1,0:T(8,128)S(1)}, f32[2,4,16,128]{3,2,1,0:T(8,128)S(1)}) custom-call(s32[256]{0:T(256)S(1)} %reshape.21.places_ref, s32[16]{0:T(128)S(1)} %reshape.22.slots_ref, s32[2]{0:T(128)S(1)} %copy-done.4, f32[768,8,128]{2,1,0:T(8,128)S(1)} %bitcast.36, bf16[16,128,1024]{2,1,0:T(8,128)(2,1)S(1)} %prepare.1.matrices_ref, ...), custom_call_target="tpu_custom_call" | custom-call | flops 134217728 | bytes 8388608 | tf_op jit(solution)/shard_map/apply_first/pallas_call | solution.py:268
  39.3 1.9 %collective-permute-start.11 = (f32[16,8,128]{2,1,0:T(8,128)S(1)}, f32[16,8,128]{2,1,0:T(8,128)S(1)}, u32[]{:S(2)}, u32[]{:S(2)}) collective-permute-start(f32[16,8,128]{2,1,0:T(8,128)S(1)} %get-tuple-element.14.image_ref), channel_id=1, source_target_pairs={{0,2},{1,3},{2,0},{3,1},{4,6},{5,7},{6,4},{7,5},{8,10},{9,11},{10,... | collective-permute-start | bytes 196616 | tf_op jit(solution)/shard_map/ppermute | solution.py:40
  41.2 1.6 %collective-permute-start.10 = (f32[16,8,128]{2,1,0:T(8,128)S(1)}, f32[16,8,128]{2,1,0:T(8,128)S(1)}, u32[]{:S(2)}, u32[]{:S(2)}) collective-permute-start(f32[16,8,128]{2,1,0:T(8,128)S(1)} %get-tuple-element.14.image_ref), channel_id=1, source_target_pairs={{0,1},{1,2},{2,3},{3,0},{4,5},{5,6},{6,7},{7,4},{8,9},{9,10},{10,1... | collective-permute-start | bytes 196616 | tf_op jit(solution)/shard_map/ppermute | solution.py:40
  42.7 1.1 %collective-permute-start.9 = (f32[16,8,128]{2,1,0:T(8,128)S(1)}, f32[16,8,128]{2,1,0:T(8,128)S(1)}, u32[]{:S(2)}, u32[]{:S(2)}) collective-permute-start(f32[16,8,128]{2,1,0:T(8,128)S(1)} %get-tuple-element.14.image_ref), channel_id=1, source_target_pairs={{0,3},{1,0},{2,1},{3,2},{4,7},{5,4},{6,5},{7,6},{8,11},{9,8},{10,9... | collective-permute-start | bytes 196616 | tf_op jit(solution)/shard_map/ppermute | solution.py:40
  44.0 1.8 %collective-permute-done.10 = f32[16,8,128]{2,1,0:T(8,128)S(1)} collective-permute-done((f32[16,8,128]{2,1,0:T(8,128)S(1)}, f32[16,8,128]{2,1,0:T(8,128)S(1)}, u32[]{:S(2)}, u32[]{:S(2)}) %collective-permute-start.10) | collective-permute-done | bytes 65568 | tf_op jit(solution)/shard_map/ppermute | solution.py:40
  45.8 0.4 collective-permute-done.9
  46.2 1.3 %collective-permute-start.14 = (f32[4,16,8,128]{3,2,1,0:T(8,128)S(1)}, f32[4,16,8,128]{3,2,1,0:T(8,128)S(1)}, u32[]{:S(2)}, u32[]{:S(2)}) collective-permute-start(f32[4,16,8,128]{3,2,1,0:T(8,128)S(1)} %get-tuple-element.24), channel_id=1, source_target_pairs={{0,8},{1,9},{2,10},{3,11},{4,12},{5,13},{6,14},{7,15},{8,0},{9,1},... | collective-permute-start | bytes 786440 | tf_op jit(solution)/shard_map/ppermute | solution.py:40
  47.5 2.3 %collective-permute-start.13 = (f32[4,16,8,128]{3,2,1,0:T(8,128)S(1)}, f32[4,16,8,128]{3,2,1,0:T(8,128)S(1)}, u32[]{:S(2)}, u32[]{:S(2)}) collective-permute-start(f32[4,16,8,128]{3,2,1,0:T(8,128)S(1)} %get-tuple-element.24), channel_id=1, source_target_pairs={{0,4},{1,5},{2,6},{3,7},{4,8},{5,9},{6,10},{7,11},{8,12},{9,13},{1... | collective-permute-start | bytes 786440 | tf_op jit(solution)/shard_map/ppermute | solution.py:40
  50.1 6.6 %collective-permute-start.15 = (f32[4,16,8,128]{3,2,1,0:T(8,128)S(1)}, f32[4,16,8,128]{3,2,1,0:T(8,128)S(1)}, u32[]{:S(2)}, u32[]{:S(2)}) collective-permute-start(f32[4,16,8,128]{3,2,1,0:T(8,128)S(1)} %get-tuple-element.24), channel_id=1, source_target_pairs={{16,32},{17,33},{18,34},{19,35},{20,36},{21,37},{22,38},{23,39},{2... | collective-permute-start | bytes 786440 | tf_op jit(solution)/shard_map/ppermute | solution.py:40
  56.9 5.7 %collective-permute-start.16 = (f32[3,4,16,8,128]{4,3,2,1,0:T(8,128)S(1)}, f32[3,4,16,8,128]{4,3,2,1,0:T(8,128)S(1)}, u32[]{:S(2)}, u32[]{:S(2)}) collective-permute-start(f32[3,4,16,8,128]{4,3,2,1,0:T(8,128)S(1)} %pad_maximum_fusion.3.ready_ref), channel_id=1, source_target_pairs={{16,32},{17,33},{18,34},{19,35},{20,36},{21,37},{22,38},{23,39},{2... | collective-permute-start | bytes 2359304 | tf_op jit(solution)/shard_map/ppermute | solution.py:40
  63.1 8.1 %fold.1 = (bf16[2,2,1024,512]{3,2,1,0:T(8,128)(2,1)S(1)}, f32[16,1024]{1,0:T(8,128)S(1)}) custom-call(bf16[2,2,1024,1024]{3,2,1,0:T(8,128)(2,1)S(1)} %get-tuple-element.13.halves_ref.inverse_ref, bf16[2,2,1024,512]{3,2,1,0:T(8,128)(2,1)S(1)} %get-tuple-element.15.coupling_ref, f32[2,16,1024]{2,1,0:T(8,128)S(1)} %copy-done.3, ...), custom_call_target="tpu_custom_call" | custom-call | flops 8589934592 | bytes 16777216 | tf_op jit(solution)/shard_map/fold/pallas_call | solution.py:318
  71.1 1.2 %collective-permute-done.16 = f32[3,4,16,8,128]{4,3,2,1,0:T(8,128)S(1)} collective-permute-done((f32[3,4,16,8,128]{4,3,2,1,0:T(8,128)S(1)}, f32[3,4,16,8,128]{4,3,2,1,0:T(8,128)S(1)}, u32[]{:S(2)}, u32[]{:S(2)}) %collective-permute-start.16) | collective-permute-done | bytes 786464 | tf_op jit(solution)/shard_map/ppermute | solution.py:40
  72.5 3.2 %apply_second.1 = (f32[16,8,128]{2,1,0:T(8,128)S(1)}, f32[64,8,128]{2,1,0:T(8,128)S(1)}, f32[2,32,1024]{2,1,0:T(8,128)S(1)}) custom-call(s32[256]{0:T(256)S(1)} %reshape.21.places_ref, s32[16]{0:T(128)S(1)} %reshape.22.slots_ref, s32[2]{0:T(128)S(1)} %copy-done.4, f32[768,8,128]{2,1,0:T(8,128)S(1)} %bitcast.37, ...), custom_call_target="tpu_custom_call" | custom-call | flops 134217728 | bytes 8388608 | tf_op jit(solution)/shard_map/apply_second/pallas_call | solution.py:281
  75.7 17.1 %all_to_all.5 = f32[64,8,128]{2,1,0:T(8,128)S(1)} all-to-all(f32[64,8,128]{2,1,0:T(8,128)S(1)} %get-tuple-element.18), channel_id=1, replica_groups=mesh['y'=4,'core'=2,'x'=4,'z'=4] {'y','x','z'}, dimensions={0} | all-to-all | bytes 524288 | tf_op jit(solution)/shard_map/all_to_all | solution.py:428
  92.9 2.5 %collective-permute-start.18 = (f32[8,128]{1,0:T(8,128)S(1)}, f32[8,128]{1,0:T(8,128)S(1)}, u32[]{:S(2)}, u32[]{:S(2)}) collective-permute-start(f32[8,128]{1,0:T(8,128)S(1)} %reduce_sum.9.sums_ref), channel_id=1, source_target_pairs={{0,16},{1,17},{2,18},{3,19},{4,20},{5,21},{6,22},{7,23},{8,24},{9,... | collective-permute-start | bytes 12296 | tf_op jit(solution)/shard_map/ppermute | solution.py:40
  95.4 0.8 collective-permute-done.18.others_ref
  96.2 0.9 finish.1
  (49 shorter events, 2.3 us)
Async XLA Ops:
  1.5 7.1 %collective-permute-start.2 = (f32[16,8,128]{2,1,0:T(8,128)S(1)}, f32[16,8,128]{2,1,0:T(8,128)S(1)}, u32[]{:S(2)}, u32[]{:S(2)}) collective-permute-start(f32[16,8,128]{2,1,0:T(8,128)S(1)} %bitcast.38), channel_id=1, source_target_pairs={{0,2},{1,3},{2,0},{3,1},{4,6},{5,7},{6,4},{7,5},{8,10},{9,11},{10,... | collective-permute-start | bytes 196616 | tf_op jit(solution)/shard_map/ppermute | solution.py:40
  5.1 4.3 %collective-permute-start.1 = (f32[16,8,128]{2,1,0:T(8,128)S(1)}, f32[16,8,128]{2,1,0:T(8,128)S(1)}, u32[]{:S(2)}, u32[]{:S(2)}) collective-permute-start(f32[16,8,128]{2,1,0:T(8,128)S(1)} %bitcast.39), channel_id=1, source_target_pairs={{0,1},{1,2},{2,3},{3,0},{4,5},{5,6},{6,7},{7,4},{8,9},{9,10},{10,1... | collective-permute-start | bytes 196616 | tf_op jit(solution)/shard_map/ppermute | solution.py:40
  5.5 4.0 %collective-permute-start = (f32[16,8,128]{2,1,0:T(8,128)S(1)}, f32[16,8,128]{2,1,0:T(8,128)S(1)}, u32[]{:S(2)}, u32[]{:S(2)}) collective-permute-start(f32[16,8,128]{2,1,0:T(8,128)S(1)} %bitcast.40), channel_id=1, source_target_pairs={{0,3},{1,0},{2,1},{3,2},{4,7},{5,4},{6,5},{7,6},{8,11},{9,8},{10,9... | collective-permute-start | bytes 196616 | tf_op jit(solution)/shard_map/ppermute | solution.py:40
  9.5 13.5 %collective-permute-start.5 = (f32[4,16,8,128]{3,2,1,0:T(8,128)S(1)}, f32[4,16,8,128]{3,2,1,0:T(8,128)S(1)}, u32[]{:S(2)}, u32[]{:S(2)}) collective-permute-start(f32[4,16,8,128]{3,2,1,0:T(8,128)S(1)} %get-tuple-element.26), channel_id=1, source_target_pairs={{0,8},{1,9},{2,10},{3,11},{4,12},{5,13},{6,14},{7,15},{8,0},{9,1},... | collective-permute-start | bytes 786440 | tf_op jit(solution)/shard_map/ppermute | solution.py:40
  13.2 9.8 %collective-permute-start.4 = (f32[4,16,8,128]{3,2,1,0:T(8,128)S(1)}, f32[4,16,8,128]{3,2,1,0:T(8,128)S(1)}, u32[]{:S(2)}, u32[]{:S(2)}) collective-permute-start(f32[4,16,8,128]{3,2,1,0:T(8,128)S(1)} %get-tuple-element.26), channel_id=1, source_target_pairs={{0,4},{1,5},{2,6},{3,7},{4,8},{5,9},{6,10},{7,11},{8,12},{9,13},{1... | collective-permute-start | bytes 786440 | tf_op jit(solution)/shard_map/ppermute | solution.py:40
  13.9 9.1 %collective-permute-start.3 = (f32[4,16,8,128]{3,2,1,0:T(8,128)S(1)}, f32[4,16,8,128]{3,2,1,0:T(8,128)S(1)}, u32[]{:S(2)}, u32[]{:S(2)}) collective-permute-start(f32[4,16,8,128]{3,2,1,0:T(8,128)S(1)} %get-tuple-element.26), channel_id=1, source_target_pairs={{0,12},{1,13},{2,14},{3,15},{4,0},{5,1},{6,2},{7,3},{8,4},{9,5},{1... | collective-permute-start | bytes 786440 | tf_op jit(solution)/shard_map/ppermute | solution.py:40
  16.7 10.0 %copy-start.2 = (f32[16,16,4096]{2,1,0:T(8,128)S(1)}, f32[16,16,4096]{2,1,0:T(8,128)}, u32[]{:S(2)}) copy-start(f32[16,16,4096]{2,1,0:T(8,128)} %values_ref.1) | copy-start | bytes 12582916
  16.7 19.9 %collective-permute-start.6 = (f32[4,16,8,128]{3,2,1,0:T(8,128)S(1)}, f32[4,16,8,128]{3,2,1,0:T(8,128)S(1)}, u32[]{:S(2)}, u32[]{:S(2)}) collective-permute-start(f32[4,16,8,128]{3,2,1,0:T(8,128)S(1)} %get-tuple-element.26), channel_id=1, source_target_pairs={{16,32},{17,33},{18,34},{19,35},{20,36},{21,37},{22,38},{23,39},{2... | collective-permute-start | bytes 786440 | tf_op jit(solution)/shard_map/ppermute | solution.py:40
  23.2 13.5 %collective-permute-start.7 = (f32[3,4,16,8,128]{4,3,2,1,0:T(8,128)S(1)}, f32[3,4,16,8,128]{4,3,2,1,0:T(8,128)S(1)}, u32[]{:S(2)}, u32[]{:S(2)}) collective-permute-start(f32[3,4,16,8,128]{4,3,2,1,0:T(8,128)S(1)} %pad_maximum_fusion.2.ready_ref), channel_id=1, source_target_pairs={{16,32},{17,33},{18,34},{19,35},{20,36},{21,37},{22,38},{23,39},{2... | collective-permute-start | bytes 2359304 | tf_op jit(solution)/shard_map/ppermute | solution.py:40
  26.6 10.2 %collective-permute-start.8 = (f32[4,4,16,8,128]{4,3,2,1,0:T(8,128)S(1)}, f32[4,4,16,8,128]{4,3,2,1,0:T(8,128)S(1)}, u32[]{:S(2)}, u32[]{:S(2)}) collective-permute-start(f32[4,4,16,8,128]{4,3,2,1,0:T(8,128)S(1)} %pad_maximum_fusion), channel_id=1, source_target_pairs={{0,16},{1,17},{2,18},{3,19},{4,20},{5,21},{6,22},{7,23},{8,24},{9,... | collective-permute-start | bytes 3145736 | tf_op jit(solution)/shard_map/ppermute | solution.py:40
  26.7 2.9 %copy-start.1 = (f32[2,1024,512]{2,1,0:T(8,128)S(1)}, f32[2,1024,512]{2,1,0:T(8,128)}, u32[]{:S(2)}) copy-start(f32[2,1024,512]{2,1,0:T(8,128)} %coupling_ref.1) | copy-start | bytes 12582916
  26.7 2.9 %copy-start.3 = (f32[2,16,1024]{2,1,0:T(8,128)S(1)}, f32[2,16,1024]{2,1,0:T(8,128)}, u32[]{:S(2)}) copy-start(f32[2,16,1024]{2,1,0:T(8,128)} %load_ref.3) | copy-start | bytes 393220
  29.6 3.4 %copy-start = (f32[2,1024,1024]{2,1,0:T(8,128)S(1)}, f32[2,1024,1024]{2,1,0:T(8,128)}, u32[]{:S(2)}) copy-start(f32[2,1024,1024]{2,1,0:T(8,128)} %inverse_ref.1) | copy-start | bytes 25165828
  36.6 0.7 copy-start.4
  39.3 4.7 %collective-permute-start.11 = (f32[16,8,128]{2,1,0:T(8,128)S(1)}, f32[16,8,128]{2,1,0:T(8,128)S(1)}, u32[]{:S(2)}, u32[]{:S(2)}) collective-permute-start(f32[16,8,128]{2,1,0:T(8,128)S(1)} %get-tuple-element.14.image_ref), channel_id=1, source_target_pairs={{0,2},{1,3},{2,0},{3,1},{4,6},{5,7},{6,4},{7,5},{8,10},{9,11},{10,... | collective-permute-start | bytes 196616 | tf_op jit(solution)/shard_map/ppermute | solution.py:40
  41.2 4.6 %collective-permute-start.10 = (f32[16,8,128]{2,1,0:T(8,128)S(1)}, f32[16,8,128]{2,1,0:T(8,128)S(1)}, u32[]{:S(2)}, u32[]{:S(2)}) collective-permute-start(f32[16,8,128]{2,1,0:T(8,128)S(1)} %get-tuple-element.14.image_ref), channel_id=1, source_target_pairs={{0,1},{1,2},{2,3},{3,0},{4,5},{5,6},{6,7},{7,4},{8,9},{9,10},{10,1... | collective-permute-start | bytes 196616 | tf_op jit(solution)/shard_map/ppermute | solution.py:40
  42.7 3.4 %collective-permute-start.9 = (f32[16,8,128]{2,1,0:T(8,128)S(1)}, f32[16,8,128]{2,1,0:T(8,128)S(1)}, u32[]{:S(2)}, u32[]{:S(2)}) collective-permute-start(f32[16,8,128]{2,1,0:T(8,128)S(1)} %get-tuple-element.14.image_ref), channel_id=1, source_target_pairs={{0,3},{1,0},{2,1},{3,2},{4,7},{5,4},{6,5},{7,6},{8,11},{9,8},{10,9... | collective-permute-start | bytes 196616 | tf_op jit(solution)/shard_map/ppermute | solution.py:40
  46.2 10.6 %collective-permute-start.14 = (f32[4,16,8,128]{3,2,1,0:T(8,128)S(1)}, f32[4,16,8,128]{3,2,1,0:T(8,128)S(1)}, u32[]{:S(2)}, u32[]{:S(2)}) collective-permute-start(f32[4,16,8,128]{3,2,1,0:T(8,128)S(1)} %get-tuple-element.24), channel_id=1, source_target_pairs={{0,8},{1,9},{2,10},{3,11},{4,12},{5,13},{6,14},{7,15},{8,0},{9,1},... | collective-permute-start | bytes 786440 | tf_op jit(solution)/shard_map/ppermute | solution.py:40
  47.5 9.3 %collective-permute-start.13 = (f32[4,16,8,128]{3,2,1,0:T(8,128)S(1)}, f32[4,16,8,128]{3,2,1,0:T(8,128)S(1)}, u32[]{:S(2)}, u32[]{:S(2)}) collective-permute-start(f32[4,16,8,128]{3,2,1,0:T(8,128)S(1)} %get-tuple-element.24), channel_id=1, source_target_pairs={{0,4},{1,5},{2,6},{3,7},{4,8},{5,9},{6,10},{7,11},{8,12},{9,13},{1... | collective-permute-start | bytes 786440 | tf_op jit(solution)/shard_map/ppermute | solution.py:40
  49.8 7.0 %collective-permute-start.12 = (f32[4,16,8,128]{3,2,1,0:T(8,128)S(1)}, f32[4,16,8,128]{3,2,1,0:T(8,128)S(1)}, u32[]{:S(2)}, u32[]{:S(2)}) collective-permute-start(f32[4,16,8,128]{3,2,1,0:T(8,128)S(1)} %get-tuple-element.24), channel_id=1, source_target_pairs={{0,12},{1,13},{2,14},{3,15},{4,0},{5,1},{6,2},{7,3},{8,4},{9,5},{1... | collective-permute-start | bytes 786440 | tf_op jit(solution)/shard_map/ppermute | solution.py:40
  50.1 12.9 %collective-permute-start.15 = (f32[4,16,8,128]{3,2,1,0:T(8,128)S(1)}, f32[4,16,8,128]{3,2,1,0:T(8,128)S(1)}, u32[]{:S(2)}, u32[]{:S(2)}) collective-permute-start(f32[4,16,8,128]{3,2,1,0:T(8,128)S(1)} %get-tuple-element.24), channel_id=1, source_target_pairs={{16,32},{17,33},{18,34},{19,35},{20,36},{21,37},{22,38},{23,39},{2... | collective-permute-start | bytes 786440 | tf_op jit(solution)/shard_map/ppermute | solution.py:40
  56.9 15.4 %collective-permute-start.16 = (f32[3,4,16,8,128]{4,3,2,1,0:T(8,128)S(1)}, f32[3,4,16,8,128]{4,3,2,1,0:T(8,128)S(1)}, u32[]{:S(2)}, u32[]{:S(2)}) collective-permute-start(f32[3,4,16,8,128]{4,3,2,1,0:T(8,128)S(1)} %pad_maximum_fusion.3.ready_ref), channel_id=1, source_target_pairs={{16,32},{17,33},{18,34},{19,35},{20,36},{21,37},{22,38},{23,39},{2... | collective-permute-start | bytes 2359304 | tf_op jit(solution)/shard_map/ppermute | solution.py:40
  62.7 9.7 %collective-permute-start.17 = (f32[4,4,16,8,128]{4,3,2,1,0:T(8,128)S(1)}, f32[4,4,16,8,128]{4,3,2,1,0:T(8,128)S(1)}, u32[]{:S(2)}, u32[]{:S(2)}) collective-permute-start(f32[4,4,16,8,128]{4,3,2,1,0:T(8,128)S(1)} %pad_maximum_fusion.1), channel_id=1, source_target_pairs={{0,16},{1,17},{2,18},{3,19},{4,20},{5,21},{6,22},{7,23},{8,24},{9,... | collective-permute-start | bytes 3145736 | tf_op jit(solution)/shard_map/ppermute | solution.py:40
  92.9 3.3 %collective-permute-start.18 = (f32[8,128]{1,0:T(8,128)S(1)}, f32[8,128]{1,0:T(8,128)S(1)}, u32[]{:S(2)}, u32[]{:S(2)}) collective-permute-start(f32[8,128]{1,0:T(8,128)S(1)} %reduce_sum.9.sums_ref), channel_id=1, source_target_pairs={{0,16},{1,17},{2,18},{3,19},{4,20},{5,21},{6,22},{7,23},{8,24},{9,... | collective-permute-start | bytes 12296 | tf_op jit(solution)/shard_map/ppermute | solution.py:40
